TPU v7x, 32 devices: a whole 2x2x4 slice. The times are simulated.
32 devices in a mesh: src: 4 (over z), tm: 8 (over y, x, core).
Axes of the slice: x: 2, y: 2, z: 4, core: 2. Of those that a mesh axis runs over, the one named last changes fastest.
Arguments:
- src_design: float32 [4096, 5, 128], P(('src', 'tm')), may hold values from -6 to 6
- att_design: float32 [4096, 3, 128], P(('src', 'tm')), may hold values from -6 to 6
- obs_frac: float32 [4096, 128], P(('src', 'tm')), may hold values from 0 to 1
- obs_knot: int32 [4096, 128], P(('src', 'tm')), may hold values from 0 to 124
- observed: float32 [4096, 128], P(('src', 'tm'))
- tile_slot: int32 [4096], P(('src', 'tm')), may hold values from 0 to 63, as said below
- tile_offset: int32 [4096], P(('src', 'tm')), may hold values from 0 to 4095
- tile_valid: int32 [4096], P(('src', 'tm')), may hold values from 8 to 128, as said below
- slot_block: int32 [256, 8], P(('src', 'tm')), may hold values from 0 to 31, as said below
Outputs:
- src_solution: float32 [1024, 5, 128], P(('src', 'tm'))
- att_solution: float32 [3, 32768], P(None, 'tm')
Inputs may be any that keep to these rules, and one draw needn't show every extreme that they name: `slot_block`: each row lists 8 distinct local source blocks. `tile_slot`: every slot of every device is named by at least one of that device's tiles. Rows at or after tile_valid are padding.
All inputs are finite; a program needn't handle non-finite values.
Results may differ from a plain program's by a relative error of at most 0.00026.
Values sent between devices are 32-bit elements; how exact they have to be, the bound alone decides.
No kernel may reach another device: no remote copies, remote signals or barrier semaphores. Data moves between devices by JAX's collectives and lax.ppermute only.
A program may use at most 64 MiB of HBM per device.

v0:
```python
import jax
import jax.numpy as jnp
from jax import lax
from jax.sharding import PartitionSpec as P

KN = 4096
HW = 128
SB_DEV = 32
ITERS = 2


damping = 1.0


def passed_along(block, axis, distance):
    devices = range(lax.axis_size(axis))
    route = [(i - distance, i) for i in devices if i - distance in devices]
    return lax.ppermute(block, axis, route)


def spline_weights(fraction):
    remain = 1.0 - fraction
    square = fraction * fraction
    cubed = square * fraction
    return (
        remain * remain * remain / 6.0,
        (3.0 * cubed - 6.0 * square + 4.0) / 6.0,
        (-3.0 * cubed + 3.0 * square + 3.0 * fraction + 1.0) / 6.0,
        cubed / 6.0,
    )


def spline_basis(knots, wstack):
    columns = lax.broadcasted_iota(jnp.int32, (1, 1, HW), 2)
    total = jnp.zeros((knots.shape[0], knots.shape[1], HW), jnp.float32)
    for order in range(4):
        hit = (knots[:, :, None] + order == columns).astype(jnp.float32)
        total = total + wstack[:, order, :][:, :, None] * hit
    return total


def shards(
    src_design,
    att_design,
    obs_frac,
    obs_knot,
    observed,
    tile_slot,
    tile_offset,
    tile_valid,
    slot_block,
):
    tile_count, params, lane_count = src_design.shape
    tm_count = lax.axis_size("tm")
    slot_cap = slot_block.shape[1]
    on_first = lax.axis_index("src") == 0
    valid_rows = (
        lax.broadcasted_iota(jnp.int32, (tile_count, lane_count), 1) < tile_valid[:, None]
    ).astype(jnp.float32)
    wstack = jnp.stack(spline_weights(obs_frac), axis=1)
    block_len = min(32, tile_count)
    block_count = tile_count // block_len
    knot_blocks = obs_knot.reshape(block_count, block_len, lane_count)
    weight_blocks = wstack.reshape(block_count, block_len, 4, lane_count)
    window_index = tile_offset[:, None] + lax.broadcasted_iota(jnp.int32, (tile_count, HW), 1)
    owner_tm = tile_slot // slot_cap
    shard_block = owner_tm * SB_DEV + slot_block.reshape(-1)[tile_slot]

    def return_sources(src_part):
        per_block = jax.ops.segment_sum(src_part, shard_block, num_segments=tm_count * SB_DEV)
        return lax.psum_scatter(per_block, "tm", scatter_dimension=0, tiled=True)

    def cut_window(extended, start):
        return lax.dynamic_slice(extended, (jnp.int32(0), start), (3, HW))

    def forward_block(items):
        knots, wts, window = items
        basis = spline_basis(knots, wts)
        return jnp.einsum("trk,tak->tar", basis, window, precision=lax.Precision.HIGHEST)

    def adjoint_block(items):
        knots, wts, scaled = items
        basis = spline_basis(knots, wts)
        return jnp.einsum("trk,tar->tak", basis, scaled, precision=lax.Precision.HIGHEST)

    def adjoint(resid):
        src_term = return_sources(src_design * resid[:, None, :])
        scaled = att_design * resid[:, None, :]
        win_sums = lax.map(
            adjoint_block,
            (knot_blocks, weight_blocks, scaled.reshape(block_count, block_len, 3, lane_count)),
        )
        win_sums = jnp.transpose(win_sums.reshape(tile_count, 3, HW), (1, 0, 2))
        knot_part = jnp.zeros((3, KN + HW), jnp.float32).at[:, window_index].add(win_sums)
        spill = passed_along(knot_part[:, KN:], "tm", 1)
        own_part = knot_part[:, :KN].at[:, :HW].add(spill)
        return (src_term, lax.psum(own_part, "src"))

    def local_dot(left, right):
        return jnp.sum(left[0] * right[0]) + jnp.where(on_first, jnp.sum(left[1] * right[1]), 0.0)

    def norm_sum(vector):
        return lax.psum(local_dot(vector, vector), ("src", "tm"))

    def combine(first, scale, second):
        return (first[0] + scale * second[0], first[1] + scale * second[1])

    solution = (
        jnp.zeros((SB_DEV, params, lane_count), jnp.float32),
        jnp.zeros((3, KN), jnp.float32),
    )
    residual = adjoint(valid_rows * observed)
    direction = residual
    norm_now = norm_sum(residual)
    for step in range(ITERS):
        dir_att = direction[1]
        whole = lax.all_gather(direction[0], "tm", axis=0, tiled=True)
        src_tiles = whole[shard_block]
        rim_knots = passed_along(dir_att[:, :HW], "tm", -1)
        forward_extended = jnp.concatenate([dir_att, rim_knots], axis=1)
        windows = jax.vmap(cut_window, in_axes=(None, 0))(forward_extended, tile_offset)
        spline = lax.map(
            forward_block,
            (knot_blocks, weight_blocks, windows.reshape(block_count, block_len, 3, HW)),
        )
        spline = spline.reshape(tile_count, 3, lane_count)
        predicted = jnp.sum(src_design * src_tiles, axis=1) + jnp.sum(att_design * spline, axis=1)
        image = adjoint(valid_rows * predicted)
        image = (image[0] + damping * direction[0], image[1] + damping * direction[1])
        curv = lax.psum(local_dot(direction, image), ("src", "tm"))
        step_len = norm_now / curv
        solution = combine(solution, step_len, direction)
        residual = combine(residual, -step_len, image)
        if step + 1 < ITERS:
            norm_next = norm_sum(residual)
            direction = combine(residual, norm_next / norm_now, direction)
            norm_now = norm_next
    return (solution[0], solution[1])


def solution(mesh):
    placed = (
        P(("src", "tm"), None, None),
        P(("src", "tm"), None, None),
        P(("src", "tm"), None),
        P(("src", "tm"), None),
        P(("src", "tm"), None),
        P(("src", "tm")),
        P(("src", "tm")),
        P(("src", "tm")),
        P(("src", "tm"), None),
    )
    return jax.shard_map(
        shards,
        mesh=mesh,
        in_specs=placed,
        out_specs=(P(("src", "tm"), None, None), P(None, "tm")),
        check_vma=False,
    )
```

profile of v0, /device:TPU:0, one launch (start us, length us, event | category | flops | bytes accessed | tf_op | source)
XLA Modules:
  0.0 1335.7 jit_solution(15962289822977489841)
XLA Ops:
  19.2 35.6 %while.55 = (s32[]{:T(128)}, f32[4,32,3,128]{3,2,1,0:T(4,128)S(1)}, f32[4,32,3,128]{3,2,1,0:T(4,128)S(1)}, s32[4,32,128]{2,1,0:T(8,128)S(1)}, f32[4,32,4,128]{3,1,2,0:T(8,128)S(1)}, /*index=5*/s32[]{:T(128)}) while((s32[]{:T(128)}, f32[4,32,3,128]{3,2,1,0:T(4,128)S(1)}, f32[4,32,3,128]{3,2,1,0:T(4,128)S(1)}, s32[4,32,128]{2,1,0:T(8,128)S(1)}, ...), condition=%wide.region_4.5_spmd, body=%wide.region_3.4_spmd.sunk | while | flops 24653824 | bytes 623701 | solution.py:89
  19.3 8.8 fusion.179
  28.2 8.8 fusion.179
  37.1 8.8 fusion.179
  46.0 8.8 fusion.179
  59.7 89.1 %scatter_custom_fusion.1 = f32[3,4224]{0,1:T(8,128)} fusion(s32[16384]{0:T(1024)S(1)} %fusion.158, f32[16384,3]{1,0:T(8,128)} %bitcast.183, f32[]{:T(128)} %constant.206.clone.1), kind=kCustom, calls=%fused_computation.205 | custom fusion | flops 49152 | bytes 51200 | tf_op jit(solution)/shard_map/scatter-add | solution.py:94
  157.9 80.1 %psum.49 = f32[3,4096]{0,1:T(8,128)S(1)} all-reduce(f32[3,4096]{0,1:T(8,128)} %fusion.155), channel_id=1, replica_groups=mesh['src'=4,'tm'=8] {'src'}, use_global_device_ids=true, to_apply=%region_7.8 | all-reduce | flops 12288 | bytes 98304 | tf_op jit(solution)/shard_map/psum | solution.py:97
  241.3 185.1 %while.60 = (s32[]{:T(128)}, f32[3,4224]{1,0:T(4,128)S(1)}, s32[128,2]{0,1:T(2,128)S(1)}, f32[128,3,128]{2,1,0:T(4,128)S(1)}, s32[]{:T(128)}) while((s32[]{:T(128)}, f32[3,4224]{1,0:T(4,128)S(1)}, s32[128,2]{0,1:T(2,128)S(1)}, f32[128,3,128]{2,1,0:T(4,128)S(1)}, s32[]{:T(128)}) %tuple.181), condition=%wide.while_cond.3, body=%wide.while_body.3.sunk | while | flops 2 | bytes 4201 | solution.py:74
  426.4 41.1 %while.56 = (s32[]{:T(128)}, f32[4,32,3,128]{3,2,1,0:T(4,128)S(1)}, f32[4,32,3,128]{3,2,1,0:T(4,128)S(1)}, s32[4,32,128]{2,1,0:T(8,128)S(1)}, f32[4,32,4,128]{3,1,2,0:T(8,128)S(1)}, /*index=5*/s32[]{:T(128)}) while((s32[]{:T(128)}, f32[4,32,3,128]{3,2,1,0:T(4,128)S(1)}, f32[4,32,3,128]{3,2,1,0:T(4,128)S(1)}, s32[4,32,128]{2,1,0:T(8,128)S(1)}, ...), condition=%wide.region_12.13_spmd, body=%wide.region_11.12_spmd.sunk | while | flops 24653824 | bytes 623701 | solution.py:122
  426.5 10.2 fusion.182
  436.7 10.2 fusion.182
  447.0 10.2 fusion.182
  457.3 10.2 fusion.182
  468.5 13.0 all_gather.6
  487.2 13.1 scatter_fusion.1
  501.7 35.6 %while.57 = (s32[]{:T(128)}, f32[4,32,3,128]{3,2,1,0:T(4,128)S(1)}, f32[4,32,3,128]{3,2,1,0:T(4,128)S(1)}, s32[4,32,128]{2,1,0:T(8,128)S(1)}, f32[4,32,4,128]{3,1,2,0:T(8,128)S(1)}, /*index=5*/s32[]{:T(128)}) while((s32[]{:T(128)}, f32[4,32,3,128]{3,2,1,0:T(4,128)S(1)}, f32[4,32,3,128]{3,2,1,0:T(4,128)S(1)}, s32[4,32,128]{2,1,0:T(8,128)S(1)}, ...), condition=%wide.region_18.19_spmd, body=%wide.region_17.18_spmd.sunk | while | flops 24653824 | bytes 623701 | solution.py:89
  542.2 89.1 %scatter_custom_fusion.3 = f32[3,4224]{0,1:T(8,128)} fusion(s32[16384]{0:T(1024)} %copy-done.11, f32[16384,3]{1,0:T(8,128)} %bitcast.184, f32[]{:T(128)} %constant.206.clone.1), kind=kCustom, calls=%fused_computation.203 | custom fusion | flops 49152 | bytes 51200 | tf_op jit(solution)/shard_map/scatter-add | solution.py:94
  639.5 77.2 %psum.51 = f32[3,4096]{0,1:T(8,128)} all-reduce(f32[3,4096]{0,1:T(8,128)} %fusion.156), channel_id=1, replica_groups=mesh['src'=4,'tm'=8] {'src'}, use_global_device_ids=true, to_apply=%region_20.21 | all-reduce | flops 12288 | bytes 98304 | tf_op jit(solution)/shard_map/psum | solution.py:97
  725.2 38.6 %all-reduce.1 = (f32[]{:T(128)}, f32[]{:T(128)}) all-reduce(f32[]{:T(128)S(6)} %add.363, f32[]{:T(128)S(6)} %add.370), channel_id=1, replica_groups=mesh['src'=4,'tm'=8] {'src','tm'}, use_global_device_ids=true, to_apply=%region_9.10 | all-reduce | flops 2 | bytes 16 | tf_op jit(solution)/shard_map/psum | solution.py:103
  769.6 41.3 %psum.53 = f32[]{:T(128)} all-reduce(f32[]{:T(128)S(6)} %add.373), channel_id=1, replica_groups=mesh['src'=4,'tm'=8] {'src','tm'}, use_global_device_ids=true, to_apply=%region_25.26 | all-reduce | flops 1 | bytes 8 | tf_op jit(solution)/shard_map/psum | solution.py:103
  815.4 11.1 all_gather.7
  836.6 168.5 %while.61 = (s32[]{:T(128)}, f32[3,4224]{1,0:T(4,128)S(1)}, s32[128,2]{0,1:T(2,128)S(1)}, f32[128,3,128]{2,1,0:T(4,128)S(1)}, s32[]{:T(128)}) while((s32[]{:T(128)}, f32[3,4224]{1,0:T(4,128)S(1)}, s32[128,2]{0,1:T(2,128)S(1)}, f32[128,3,128]{2,1,0:T(4,128)S(1)}, s32[]{:T(128)}) %tuple.219), condition=%wide.while_cond.4, body=%wide.while_body.4.sunk | while | flops 2 | bytes 4201 | solution.py:74
  1005.9 37.5 %while.58 = (s32[]{:T(128)}, f32[4,32,3,128]{3,2,1,0:T(4,128)S(1)}, f32[4,32,3,128]{3,2,1,0:T(4,128)}, s32[4,32,128]{2,1,0:T(8,128)S(1)}, f32[4,32,4,128]{3,1,2,0:T(8,128)S(1)}, /*index=5*/s32[]{:T(128)}) while((s32[]{:T(128)}, f32[4,32,3,128]{3,2,1,0:T(4,128)S(1)}, f32[4,32,3,128]{3,2,1,0:T(4,128)}, s32[4,32,128]{2,1,0:T(8,128)S(1)}, ...), condition=%wide.region_28.29_spmd, body=%wide.region_27.28_spmd.sunk | while | flops 24653824 | bytes 623701 | solution.py:122
  1006.0 9.3 fusion.188
  1015.3 9.3 fusion.188
  1024.7 9.3 fusion.188
  1034.1 9.3 fusion.188
  1045.3 9.5 scatter_fusion.2
  1057.0 38.0 %while.59 = (s32[]{:T(128)}, f32[4,32,3,128]{3,2,1,0:T(4,128)S(1)}, f32[4,32,3,128]{3,2,1,0:T(4,128)S(1)}, s32[4,32,128]{2,1,0:T(8,128)}, f32[4,32,4,128]{3,1,2,0:T(8,128)S(1)}, /*index=5*/s32[]{:T(128)}) while((s32[]{:T(128)}, f32[4,32,3,128]{3,2,1,0:T(4,128)S(1)}, f32[4,32,3,128]{3,2,1,0:T(4,128)S(1)}, s32[4,32,128]{2,1,0:T(8,128)}, ...), condition=%wide.region_34.35_spmd, body=%wide.region_33.34_spmd.sunk | while | flops 24653824 | bytes 623701 | solution.py:89
  1099.9 89.1 %scatter_custom_fusion.5 = f32[3,4224]{0,1:T(8,128)} fusion(s32[16384]{0:T(1024)} %copy-done.11, f32[16384,3]{1,0:T(8,128)} %bitcast.182, f32[]{:T(128)} %constant.206.clone.1), kind=kCustom, calls=%fused_computation.201 | custom fusion | flops 49152 | bytes 51200 | tf_op jit(solution)/shard_map/scatter-add | solution.py:94
  1198.0 78.4 %psum.54 = f32[3,4096]{0,1:T(8,128)} all-reduce(f32[3,4096]{0,1:T(8,128)} %fusion.157), channel_id=1, replica_groups=mesh['src'=4,'tm'=8] {'src'}, use_global_device_ids=true, to_apply=%region_36.37 | all-reduce | flops 12288 | bytes 98304 | tf_op jit(solution)/shard_map/psum | solution.py:97
  1282.7 38.6 %psum.55 = f32[]{:T(128)} all-reduce(f32[]{:T(128)S(6)} %add.380), channel_id=1, replica_groups=mesh['src'=4,'tm'=8] {'src','tm'}, use_global_device_ids=true, to_apply=%region_38.39 | all-reduce | flops 1 | bytes 8 | tf_op jit(solution)/shard_map/psum | solution.py:130
  (983 shorter events, 530.1 us)
Async XLA Ops:
  7.2 460.4 %reduce-scatter.4.cloned.1.call-start = ((), (), s32[]{:S(2)}) async-start(), calls=%async_computation.3 | async-start | bytes 1179648 | tf_op jit(solution)/shard_map/reduce_scatter | solution.py:71
  12.5 6.3 copy-start.13
  12.5 6.4 copy-start.3
  12.7 6.4 copy-start.10
  12.8 6.4 copy-start.5
  17.7 1.0 copy-start.2
  18.8 703.4 %reduce-scatter.6.cloned.1.call-start = ((), (), s32[]{:S(2)}) async-start(), calls=%async_computation.4 | async-start | bytes 1179648 | tf_op jit(solution)/shard_map/reduce_scatter | solution.py:71
  18.9 40.8 %copy-start.11 = (s32[16384]{0:T(1024)}, s32[16384]{0:T(1024)S(1)}, u32[]{:S(2)}) copy-start(s32[16384]{0:T(1024)S(1)} %fusion.158) | copy-start | bytes 196612
  149.7 6.1 collective-permute-start
  238.0 3.1 collective-permute-start.1
  467.4 17.3 %copy-start = (f32[128,5,128]{2,0,1:T(8,128)S(1)}, f32[128,5,128]{2,0,1:T(8,128)}, u32[]{:S(2)}) copy-start(f32[128,5,128]{2,0,1:T(8,128)} %param.25) | copy-start | bytes 983044
  468.5 16.7 %copy-start.12 = (s32[128]{0:T(128)S(1)}, s32[128]{0:T(128)}, u32[]{:S(2)}) copy-start(s32[128]{0:T(128)} %param.32) | copy-start | bytes 1540
  500.4 780.2 %reduce-scatter.8.cloned.1.call-start = ((), (), s32[]{:S(2)}) async-start(), calls=%async_computation.5 | async-start | bytes 1179648 | tf_op jit(solution)/shard_map/reduce_scatter | solution.py:71
  632.1 5.3 collective-permute-start.2
  716.7 5.5 copy-start.4
  815.3 18.9 %copy-start.7 = (f32[32,5,128]{2,1,0:T(8,128)}, f32[32,5,128]{2,1,0:T(8,128)S(1)}, u32[]{:S(2)}) copy-start(f32[32,5,128]{2,1,0:T(8,128)S(1)} %multiply_add_fusion.4) | copy-start | bytes 245764
  831.4 5.1 collective-permute-start.3
  1005.2 0.7 copy-start.9
  1043.4 0.9 copy-start.6
  1054.8 1.0 copy-start.1
  1189.8 6.1 collective-permute-start.4
  1276.4 4.1 copy-start.8
Sparse Core Ops, SparseCore 0:
  18.9 39.0 reduce-scatter.3
  500.5 34.0 reduce-scatter.5
  1056.0 36.2 reduce-scatter.7
where the time goes:
time: 1340 us
  local copies, waits for them, and re-layouts  405 us (30%)
  blocking collectives  378 us (28%)
  other arithmetic  332 us (25%)
  matrix products  183 us (14%)
  between operations  23.2 us (2%)
    gather x768, local copies, waits for them, and re-layouts  353 us
    scatter-add x3, other arithmetic, adjoint(): jnp.zeros((3, KN + HW), jnp.float32).at[:, window_index].add(win_sums)  267 us
    psum x3, blocking collectives, adjoint(): return (src_term, lax.psum(own_part, 'src'))  236 us
    dot_general x12, matrix products, adjoint_block(): jnp.einsum('trk,tar->tak', basis, scaled, precision=lax.Precision.HIGHEST)  106 us
    psum x2, blocking collectives, norm_sum(): return lax.psum(local_dot(vector, vector), ('src', 'tm'))  79.9 us
    dot_general x8, matrix products, forward_block(): jnp.einsum('trk,tak->tar', basis, window, precision=lax.Precision.HIGHEST)  77.9 us
    psum x1, blocking collectives, shards(): curv = lax.psum(local_dot(direction, image), ('src', 'tm'))  38.6 us
    scatter-add x3, other arithmetic, return_sources(): jax.ops.segment_sum(src_part, shard_block, num_segments=tm_count * SB_DEV)  27.5 us
  transfers between devices with their start and end apart: 8, of which 1 were waited for; matrix products, arithmetic and copies ran while one was open for 49% of the time, Pallas kernels for 0%

commit v1 on v0

v1 whole, which is shorter than its diff:
```python
import functools

import jax
import jax.numpy as jnp
from jax import lax
from jax.experimental import pallas as pl
from jax.experimental.pallas import tpu as pltpu
from jax.sharding import PartitionSpec as P

KN = 4096
HW = 128
SB_DEV = 32
damping = 1.0

LANES = 128
ROWS = KN // LANES
ROWS_PAD = (ROWS + 8) // 8 * 8
AXES = 3
PARAMS = 5
CAP = 8
EXTRA = PARAMS * CAP
PIECE = EXTRA + 8
UNROLL = 4
F32 = jnp.float32
BF16 = jnp.bfloat16


def iota(shape, dim):
    return lax.broadcasted_iota(jnp.int32, shape, dim)


def spline_weights(fraction):
    remain = 1.0 - fraction
    square = fraction * fraction
    cubed = square * fraction
    return (
        remain * remain * remain / 6.0,
        (3.0 * cubed - 6.0 * square + 4.0) / 6.0,
        (-3.0 * cubed + 3.0 * square + 3.0 * fraction + 1.0) / 6.0,
        cubed / 6.0,
    )


def split2(value):
    high = value.astype(BF16)
    return high, (value - high.astype(F32)).astype(BF16)


def split3(value):
    high, rest = value.astype(BF16), None
    rest = value - high.astype(F32)
    middle = rest.astype(BF16)
    return high, middle, (rest - middle.astype(F32)).astype(BF16)


def total(value):
    return jnp.sum(jnp.sum(value, axis=0, keepdims=True), axis=1, keepdims=True)


def row_of(ref, row):
    return jnp.broadcast_to(ref[pl.ds(row, 1), :], (8, LANES))


def add_adjoint(tiles, values, design, slot_ref, offset_ref, knot_ref, acc, knots):
    lane_row = iota((LANES, LANES), 0).astype(F32)
    outs = []
    for t, resid in zip(tiles, values):
        shift = offset_ref[t] % LANES
        place = knot_ref[pl.ds(t, 1), :] + shift
        first = place < LANES
        lane = jnp.where(first, place, place - LANES)
        hot = (lane_row == lane.astype(F32)).astype(BF16)
        spread = jnp.concatenate([design[t, 0:8, :] * resid, design[t, 8:16, :] * resid], axis=0)
        mask = jnp.broadcast_to(first.astype(F32), spread.shape)
        here = spread * mask
        parts = split2(here) + split2(spread - here)
        outs.append(
            lax.dot_general(
                jnp.concatenate(parts, axis=0),
                hot,
                (((1,), (1,)), ((), ())),
                preferred_element_type=F32,
            )
        )
    for t, resid, out in zip(tiles, values, outs):
        slot = slot_ref[t]
        acc[slot] += design[t, 16:24, :] * resid
        row = offset_ref[t] // LANES
        knots[row] += out[0:16] + out[16:32]
        knots[row + 1] += out[32:48] + out[48:64]


def send_sums(acc, knots, piece_ref, att_ref, owners):
    for owner in range(owners):
        for param in range(PARAMS):
            piece_ref[owner * PIECE + param * CAP : owner * PIECE + param * CAP + CAP, :] = acc[
                owner * CAP : owner * CAP + CAP, param, :
            ]
    lane = iota((8, LANES), 1)
    low = iota((8, LANES), 0) < 4
    before = [jnp.zeros((8, LANES), F32)] * 3
    for row in range(ROWS + 1):
        one, two = knots[row, 0:8, :], knots[row, 8:16, :]
        now = [pltpu.roll(one, 1, 1), pltpu.roll(two, 2, 1), pltpu.roll(two, 3, 1)]
        moved = [jnp.where(lane >= k + 1, now[k], before[k]) for k in range(3)]
        both = jnp.where(low, one + moved[1], moved[0] + moved[2])
        both = both + pltpu.roll(both, 4, 0)
        for axis in range(AXES):
            att_ref[axis * ROWS_PAD + row : axis * ROWS_PAD + row + 1, :] = both[axis : axis + 1]
        before = now


def first_kernel(
    slot_ref,
    offset_ref,
    valid_ref,
    src_ref,
    att_ref,
    frac_ref,
    knot_ref,
    obs_ref,
    table_ref,
    design,
    piece_ref,
    part_ref,
    acc,
    knots,
    wts,
):
    tiles = src_ref.shape[0]
    owners = table_ref.shape[0]
    acc[...] = jnp.zeros_like(acc)
    knots[...] = jnp.zeros_like(knots)
    part_ref[...] = jnp.zeros_like(part_ref)
    for k, weight in enumerate(spline_weights(frac_ref[...])):
        wts[k] = weight
    sub = iota((8, LANES), 0)
    lane = iota((8, LANES), 1)

    def body(step, carry):
        batch = [step * UNROLL + k for k in range(UNROLL)]
        for t in batch:
            live = lane < valid_ref[t]
            three = [row_of(att_ref.at[t], axis) for axis in range(AXES)]
            axis_of = sub % 4
            mixed = jnp.where(axis_of == 0, three[0], jnp.where(axis_of == 1, three[1], three[2]))
            mixed = jnp.where(live & (axis_of < 3), mixed, 0.0)
            weights = [row_of(wts.at[k], t) for k in range(4)]
            design[t, 0:8, :] = mixed * jnp.where(sub < 4, weights[0], weights[1])
            design[t, 8:16, :] = mixed * jnp.where(sub < 4, weights[2], weights[3])
            design[t, 16:24, :] = jnp.zeros((8, LANES), F32)
            design[t, 16 : 16 + PARAMS, :] = jnp.where(live[0:PARAMS], src_ref[t], 0.0)
        values = [row_of(obs_ref, t) for t in batch]
        add_adjoint(batch, values, design, slot_ref, offset_ref, knot_ref, acc, knots)
        return carry

    lax.fori_loop(0, tiles // UNROLL, body, 0)
    send_sums(acc, knots, piece_ref, part_ref, owners)
    me = lax.axis_index("tm")
    placed = (iota((CAP, LANES), 1) == iota((CAP, LANES), 0) + me * CAP).astype(BF16)
    names = jnp.dot(
        table_ref[...].astype(F32).astype(BF16), placed, preferred_element_type=F32
    )
    for owner in range(owners):
        piece_ref[owner * PIECE + EXTRA : owner * PIECE + PIECE, :] = jnp.where(
            sub == 0, jnp.broadcast_to(names[owner : owner + 1], (8, LANES)), 0.0
        )


def owner_kernel(count, with_names, *refs):
    piece_ref, parts, rest = refs[0], refs[1 : 1 + count], refs[1 + count :]
    if with_names:
        own_ref, att_ref, back_ref, names_ref = rest
    else:
        names_in, own_in, own_ref, att_ref, back_ref = rest
    owners = piece_ref.shape[0]
    rows = owners * CAP
    sub = iota((8, LANES), 0)
    if with_names:
        names = piece_ref[0, EXTRA : EXTRA + 8, :]
        for owner in range(1, owners):
            names = names + piece_ref[owner, EXTRA : EXTRA + 8, :]
        names_ref[...] = names
    else:
        names = names_in[...]
    hot = (iota((LANES, LANES), 0).astype(F32) == jnp.broadcast_to(names[0:1], (LANES, LANES))).astype(F32)
    pick = hot[0:SB_DEV, 0:rows].astype(BF16)
    give = hot.T[0:rows, 0:SB_DEV].astype(BF16)
    pick = jnp.concatenate([pick] * 3, axis=1)
    give = jnp.concatenate([give] * 3, axis=1)
    square = jnp.zeros((SB_DEV, LANES), F32)
    if not with_names:
        sums = piece_ref[0, EXTRA : EXTRA + 8, :]
        for owner in range(1, owners):
            sums = sums + piece_ref[owner, EXTRA : EXTRA + 8, :]
        sigma = sums[1:2, 0:1] / sums[1:2, 1:2]
        across = jnp.zeros((SB_DEV, LANES), F32)
    for param in range(PARAMS):
        got = piece_ref[:, param * CAP : param * CAP + CAP, :].reshape(rows, LANES)
        mine = jnp.dot(pick, jnp.concatenate(split3(got), axis=0), preferred_element_type=F32)
        own_ref[param] = mine
        back = jnp.dot(give, jnp.concatenate(split3(mine), axis=0), preferred_element_type=F32)
        back_ref[:, param * CAP : param * CAP + CAP, :] = back.reshape(owners, CAP, LANES)
        if with_names:
            square = square + mine * mine
        else:
            before = own_in[param]
            rest_ = mine - sigma * before
            square = square + rest_ * rest_
            across = across + rest_ * before
    level = [part[...] for part in parts]
    while len(level) > 1:
        level = [level[k] + level[k + 1] for k in range(0, len(level), 2)]
    att_ref[...] = level[0]
    extra = jnp.zeros((8, LANES), F32)
    for axis in range(AXES):
        at = axis * ROWS_PAD
        extra = jnp.where(sub == axis, level[0][at : at + 1], extra)
        extra = jnp.where(sub == AXES + axis, level[0][at + ROWS : at + ROWS + 1], extra)
    lane = iota((8, LANES), 1)
    numbers = jnp.where(lane == 0, total(square), 0.0)
    if not with_names:
        numbers = jnp.where(lane == 1, total(across), numbers)
        numbers = jnp.where(lane == 2, sigma, numbers)
        numbers = jnp.where(lane == 3, sums[1:2, 0:1], numbers)
        numbers = jnp.where(lane == 4, sums[1:2, 1:2], numbers)
    extra = jnp.where(sub == 2 * AXES, numbers, extra)
    for owner in range(owners):
        back_ref[owner, EXTRA : EXTRA + 8, :] = extra


def load_vector(got_ref, part_ref, slots, table, true_ref):
    owners = got_ref.shape[0] // PIECE
    me = lax.axis_index("tm")
    slots[...] = jnp.zeros_like(slots)
    for owner in range(owners):
        for param in range(PARAMS):
            slots[owner * CAP : owner * CAP + CAP, param, :] = got_ref[
                owner * PIECE + param * CAP : owner * PIECE + param * CAP + CAP, :
            ]
    left = got_ref[pl.ds(jnp.maximum(me - 1, 0) * PIECE + EXTRA, 8), :]
    right = got_ref[pl.ds(jnp.minimum(me + 1, owners - 1) * PIECE + EXTRA, 8), :]
    left = jnp.where(me > 0, left, 0.0)
    right = jnp.where(me < owners - 1, right, 0.0)
    has_right = jnp.where(me < owners - 1, 1.0, 0.0)
    sub = iota((8, LANES), 0)
    lane = iota((8, LANES), 1)
    low = sub < 4
    axis_of = sub % 4
    for axis in range(AXES):
        at = axis * ROWS_PAD
        true_ref[axis] = part_ref[at : at + ROWS, :]
        true_ref[axis, 0:1, :] = part_ref[at : at + 1, :] + left[AXES + axis : AXES + axis + 1]

    def mixed(row):
        if row < ROWS:
            three = [true_ref[axis, row : row + 1, :] for axis in range(AXES)]
        else:
            three = [
                right[axis : axis + 1] + has_right * part_ref[axis * ROWS_PAD + ROWS : axis * ROWS_PAD + ROWS + 1, :]
                for axis in range(AXES)
            ]
        three = [jnp.broadcast_to(v, (8, LANES)) for v in three]
        out = jnp.where(axis_of == 0, three[0], jnp.where(axis_of == 1, three[1], three[2]))
        return jnp.where(axis_of < 3, out, 0.0)

    def rolled(value):
        return [pltpu.roll(value, LANES - k, 1) for k in (1, 2, 3)]

    now = mixed(0)
    now_rolled = rolled(now)
    for row in range(ROWS + 1):
        after = mixed(row + 1) if row < ROWS else jnp.zeros((8, LANES), F32)
        after_rolled = rolled(after)
        moved = [jnp.where(lane < LANES - 1 - k, now_rolled[k], after_rolled[k]) for k in range(3)]
        table[row, 0:8, :] = jnp.where(low, now, moved[0])
        table[row, 8:16, :] = jnp.where(low, moved[1], moved[2])
        now, now_rolled = after, after_rolled


def forward(tiles, design, slot_ref, offset_ref, knot_ref, slots, table):
    values = []
    for t in tiles:
        shift = offset_ref[t] % LANES
        row = offset_ref[t] // LANES
        place = row_of(knot_ref, t) + shift
        first = place < LANES
        lane = jnp.where(first, place, place - LANES)
        summed = design[t, 16:24, :] * slots[slot_ref[t]]
        for half in (0, 8):
            here = jnp.take_along_axis(table[row, half : half + 8, :], lane, axis=1)
            there = jnp.take_along_axis(table[row + 1, half : half + 8, :], lane, axis=1)
            summed = summed + design[t, half : half + 8, :] * jnp.where(first, here, there)
        summed = summed + pltpu.roll(summed, 4, 0)
        summed = summed + pltpu.roll(summed, 2, 0)
        values.append(summed + pltpu.roll(summed, 1, 0))
    return values


def middle_kernel(
    copies,
    slot_ref,
    offset_ref,
    got_ref,
    part_ref,
    design,
    knot_ref,
    piece_ref,
    sum_ref,
    true_ref,
    y_ref,
    acc,
    knots,
    slots,
    table,
):
    tiles = design.shape[0]
    owners = got_ref.shape[0] // PIECE
    acc[...] = jnp.zeros_like(acc)
    knots[...] = jnp.zeros_like(knots)
    sum_ref[...] = jnp.zeros_like(sum_ref)
    load_vector(got_ref, part_ref, slots, table, true_ref)

    def body(step, square):
        batch = [step * UNROLL + k for k in range(UNROLL)]
        values = forward(batch, design, slot_ref, offset_ref, knot_ref, slots, table)
        for t, value in zip(batch, values):
            y_ref[pl.ds(t, 1), :] = value[0:1]
            square = square + value * value
        add_adjoint(batch, values, design, slot_ref, offset_ref, knot_ref, acc, knots)
        return square

    square = lax.fori_loop(0, tiles // UNROLL, body, jnp.zeros((8, LANES), F32))
    send_sums(acc, knots, piece_ref, sum_ref, owners)
    norm_att = jnp.zeros((ROWS, LANES), F32)
    for axis in range(AXES):
        norm_att = norm_att + true_ref[axis] * true_ref[axis]
    me = lax.axis_index("tm")
    sent = got_ref[pl.ds(me * PIECE + EXTRA, 8), :]
    norm = sent[2 * AXES : 2 * AXES + 1, 0:1] + total(norm_att) / copies
    lane = iota((8, LANES), 1)
    numbers = jnp.where(lane == 0, total(square[0:1]), jnp.where(lane == 1, norm, 0.0))
    numbers = jnp.where(iota((8, LANES), 0) == 1, numbers, 0.0)
    for owner in range(owners):
        piece_ref[owner * PIECE + EXTRA : owner * PIECE + PIECE, :] = numbers


def last_kernel(
    copies,
    slot_ref,
    offset_ref,
    got_ref,
    part_ref,
    design,
    knot_ref,
    y_ref,
    numbers_ref,
    before_ref,
    true_ref,
    out_ref,
    slots,
    table,
):
    tiles = design.shape[0]
    owners = got_ref.shape[0] // PIECE
    load_vector(got_ref, part_ref, slots, table, true_ref)
    me = lax.axis_index("tm")
    sent = got_ref[pl.ds(me * PIECE + EXTRA, 8), :][2 * AXES : 2 * AXES + 1]
    group = got_ref[EXTRA : EXTRA + 8, :]
    for owner in range(1, owners):
        group = group + got_ref[owner * PIECE + EXTRA : owner * PIECE + EXTRA + 8, :]
    group = group[2 * AXES : 2 * AXES + 1]
    sigma, s_group, n_group = sent[:, 2:3], sent[:, 3:4], sent[:, 4:5]
    square_att = jnp.zeros((ROWS, LANES), F32)
    across_att = jnp.zeros((ROWS, LANES), F32)
    for axis in range(AXES):
        rest = true_ref[axis] - sigma * before_ref[axis]
        square_att = square_att + rest * rest
        across_att = across_att + rest * before_ref[axis]
    square_att = total(square_att) / copies
    across_att = total(across_att) / copies
    d_group = group[:, 0:1] + square_att * owners
    tau = sigma + d_group / (s_group + n_group)
    tau_full = jnp.broadcast_to(tau, (8, LANES))

    def body(step, carry):
        square, across = carry
        batch = [step * UNROLL + k for k in range(UNROLL)]
        values = forward(batch, design, slot_ref, offset_ref, knot_ref, slots, table)
        for t, value in zip(batch, values):
            before = row_of(y_ref, t)
            rest = value - tau_full * before
            square = square + rest * rest
            across = across + rest * before
        return square, across

    zero = jnp.zeros((8, LANES), F32)
    square, across = lax.fori_loop(0, tiles // UNROLL, body, (zero, zero))
    own = numbers_ref[...][EXTRA + 1 : EXTRA + 2]
    numbers = [
        own[:, 1:2],
        own[:, 0:1],
        sent[:, 0:1] + square_att,
        sent[:, 1:2] + across_att,
        sigma,
        total(square[0:1]),
        total(across[0:1]),
        tau,
    ]
    lane = iota((1, LANES), 1)
    out = jnp.zeros((1, LANES), F32)
    for k, number in enumerate(numbers):
        out = jnp.where(lane == k, number, out)
    out_ref[...] = jnp.broadcast_to(out[None], out_ref.shape)


def final_kernel(got_ref, z_src, w_src, z_att, w_att, src_out, att_out):
    devices = got_ref.shape[0]
    got = got_ref[...].reshape(devices, LANES)

    def column(k):
        return got[:, k : k + 1]

    def summed(value):
        return jnp.sum(value, axis=0, keepdims=True)

    n_of, s_of = column(0), column(1)
    n, s = summed(n_of), summed(s_of)
    sigma = s / n
    alpha = n / (s + n)
    off = column(4) - sigma
    d = summed(column(2) + 2.0 * off * column(3) + off * off * n_of)
    gamma = alpha * d / n
    tau = sigma + gamma
    off = column(7) - tau
    e = summed(column(5) + 2.0 * off * column(6) + off * off * s_of)
    second = d / (e + damping * (d + gamma * gamma * n))
    c_z = alpha * (1.0 + second * tau)
    c_w = alpha * second
    for param in range(PARAMS):
        src_out[:, param, :] = c_z * z_src[param] - c_w * w_src[param]
    for axis in range(AXES):
        value = c_z * z_att[axis] - c_w * w_att[axis]
        for row in range(ROWS):
            att_out[axis : axis + 1, row * LANES : (row + 1) * LANES] = value[row : row + 1]


VMEM = pl.BlockSpec(memory_space=pltpu.VMEM)
SMEM = pl.BlockSpec(memory_space=pltpu.SMEM)
PARAMETERS = pltpu.CompilerParams(vmem_limit_bytes=24 * 1024 * 1024)


def f32(*shape):
    return jax.ShapeDtypeStruct(shape, F32)


def call(kernel, out_shape, in_specs, scratch=(), name=None):
    return pl.pallas_call(
        kernel,
        out_shape=out_shape,
        in_specs=in_specs,
        out_specs=jax.tree.map(lambda _: VMEM, out_shape),
        scratch_shapes=list(scratch),
        compiler_params=PARAMETERS,
        name=name,
    )


def shards(
    src_design,
    att_design,
    obs_frac,
    obs_knot,
    observed,
    tile_slot,
    tile_offset,
    tile_valid,
    slot_block,
):
    tiles = src_design.shape[0]
    owners = lax.axis_size("tm")
    copies = lax.axis_size("src")
    devices = owners * copies
    slot_count = owners * CAP
    acc = pltpu.VMEM((slot_count, 8, LANES), F32)
    knots = pltpu.VMEM((ROWS + 1, 16, LANES), F32)
    piece = f32(owners * PIECE, LANES)
    part = f32(AXES * ROWS_PAD, LANES)
    true = f32(AXES, ROWS, LANES)

    def exchange(pieces):
        return lax.all_to_all(pieces.reshape(owners, PIECE, LANES), "tm", 0, 0, tiled=True)

    def src_parts(own):
        return [own] + [
            lax.ppermute(own, "src", [(i, i ^ k) for i in range(copies)]) for k in range(1, copies)
        ]

    design, pieces, own = call(
        first_kernel,
        (f32(tiles, 24, LANES), piece, part),
        [SMEM] * 3 + [VMEM] * 6,
        [acc, knots, pltpu.VMEM((4, tiles, LANES), F32)],
        "first",
    )(tile_slot, tile_offset, tile_valid, src_design, att_design, obs_frac, obs_knot, observed, slot_block)
    got, parts = exchange(pieces), src_parts(own)
    z_src, z_part, back, names = call(
        functools.partial(owner_kernel, copies, True),
        (f32(PARAMS, SB_DEV, LANES), part, f32(owners, PIECE, LANES), f32(8, LANES)),
        [VMEM] * (1 + copies),
        name="owner_first",
    )(got, *parts)
    got = exchange(back).reshape(owners * PIECE, LANES)
    pieces, own, z_att, y = call(
        functools.partial(middle_kernel, copies),
        (piece, part, true, f32(tiles, LANES)),
        [SMEM] * 2 + [VMEM] * 4,
        [acc, knots, acc, knots],
        "middle",
    )(tile_slot, tile_offset, got, z_part, design, obs_knot)
    numbers = pieces
    got, parts = exchange(pieces), src_parts(own)
    w_src, w_part, back = call(
        functools.partial(owner_kernel, copies, False),
        (f32(PARAMS, SB_DEV, LANES), part, f32(owners, PIECE, LANES)),
        [VMEM] * (3 + copies),
        name="owner_second",
    )(got, *parts, names, z_src)
    got = exchange(back).reshape(owners * PIECE, LANES)
    w_att, row = call(
        functools.partial(last_kernel, copies),
        (true, f32(devices, 1, LANES)),
        [SMEM] * 2 + [VMEM] * 7,
        [acc, knots],
        "last",
    )(tile_slot, tile_offset, got, w_part, design, obs_knot, y, numbers, z_att)
    row = lax.all_to_all(row, ("src", "tm"), 0, 0, tiled=True)
    return call(
        final_kernel,
        (f32(SB_DEV, PARAMS, LANES), f32(AXES, KN)),
        [VMEM] * 5,
        name="final",
    )(row, z_src, w_src, z_att, w_att)


def solution(mesh):
    placed = (
        P(("src", "tm"), None, None),
        P(("src", "tm"), None, None),
        P(("src", "tm"), None),
        P(("src", "tm"), None),
        P(("src", "tm"), None),
        P(("src", "tm")),
        P(("src", "tm")),
        P(("src", "tm")),
        P(("src", "tm"), None),
    )
    return jax.shard_map(
        shards,
        mesh=mesh,
        in_specs=placed,
        out_specs=(P(("src", "tm"), None, None), P(None, "tm")),
        check_vma=False,
    )
```

time: 1340 us -> 92.8 us (0.07)
  local copies, waits for them, and re-layouts: 405 us -> 8.1 us
  blocking collectives: 378 us -> 29.7 us
  other arithmetic: 332 us -> 0 us
  matrix products: 183 us -> 0 us
  Pallas kernels: 0 us -> 26.9 us
  between operations: 23.2 us -> 0.7 us
    gather x771 -> x0, local copies, waits for them, and re-layouts: 359 us -> none
    psum x6 -> x0, blocking collectives: 354 us -> none  [the longest x3 236 us: adjoint(): return (src_term, lax.psum(own_part, 'src'))]
    scatter-add x9 -> x0, other arithmetic: 301 us -> none  [the longest x3 267 us: adjoint(): jnp.zeros((3, KN + HW), jnp.float32).at[:, window_index].add(win_sums)]
    dot_general x20 -> x0, matrix products: 183 us -> none  [the longest x12 106 us: adjoint_block(): jnp.einsum('trk,tar->tak', basis, scaled, precision=lax.Precision.HIGHEST)]
    all_to_all x0 -> x3, blocking collectives: none -> 29.7 us  [the longest x2 20.1 us: exchange(): lax.all_to_all(pieces.reshape(owners, PIECE, LANES), 'tm', 0, 0, tiled=True)]
    pallas_call x0 -> x6, Pallas kernels: none -> 26.9 us  [the longest x1 10.4 us: shards(): call(functools.partial(middle_kernel, copies), (piece, part, true, f32(ti...]
    all_gather x2 -> x0, blocking collectives: 24.1 us -> none  [shards(): whole = lax.all_gather(direction[0], 'tm', axis=0, tiled=True)]
    reduce_sum x10 -> x0, other arithmetic: 15.9 us -> none  [the longest x3 10.2 us: local_dot(): jnp.sum(left[1] * right[1])]
  transfers between devices with their start and end apart: 8 -> 8, of which waited for: 1 -> 4; matrix products, arithmetic and copies ran while one was open for 49% -> 0% of each run, Pallas kernels for 0% -> 0%
where the time goes in v1:
time: 92.8 us; the launch traced here: 92.1 us
  blocking collectives  29.7 us (32%)
  Pallas kernels  26.9 us (29%)
  starting transfers between devices  17.4 us (19%)
  waiting for transfers between devices  9.34 us (10%)
  local copies, waits for them, and re-layouts  8.1 us (9%)
    all_to_all x2, blocking collectives, exchange(): lax.all_to_all(pieces.reshape(owners, PIECE, LANES), 'tm', 0, 0, tiled=True)  20.1 us
    pallas_call x1, Pallas kernels, shards(): call(functools.partial(middle_kernel, copies), (piece, part, true, f32(ti...  10.4 us
    all_to_all x1, blocking collectives, shards(): row = lax.all_to_all(row, ('src', 'tm'), 0, 0, tiled=True)  9.52 us
    ppermute x6, waiting for transfers between devices, src_parts(): lax.ppermute(own, 'src', [(i, i ^ k) for i in range(copies)])  9.33 us
    ppermute x6, starting transfers between devices, src_parts(): lax.ppermute(own, 'src', [(i, i ^ k) for i in range(copies)])  8.84 us
    all_to_all x2, starting transfers between devices, exchange(): lax.all_to_all(pieces.reshape(owners, PIECE, LANES), 'tm', 0, 0, tiled=True)  8.57 us
    pallas_call x1, Pallas kernels, shards(): call(first_kernel, (f32(tiles, 24, LANES), piece, part), [SMEM] * 3 + [VM...  8.48 us
    unnamed x22, local copies, waits for them, and re-layouts  7.45 us
  transfers between devices with their start and end apart: 8, of which 4 were waited for; matrix products, arithmetic and copies ran while one was open for 0% of the time, Pallas kernels for 0%

profile of v1, /device:TPU:0, one launch (start us, length us, event | category | flops | bytes accessed | tf_op | source)
XLA Modules:
  0.0 92.1 jit_solution(11649915760891220070)
XLA Ops:
  0.6 1.1 %copy.12.att_ref = f32[128,3,128]{2,1,0:T(4,128)S(1)} copy(f32[128,3,128]{2,0,1:T(8,128)} %param.10) | data formatting | bytes 393216 | tf_op args[1]
  1.7 0.0 copy-start.1
  1.7 0.0 copy-start.5
  1.7 1.2 %copy.11.src_ref = f32[128,5,128]{2,1,0:T(8,128)S(1)} copy(f32[128,5,128]{2,0,1:T(8,128)} %param.9) | data formatting | bytes 655360 | tf_op args[0]
  3.0 0.8 copy-done
  3.8 0.8 copy-done.2
  4.6 0.8 copy-done.3
  5.5 0.7 copy-done.4
  6.1 0.7 copy-done.6
  6.8 0.7 copy-done.8
  7.5 0.7 copy-done.9
  8.1 8.5 %first.1 = (f32[128,24,128]{2,1,0:T(8,128)S(1)}, f32[384,128]{1,0:T(8,128)}, f32[120,128]{1,0:T(8,128)S(1)}) custom-call(s32[128]{0:T(128)S(1)} %copy-done.4, s32[128]{0:T(128)S(1)} %copy-done.6, s32[128]{0:T(128)S(1)} %copy-done.9, f32[128,5,128]{2,1,0:T(8,128)S(1)} %copy.11.src_ref, f32[128,3,128]{2,1,0:T(4,128)S(1)} %copy.12.att_ref, ...), custom_call_target="tpu_custom_call" | custom-call | tf_op jit(solution)/shard_map/first/pallas_call | solution.py:499
  16.6 5.2 %all-to-all-start = ((f32[8,48,128]{2,1,0:T(8,128)}), f32[8,48,128]{2,1,0:T(8,128)S(1)}, u32[]{:S(2)}, u32[]{:S(2)}) async-start(f32[8,48,128]{2,1,0:T(8,128)} %bitcast), calls=%async_computation | async-start | bytes 393216 | tf_op jit(solution)/shard_map/all_to_all | solution.py:492
  21.8 3.6 %collective-permute-start.2 = (f32[120,128]{1,0:T(8,128)S(1)}, f32[120,128]{1,0:T(8,128)S(1)}, u32[]{:S(2)}, u32[]{:S(2)}) collective-permute-start(f32[120,128]{1,0:T(8,128)S(1)} %get-tuple-element.19.refs_1_), channel_id=1, source_target_pairs={{0,24},{8,16},{16,8},{24,0},{1,25},{9,17},{17,9},{25,1},{2,26},{10... | collective-permute-start | bytes 184328 | tf_op jit(solution)/shard_map/ppermute | solution.py:496
  25.4 0.8 collective-permute-start
  26.2 2.0 %collective-permute-done.2.refs_4_ = f32[120,128]{1,0:T(8,128)S(1)} collective-permute-done((f32[120,128]{1,0:T(8,128)S(1)}, f32[120,128]{1,0:T(8,128)S(1)}, u32[]{:S(2)}, u32[]{:S(2)}) %collective-permute-start.2) | collective-permute-done | bytes 61472 | tf_op jit(solution)/shard_map/ppermute | solution.py:496
  28.2 3.0 %collective-permute-done.1.refs_3_ = f32[120,128]{1,0:T(8,128)S(1)} collective-permute-done((f32[120,128]{1,0:T(8,128)S(1)}, f32[120,128]{1,0:T(8,128)S(1)}, u32[]{:S(2)}, u32[]{:S(2)}) %collective-permute-start.1) | collective-permute-done | bytes 61472 | tf_op jit(solution)/shard_map/ppermute | solution.py:496
  31.2 0.9 %owner_first.1 = (f32[5,32,128]{2,1,0:T(8,128)S(1)}, f32[120,128]{1,0:T(8,128)S(1)}, f32[8,48,128]{2,1,0:T(8,128)S(1)}, f32[8,128]{1,0:T(8,128)S(1)}) custom-call(f32[8,48,128]{2,1,0:T(8,128)S(1)} %all-to-all-done.refs_0_, f32[120,128]{1,0:T(8,128)S(1)} %get-tuple-element.19.refs_1_, f32[120,128]{1,0:T(8,128)S(1)} %collective-permute-done.refs_2_, ...), custom_call_target="tpu_custom_call" | custom-call | tf_op jit(solution)/shard_map/owner_first/pallas_call | solution.py:507
  32.1 10.0 %all_to_all.25 = f32[8,48,128]{2,1,0:T(8,128)S(1)} all-to-all(f32[8,48,128]{2,1,0:T(8,128)S(1)} %get-tuple-element.20), channel_id=1, replica_groups=mesh['src'=4,'tm'=8] {'tm'}, dimensions={0} | all-to-all | bytes 393216 | tf_op jit(solution)/shard_map/all_to_all | solution.py:492
  42.1 10.4 %middle.1 = (f32[384,128]{1,0:T(8,128)}, f32[120,128]{1,0:T(8,128)S(1)}, f32[3,32,128]{2,1,0:T(8,128)S(1)}, f32[128,128]{1,0:T(8,128)S(1)}) custom-call(s32[128]{0:T(128)S(1)} %copy-done.5, s32[128]{0:T(128)S(1)} %copy-done.7, f32[384,128]{1,0:T(8,128)S(1)} %bitcast.4, f32[120,128]{1,0:T(8,128)S(1)} %get-tuple-element.21.part_ref, ...), custom_call_target="tpu_custom_call" | custom-call | tf_op jit(solution)/shard_map/middle/pallas_call | solution.py:514
  52.5 3.4 %all-to-all-start.2 = ((f32[8,48,128]{2,1,0:T(8,128)}), f32[8,48,128]{2,1,0:T(8,128)S(1)}, u32[]{:S(2)}, u32[]{:S(2)}) async-start(f32[8,48,128]{2,1,0:T(8,128)} %bitcast.2), calls=%async_computation.2 | async-start | bytes 393216 | tf_op jit(solution)/shard_map/all_to_all | solution.py:492
  55.9 2.5 %collective-permute-start.5 = (f32[120,128]{1,0:T(8,128)S(1)}, f32[120,128]{1,0:T(8,128)S(1)}, u32[]{:S(2)}, u32[]{:S(2)}) collective-permute-start(f32[120,128]{1,0:T(8,128)S(1)} %get-tuple-element.24.refs_1_), channel_id=1, source_target_pairs={{0,24},{8,16},{16,8},{24,0},{1,25},{9,17},{17,9},{25,1},{2,26},{10... | collective-permute-start | bytes 184328 | tf_op jit(solution)/shard_map/ppermute | solution.py:496
  58.5 0.1 collective-permute-start.4
  58.6 1.8 %collective-permute-start.3 = (f32[120,128]{1,0:T(8,128)S(1)}, f32[120,128]{1,0:T(8,128)S(1)}, u32[]{:S(2)}, u32[]{:S(2)}) collective-permute-start(f32[120,128]{1,0:T(8,128)S(1)} %get-tuple-element.24.refs_1_), channel_id=1, source_target_pairs={{0,8},{8,0},{16,24},{24,16},{1,9},{9,1},{17,25},{25,17},{2,10},{10... | collective-permute-start | bytes 184328 | tf_op jit(solution)/shard_map/ppermute | solution.py:496
  60.4 2.3 %collective-permute-done.5.refs_4_ = f32[120,128]{1,0:T(8,128)S(1)} collective-permute-done((f32[120,128]{1,0:T(8,128)S(1)}, f32[120,128]{1,0:T(8,128)S(1)}, u32[]{:S(2)}, u32[]{:S(2)}) %collective-permute-start.5) | collective-permute-done | bytes 61472 | tf_op jit(solution)/shard_map/ppermute | solution.py:496
  62.7 2.0 %collective-permute-done.4.refs_3_ = f32[120,128]{1,0:T(8,128)S(1)} collective-permute-done((f32[120,128]{1,0:T(8,128)S(1)}, f32[120,128]{1,0:T(8,128)S(1)}, u32[]{:S(2)}, u32[]{:S(2)}) %collective-permute-start.4) | collective-permute-done | bytes 61472 | tf_op jit(solution)/shard_map/ppermute | solution.py:496
  64.7 1.0 %owner_second.1 = (f32[5,32,128]{2,1,0:T(8,128)S(1)}, f32[120,128]{1,0:T(8,128)S(1)}, f32[8,48,128]{2,1,0:T(8,128)S(1)}) custom-call(f32[8,48,128]{2,1,0:T(8,128)S(1)} %all-to-all-done.2.refs_0_, f32[120,128]{1,0:T(8,128)S(1)} %get-tuple-element.24.refs_1_, f32[120,128]{1,0:T(8,128)S(1)} %collective-permute-done.3.refs_2_, ...), custom_call_target="tpu_custom_call" | custom-call | tf_op jit(solution)/shard_map/owner_second/pallas_call | solution.py:523
  65.7 10.1 %all_to_all.26 = f32[8,48,128]{2,1,0:T(8,128)S(1)} all-to-all(f32[8,48,128]{2,1,0:T(8,128)S(1)} %get-tuple-element.27), channel_id=1, replica_groups=mesh['src'=4,'tm'=8] {'tm'}, dimensions={0} | all-to-all | bytes 393216 | tf_op jit(solution)/shard_map/all_to_all | solution.py:492
  75.8 5.0 %last.1 = (f32[3,32,128]{2,1,0:T(8,128)S(1)}, f32[32,1,128]{2,1,0:T(1,128)S(1)}) custom-call(s32[128]{0:T(128)S(1)} %copy-done.5, s32[128]{0:T(128)S(1)} %copy-done.7, f32[384,128]{1,0:T(8,128)S(1)} %bitcast.5, f32[120,128]{1,0:T(8,128)S(1)} %get-tuple-element.28.part_ref, f32[128,24,128]{2,1,0:T(8,128)S(1)} %get-tuple-element.22.design, ...), custom_call_target="tpu_custom_call" | custom-call | tf_op jit(solution)/shard_map/last/pallas_call | solution.py:530
  80.8 9.5 %all_to_all.27.got_ref = f32[32,1,128]{2,1,0:T(1,128)S(1)} all-to-all(f32[32,1,128]{2,1,0:T(1,128)S(1)} %get-tuple-element.31), channel_id=1, replica_groups=mesh['src'=4,'tm'=8] {'src','tm'}, dimensions={0} | all-to-all | bytes 32768 | tf_op jit(solution)/shard_map/all_to_all | solution.py:537
  90.3 1.1 %final.1 = (f32[32,5,128]{2,1,0:T(8,128)S(1)}, f32[3,4096]{1,0:T(4,128)}) custom-call(f32[32,1,128]{2,1,0:T(1,128)S(1)} %all_to_all.27.got_ref, f32[5,32,128]{2,1,0:T(8,128)S(1)} %get-tuple-element.26.refs_6_.z_src, f32[5,32,128]{2,1,0:T(8,128)S(1)} %get-tuple-element.32.w_src, f32[3,32,128]{2,1,0:T(8,128)S(1)} %get-tuple-element.30.before_ref.z_att, ...), custom_call_target="tpu_custom_call" | custom-call | tf_op jit(solution)/shard_map/final/pallas_call | solution.py:538
  91.4 0.7 copy.13
  (16 shorter events, 0.0 us)
Async XLA Ops:
  1.7 40.4 %copy-start.1 = (s32[128,128]{1,0:T(8,128)S(1)}, s32[128,128]{1,0:T(8,128)}, u32[]{:S(2)}) copy-start(s32[128,128]{1,0:T(8,128)} %knot_ref.5) | copy-start | bytes 196612
  1.7 40.4 %copy-start.5 = (s32[128]{0:T(128)S(1)}, s32[128]{0:T(128)}, u32[]{:S(2)}) copy-start(s32[128]{0:T(128)} %slot_ref.5) | copy-start | bytes 1540
  1.7 40.4 %copy-start.7 = (s32[128]{0:T(128)S(1)}, s32[128]{0:T(128)}, u32[]{:S(2)}) copy-start(s32[128]{0:T(128)} %offset_ref.5) | copy-start | bytes 1540
  2.9 0.8 copy-start
  3.8 0.8 copy-start.2
  4.6 0.8 copy-start.3
  5.5 0.7 copy-start.4
  6.1 0.7 copy-start.6
  6.8 0.7 copy-start.8
  7.5 0.7 copy-start.9
  16.6 14.6 %all-to-all-start = ((f32[8,48,128]{2,1,0:T(8,128)}), f32[8,48,128]{2,1,0:T(8,128)S(1)}, u32[]{:S(2)}, u32[]{:S(2)}) async-start(f32[8,48,128]{2,1,0:T(8,128)} %bitcast), calls=%async_computation | async-start | bytes 393216 | tf_op jit(solution)/shard_map/all_to_all | solution.py:492
  21.8 6.4 %collective-permute-start.2 = (f32[120,128]{1,0:T(8,128)S(1)}, f32[120,128]{1,0:T(8,128)S(1)}, u32[]{:S(2)}, u32[]{:S(2)}) collective-permute-start(f32[120,128]{1,0:T(8,128)S(1)} %get-tuple-element.19.refs_1_), channel_id=1, source_target_pairs={{0,24},{8,16},{16,8},{24,0},{1,25},{9,17},{17,9},{25,1},{2,26},{10... | collective-permute-start | bytes 184328 | tf_op jit(solution)/shard_map/ppermute | solution.py:496
  25.4 5.8 %collective-permute-start.1 = (f32[120,128]{1,0:T(8,128)S(1)}, f32[120,128]{1,0:T(8,128)S(1)}, u32[]{:S(2)}, u32[]{:S(2)}) collective-permute-start(f32[120,128]{1,0:T(8,128)S(1)} %get-tuple-element.19.refs_1_), channel_id=1, source_target_pairs={{0,16},{8,24},{16,0},{24,8},{1,17},{9,25},{17,1},{25,9},{2,18},{10... | collective-permute-start | bytes 184328 | tf_op jit(solution)/shard_map/ppermute | solution.py:496
  25.4 5.8 %collective-permute-start = (f32[120,128]{1,0:T(8,128)S(1)}, f32[120,128]{1,0:T(8,128)S(1)}, u32[]{:S(2)}, u32[]{:S(2)}) collective-permute-start(f32[120,128]{1,0:T(8,128)S(1)} %get-tuple-element.19.refs_1_), channel_id=1, source_target_pairs={{0,8},{8,0},{16,24},{24,16},{1,9},{9,1},{17,25},{25,17},{2,10},{10... | collective-permute-start | bytes 184328 | tf_op jit(solution)/shard_map/ppermute | solution.py:496
  52.5 12.2 %all-to-all-start.2 = ((f32[8,48,128]{2,1,0:T(8,128)}), f32[8,48,128]{2,1,0:T(8,128)S(1)}, u32[]{:S(2)}, u32[]{:S(2)}) async-start(f32[8,48,128]{2,1,0:T(8,128)} %bitcast.2), calls=%async_computation.2 | async-start | bytes 393216 | tf_op jit(solution)/shard_map/all_to_all | solution.py:492
  55.9 6.8 %collective-permute-start.5 = (f32[120,128]{1,0:T(8,128)S(1)}, f32[120,128]{1,0:T(8,128)S(1)}, u32[]{:S(2)}, u32[]{:S(2)}) collective-permute-start(f32[120,128]{1,0:T(8,128)S(1)} %get-tuple-element.24.refs_1_), channel_id=1, source_target_pairs={{0,24},{8,16},{16,8},{24,0},{1,25},{9,17},{17,9},{25,1},{2,26},{10... | collective-permute-start | bytes 184328 | tf_op jit(solution)/shard_map/ppermute | solution.py:496
  58.5 6.3 %collective-permute-start.4 = (f32[120,128]{1,0:T(8,128)S(1)}, f32[120,128]{1,0:T(8,128)S(1)}, u32[]{:S(2)}, u32[]{:S(2)}) collective-permute-start(f32[120,128]{1,0:T(8,128)S(1)} %get-tuple-element.24.refs_1_), channel_id=1, source_target_pairs={{0,16},{8,24},{16,0},{24,8},{1,17},{9,25},{17,1},{25,9},{2,18},{10... | collective-permute-start | bytes 184328 | tf_op jit(solution)/shard_map/ppermute | solution.py:496
  58.6 6.1 %collective-permute-start.3 = (f32[120,128]{1,0:T(8,128)S(1)}, f32[120,128]{1,0:T(8,128)S(1)}, u32[]{:S(2)}, u32[]{:S(2)}) collective-permute-start(f32[120,128]{1,0:T(8,128)S(1)} %get-tuple-element.24.refs_1_), channel_id=1, source_target_pairs={{0,8},{8,0},{16,24},{24,16},{1,9},{9,1},{17,25},{25,17},{2,10},{10... | collective-permute-start | bytes 184328 | tf_op jit(solution)/shard_map/ppermute | solution.py:496

commit v2 on v1

--- a/solution.py
+++ b/solution.py
@@ -20,7 +20,7 @@
 CAP = 8
 EXTRA = PARAMS * CAP
 PIECE = EXTRA + 8
-UNROLL = 4
+UNROLL = 32
 F32 = jnp.float32
 BF16 = jnp.bfloat16
 
@@ -62,14 +62,15 @@
 
 
 def add_adjoint(tiles, values, design, slot_ref, offset_ref, knot_ref, acc, knots):
-    lane_row = iota((LANES, LANES), 0).astype(F32)
+    lane_row = iota((LANES, LANES), 0).astype(F32).astype(BF16)
+    yes, no = jnp.ones((), BF16), jnp.zeros((), BF16)
     outs = []
     for t, resid in zip(tiles, values):
         shift = offset_ref[t] % LANES
         place = knot_ref[pl.ds(t, 1), :] + shift
         first = place < LANES
         lane = jnp.where(first, place, place - LANES)
-        hot = (lane_row == lane.astype(F32)).astype(BF16)
+        hot = jnp.where(lane_row == lane.astype(F32).astype(BF16), yes, no)
         spread = jnp.concatenate([design[t, 0:8, :] * resid, design[t, 8:16, :] * resid], axis=0)
         mask = jnp.broadcast_to(first.astype(F32), spread.shape)
         here = spread * mask
@@ -111,6 +112,21 @@
 
 
 def first_kernel(
+    slot_hbm,
+    offset_hbm,
+    valid_hbm,
+    src_hbm,
+    att_hbm,
+    frac_hbm,
+    knot_hbm,
+    obs_hbm,
+    table_hbm,
+    design,
+    piece_ref,
+    part_ref,
+    acc,
+    knots,
+    wts,
     slot_ref,
     offset_ref,
     valid_ref,
@@ -120,18 +136,29 @@
     knot_ref,
     obs_ref,
     table_ref,
-    design,
-    piece_ref,
-    part_ref,
-    acc,
-    knots,
-    wts,
+    sems,
 ):
-    tiles = src_ref.shape[0]
+    pairs = (
+        (frac_hbm, frac_ref),
+        (offset_hbm, offset_ref),
+        (valid_hbm, valid_ref),
+        (slot_hbm, slot_ref),
+        (knot_hbm, knot_ref),
+        (obs_hbm, obs_ref),
+        (att_hbm, att_ref),
+        (src_hbm, src_ref),
+        (table_hbm, table_ref),
+    )
+    copies = [pltpu.make_async_copy(a, b, sems.at[k]) for k, (a, b) in enumerate(pairs)]
+    for copy in copies:
+        copy.start()
+    tiles = knot_ref.shape[0]
     owners = table_ref.shape[0]
     acc[...] = jnp.zeros_like(acc)
     knots[...] = jnp.zeros_like(knots)
     part_ref[...] = jnp.zeros_like(part_ref)
+    for copy in copies:
+        copy.wait()
     for k, weight in enumerate(spline_weights(frac_ref[...])):
         wts[k] = weight
     sub = iota((8, LANES), 0)
@@ -141,7 +168,7 @@
         batch = [step * UNROLL + k for k in range(UNROLL)]
         for t in batch:
             live = lane < valid_ref[t]
-            three = [row_of(att_ref.at[t], axis) for axis in range(AXES)]
+            three = [row_of(att_ref, axis * tiles + t) for axis in range(AXES)]
             axis_of = sub % 4
             mixed = jnp.where(axis_of == 0, three[0], jnp.where(axis_of == 1, three[1], three[2]))
             mixed = jnp.where(live & (axis_of < 3), mixed, 0.0)
@@ -149,7 +176,9 @@
             design[t, 0:8, :] = mixed * jnp.where(sub < 4, weights[0], weights[1])
             design[t, 8:16, :] = mixed * jnp.where(sub < 4, weights[2], weights[3])
             design[t, 16:24, :] = jnp.zeros((8, LANES), F32)
-            design[t, 16 : 16 + PARAMS, :] = jnp.where(live[0:PARAMS], src_ref[t], 0.0)
+            design[t, 16 : 16 + PARAMS, :] = jnp.where(
+                live[0:PARAMS], src_ref[pl.ds(t, PARAMS, stride=tiles), :], 0.0
+            )
         values = [row_of(obs_ref, t) for t in batch]
         add_adjoint(batch, values, design, slot_ref, offset_ref, knot_ref, acc, knots)
         return carry
@@ -438,7 +467,7 @@
     c_z = alpha * (1.0 + second * tau)
     c_w = alpha * second
     for param in range(PARAMS):
-        src_out[:, param, :] = c_z * z_src[param] - c_w * w_src[param]
+        src_out[param] = c_z * z_src[param] - c_w * w_src[param]
     for axis in range(AXES):
         value = c_z * z_att[axis] - c_w * w_att[axis]
         for row in range(ROWS):
@@ -447,6 +476,7 @@
 
 VMEM = pl.BlockSpec(memory_space=pltpu.VMEM)
 SMEM = pl.BlockSpec(memory_space=pltpu.SMEM)
+HBM = pl.BlockSpec(memory_space=pltpu.HBM)
 PARAMETERS = pltpu.CompilerParams(vmem_limit_bytes=24 * 1024 * 1024)
 
 
@@ -496,13 +526,19 @@
             lax.ppermute(own, "src", [(i, i ^ k) for i in range(copies)]) for k in range(1, copies)
         ]
 
+    src_rows = jnp.transpose(src_design, (1, 0, 2)).reshape(PARAMS * tiles, LANES)
+    att_rows = jnp.transpose(att_design, (1, 0, 2)).reshape(AXES * tiles, LANES)
+    inputs = (tile_slot, tile_offset, tile_valid, src_rows, att_rows, obs_frac, obs_knot, observed, slot_block)
     design, pieces, own = call(
         first_kernel,
         (f32(tiles, 24, LANES), piece, part),
-        [SMEM] * 3 + [VMEM] * 6,
-        [acc, knots, pltpu.VMEM((4, tiles, LANES), F32)],
+        [HBM] * len(inputs),
+        [acc, knots, pltpu.VMEM((4, tiles, LANES), F32)]
+        + [pltpu.SMEM((tiles,), jnp.int32)] * 3
+        + [pltpu.VMEM(value.shape, value.dtype) for value in inputs[3:]]
+        + [pltpu.SemaphoreType.DMA((len(inputs),))],
         "first",
-    )(tile_slot, tile_offset, tile_valid, src_design, att_design, obs_frac, obs_knot, observed, slot_block)
+    )(*[pltpu.with_memory_space_constraint(value, pltpu.HBM) for value in inputs])
     got, parts = exchange(pieces), src_parts(own)
     z_src, z_part, back, names = call(
         functools.partial(owner_kernel, copies, True),
@@ -535,12 +571,13 @@
         "last",
     )(tile_slot, tile_offset, got, w_part, design, obs_knot, y, numbers, z_att)
     row = lax.all_to_all(row, ("src", "tm"), 0, 0, tiled=True)
-    return call(
+    src, att = call(
         final_kernel,
-        (f32(SB_DEV, PARAMS, LANES), f32(AXES, KN)),
+        (f32(PARAMS, SB_DEV, LANES), f32(AXES, KN)),
         [VMEM] * 5,
         name="final",
     )(row, z_src, w_src, z_att, w_att)
+    return jnp.transpose(src, (1, 0, 2)), att
 
 
 def solution(mesh):

time: 92.8 us -> 74.3 us (0.80)
  Pallas kernels: 26.9 us -> 16.7 us
  local copies, waits for them, and re-layouts: 8.1 us -> 0.01 us
    unnamed x22 -> x6, local copies, waits for them, and re-layouts: 7.45 us -> 0.01 us
    pallas_call x1, Pallas kernels: 10.4 us -> 5.41 us  [shards(): call(functools.partial(middle_kernel, copies), (piece, part, true, f32(ti...]
    pallas_call x2, Pallas kernels: 9.57 us -> 6.66 us  [the longest x1 5.61 us: shards(): call(first_kernel, (f32(tiles, 24, LANES), piece, part), [HBM] * len(inpu...]
    pallas_call x1, Pallas kernels: 5 us -> 2.74 us  [shards(): call(functools.partial(last_kernel, copies), (true, f32(devices, 1, LANES...]
where the time goes in v2:
time: 74.3 us; the launch traced here: 73.9 us
  blocking collectives  29.7 us (40%)
  starting transfers between devices  17.4 us (23%)
  Pallas kernels  16.7 us (22%)
  waiting for transfers between devices  9.34 us (13%)
    all_to_all x2, blocking collectives, exchange(): lax.all_to_all(pieces.reshape(owners, PIECE, LANES), 'tm', 0, 0, tiled=True)  20.1 us
    all_to_all x1, blocking collectives, shards(): row = lax.all_to_all(row, ('src', 'tm'), 0, 0, tiled=True)  9.54 us
    ppermute x6, waiting for transfers between devices, src_parts(): lax.ppermute(own, 'src', [(i, i ^ k) for i in range(copies)])  9.34 us
    ppermute x6, starting transfers between devices, src_parts(): lax.ppermute(own, 'src', [(i, i ^ k) for i in range(copies)])  8.84 us
    all_to_all x2, starting transfers between devices, exchange(): lax.all_to_all(pieces.reshape(owners, PIECE, LANES), 'tm', 0, 0, tiled=True)  8.57 us
    pallas_call x1, Pallas kernels, shards(): call(first_kernel, (f32(tiles, 24, LANES), piece, part), [HBM] * len(inpu...  5.61 us
    pallas_call x1, Pallas kernels, shards(): call(functools.partial(middle_kernel, copies), (piece, part, true, f32(ti...  5.41 us
    pallas_call x1, Pallas kernels, shards(): call(functools.partial(last_kernel, copies), (true, f32(devices, 1, LANES...  2.74 us
  transfers between devices with their start and end apart: 8, of which 4 were waited for; matrix products, arithmetic and copies ran while one was open for 0% of the time, Pallas kernels for 0%

profile of v2, /device:TPU:0, one launch (start us, length us, event | category | flops | bytes accessed | tf_op | source)
XLA Modules:
  0.0 73.9 jit_solution(1125119277647590433)
XLA Ops:
  0.6 0.0 copy-start.2
  0.6 0.0 copy-start.1
  0.7 0.0 copy-start
  0.7 5.6 %first.1 = (f32[128,24,128]{2,1,0:T(8,128)S(1)}, f32[384,128]{1,0:T(8,128)}, f32[120,128]{1,0:T(8,128)S(1)}) custom-call(s32[128]{0:T(128)} %slot_ref.3, s32[128]{0:T(128)} %offset_ref.3, s32[128]{0:T(128)} %valid_hbm.1, f32[640,128]{1,0:T(8,128)} %bitcast.13, f32[384,128]{1,0:T(8,128)} %bitcast.14, f32[128,128]{1,0:T(8,128)} %frac_hbm.1, ...), custom_call_target="tpu_custom_call" | custom-call | tf_op jit(solution)/shard_map/first/pallas_call | solution.py:532
  6.3 5.2 %all-to-all-start = ((f32[8,48,128]{2,1,0:T(8,128)}), f32[8,48,128]{2,1,0:T(8,128)S(1)}, u32[]{:S(2)}, u32[]{:S(2)}) async-start(f32[8,48,128]{2,1,0:T(8,128)} %bitcast.4), calls=%async_computation | async-start | bytes 393216 | tf_op jit(solution)/shard_map/all_to_all | solution.py:522
  11.5 3.6 %collective-permute-start.2 = (f32[120,128]{1,0:T(8,128)S(1)}, f32[120,128]{1,0:T(8,128)S(1)}, u32[]{:S(2)}, u32[]{:S(2)}) collective-permute-start(f32[120,128]{1,0:T(8,128)S(1)} %get-tuple-element.21.refs_1_), channel_id=1, source_target_pairs={{0,24},{8,16},{16,8},{24,0},{1,25},{9,17},{17,9},{25,1},{2,26},{10... | collective-permute-start | bytes 184328 | tf_op jit(solution)/shard_map/ppermute | solution.py:526
  15.1 0.0 collective-permute-start.1
  15.1 0.8 %collective-permute-start = (f32[120,128]{1,0:T(8,128)S(1)}, f32[120,128]{1,0:T(8,128)S(1)}, u32[]{:S(2)}, u32[]{:S(2)}) collective-permute-start(f32[120,128]{1,0:T(8,128)S(1)} %get-tuple-element.21.refs_1_), channel_id=1, source_target_pairs={{0,8},{8,0},{16,24},{24,16},{1,9},{9,1},{17,25},{25,17},{2,10},{10... | collective-permute-start | bytes 184328 | tf_op jit(solution)/shard_map/ppermute | solution.py:526
  15.9 2.0 %collective-permute-done.2.refs_4_ = f32[120,128]{1,0:T(8,128)S(1)} collective-permute-done((f32[120,128]{1,0:T(8,128)S(1)}, f32[120,128]{1,0:T(8,128)S(1)}, u32[]{:S(2)}, u32[]{:S(2)}) %collective-permute-start.2) | collective-permute-done | bytes 61472 | tf_op jit(solution)/shard_map/ppermute | solution.py:526
  17.9 3.0 %collective-permute-done.1.refs_3_ = f32[120,128]{1,0:T(8,128)S(1)} collective-permute-done((f32[120,128]{1,0:T(8,128)S(1)}, f32[120,128]{1,0:T(8,128)S(1)}, u32[]{:S(2)}, u32[]{:S(2)}) %collective-permute-start.1) | collective-permute-done | bytes 61472 | tf_op jit(solution)/shard_map/ppermute | solution.py:526
  20.8 0.0 collective-permute-done.refs_2_
  20.8 0.0 all-to-all-done.refs_0_
  20.8 0.9 %owner_first.1 = (f32[5,32,128]{2,1,0:T(8,128)S(1)}, f32[120,128]{1,0:T(8,128)S(1)}, f32[8,48,128]{2,1,0:T(8,128)S(1)}, f32[8,128]{1,0:T(8,128)S(1)}) custom-call(f32[8,48,128]{2,1,0:T(8,128)S(1)} %all-to-all-done.refs_0_, f32[120,128]{1,0:T(8,128)S(1)} %get-tuple-element.21.refs_1_, f32[120,128]{1,0:T(8,128)S(1)} %collective-permute-done.refs_2_, ...), custom_call_target="tpu_custom_call" | custom-call | tf_op jit(solution)/shard_map/owner_first/pallas_call | solution.py:543
  21.8 10.0 %all_to_all.25 = f32[8,48,128]{2,1,0:T(8,128)S(1)} all-to-all(f32[8,48,128]{2,1,0:T(8,128)S(1)} %get-tuple-element.22), channel_id=1, replica_groups=mesh['src'=4,'tm'=8] {'tm'}, dimensions={0} | all-to-all | bytes 393216 | tf_op jit(solution)/shard_map/all_to_all | solution.py:522
  31.8 0.0 copy-done.2
  31.8 0.0 copy-done.1
  31.8 0.0 copy-done
  31.8 5.4 %middle.1 = (f32[384,128]{1,0:T(8,128)}, f32[120,128]{1,0:T(8,128)S(1)}, f32[3,32,128]{2,1,0:T(8,128)S(1)}, f32[128,128]{1,0:T(8,128)S(1)}) custom-call(s32[128]{0:T(128)S(1)} %copy-done.1, s32[128]{0:T(128)S(1)} %copy-done.2, f32[384,128]{1,0:T(8,128)S(1)} %bitcast.11, f32[120,128]{1,0:T(8,128)S(1)} %get-tuple-element.23.part_ref, ...), custom_call_target="tpu_custom_call" | custom-call | tf_op jit(solution)/shard_map/middle/pallas_call | solution.py:550
  37.2 3.4 %all-to-all-start.2 = ((f32[8,48,128]{2,1,0:T(8,128)}), f32[8,48,128]{2,1,0:T(8,128)S(1)}, u32[]{:S(2)}, u32[]{:S(2)}) async-start(f32[8,48,128]{2,1,0:T(8,128)} %bitcast.6), calls=%async_computation.2 | async-start | bytes 393216 | tf_op jit(solution)/shard_map/all_to_all | solution.py:522
  40.6 2.6 %collective-permute-start.5 = (f32[120,128]{1,0:T(8,128)S(1)}, f32[120,128]{1,0:T(8,128)S(1)}, u32[]{:S(2)}, u32[]{:S(2)}) collective-permute-start(f32[120,128]{1,0:T(8,128)S(1)} %get-tuple-element.26.refs_1_), channel_id=1, source_target_pairs={{0,24},{8,16},{16,8},{24,0},{1,25},{9,17},{17,9},{25,1},{2,26},{10... | collective-permute-start | bytes 184328 | tf_op jit(solution)/shard_map/ppermute | solution.py:526
  43.2 0.1 collective-permute-start.4
  43.3 1.8 %collective-permute-start.3 = (f32[120,128]{1,0:T(8,128)S(1)}, f32[120,128]{1,0:T(8,128)S(1)}, u32[]{:S(2)}, u32[]{:S(2)}) collective-permute-start(f32[120,128]{1,0:T(8,128)S(1)} %get-tuple-element.26.refs_1_), channel_id=1, source_target_pairs={{0,8},{8,0},{16,24},{24,16},{1,9},{9,1},{17,25},{25,17},{2,10},{10... | collective-permute-start | bytes 184328 | tf_op jit(solution)/shard_map/ppermute | solution.py:526
  45.1 2.3 %collective-permute-done.5.refs_4_ = f32[120,128]{1,0:T(8,128)S(1)} collective-permute-done((f32[120,128]{1,0:T(8,128)S(1)}, f32[120,128]{1,0:T(8,128)S(1)}, u32[]{:S(2)}, u32[]{:S(2)}) %collective-permute-start.5) | collective-permute-done | bytes 61472 | tf_op jit(solution)/shard_map/ppermute | solution.py:526
  47.4 2.0 %collective-permute-done.4.refs_3_ = f32[120,128]{1,0:T(8,128)S(1)} collective-permute-done((f32[120,128]{1,0:T(8,128)S(1)}, f32[120,128]{1,0:T(8,128)S(1)}, u32[]{:S(2)}, u32[]{:S(2)}) %collective-permute-start.4) | collective-permute-done | bytes 61472 | tf_op jit(solution)/shard_map/ppermute | solution.py:526
  49.4 0.0 collective-permute-done.3.refs_2_
  49.4 0.0 all-to-all-done.2.refs_0_
  49.5 1.0 %owner_second.1 = (f32[5,32,128]{2,1,0:T(8,128)S(1)}, f32[120,128]{1,0:T(8,128)S(1)}, f32[8,48,128]{2,1,0:T(8,128)S(1)}) custom-call(f32[8,48,128]{2,1,0:T(8,128)S(1)} %all-to-all-done.2.refs_0_, f32[120,128]{1,0:T(8,128)S(1)} %get-tuple-element.26.refs_1_, f32[120,128]{1,0:T(8,128)S(1)} %collective-permute-done.3.refs_2_, ...), custom_call_target="tpu_custom_call" | custom-call | tf_op jit(solution)/shard_map/owner_second/pallas_call | solution.py:559
  50.4 10.1 %all_to_all.26 = f32[8,48,128]{2,1,0:T(8,128)S(1)} all-to-all(f32[8,48,128]{2,1,0:T(8,128)S(1)} %get-tuple-element.29), channel_id=1, replica_groups=mesh['src'=4,'tm'=8] {'tm'}, dimensions={0} | all-to-all | bytes 393216 | tf_op jit(solution)/shard_map/all_to_all | solution.py:522
  60.5 2.7 %last.1 = (f32[3,32,128]{2,1,0:T(8,128)S(1)}, f32[32,1,128]{2,1,0:T(1,128)S(1)}) custom-call(s32[128]{0:T(128)S(1)} %copy-done.1, s32[128]{0:T(128)S(1)} %copy-done.2, f32[384,128]{1,0:T(8,128)S(1)} %bitcast.12, f32[120,128]{1,0:T(8,128)S(1)} %get-tuple-element.30.part_ref, f32[128,24,128]{2,1,0:T(8,128)S(1)} %get-tuple-element.24.design, ...), custom_call_target="tpu_custom_call" | custom-call | tf_op jit(solution)/shard_map/last/pallas_call | solution.py:566
  63.3 9.5 %all_to_all.27.got_ref = f32[32,1,128]{2,1,0:T(1,128)S(1)} all-to-all(f32[32,1,128]{2,1,0:T(1,128)S(1)} %get-tuple-element.33), channel_id=1, replica_groups=mesh['src'=4,'tm'=8] {'src','tm'}, dimensions={0} | all-to-all | bytes 32768 | tf_op jit(solution)/shard_map/all_to_all | solution.py:573
  72.8 1.0 %final.1 = (f32[5,32,128]{2,1,0:T(8,128)}, f32[3,4096]{1,0:T(4,128)}) custom-call(f32[32,1,128]{2,1,0:T(1,128)S(1)} %all_to_all.27.got_ref, f32[5,32,128]{2,1,0:T(8,128)S(1)} %get-tuple-element.28.refs_6_.z_src, f32[5,32,128]{2,1,0:T(8,128)S(1)} %get-tuple-element.34.w_src, f32[3,32,128]{2,1,0:T(8,128)S(1)} %get-tuple-element.32.before_ref.z_att, ...), custom_call_target="tpu_custom_call" | custom-call | tf_op jit(solution)/shard_map/final/pallas_call | solution.py:574
Async XLA Ops:
  0.6 31.2 %copy-start.2 = (s32[128]{0:T(128)S(1)}, s32[128]{0:T(128)}, u32[]{:S(2)}) copy-start(s32[128]{0:T(128)} %offset_ref.3) | copy-start | bytes 1540
  0.6 31.2 %copy-start.1 = (s32[128]{0:T(128)S(1)}, s32[128]{0:T(128)}, u32[]{:S(2)}) copy-start(s32[128]{0:T(128)} %slot_ref.3) | copy-start | bytes 1540
  0.7 31.2 %copy-start = (s32[128,128]{1,0:T(8,128)S(1)}, s32[128,128]{1,0:T(8,128)}, u32[]{:S(2)}) copy-start(s32[128,128]{1,0:T(8,128)} %knot_ref.3) | copy-start | bytes 196612
  6.3 14.6 %all-to-all-start = ((f32[8,48,128]{2,1,0:T(8,128)}), f32[8,48,128]{2,1,0:T(8,128)S(1)}, u32[]{:S(2)}, u32[]{:S(2)}) async-start(f32[8,48,128]{2,1,0:T(8,128)} %bitcast.4), calls=%async_computation | async-start | bytes 393216 | tf_op jit(solution)/shard_map/all_to_all | solution.py:522
  11.5 6.4 %collective-permute-start.2 = (f32[120,128]{1,0:T(8,128)S(1)}, f32[120,128]{1,0:T(8,128)S(1)}, u32[]{:S(2)}, u32[]{:S(2)}) collective-permute-start(f32[120,128]{1,0:T(8,128)S(1)} %get-tuple-element.21.refs_1_), channel_id=1, source_target_pairs={{0,24},{8,16},{16,8},{24,0},{1,25},{9,17},{17,9},{25,1},{2,26},{10... | collective-permute-start | bytes 184328 | tf_op jit(solution)/shard_map/ppermute | solution.py:526
  15.1 5.8 %collective-permute-start.1 = (f32[120,128]{1,0:T(8,128)S(1)}, f32[120,128]{1,0:T(8,128)S(1)}, u32[]{:S(2)}, u32[]{:S(2)}) collective-permute-start(f32[120,128]{1,0:T(8,128)S(1)} %get-tuple-element.21.refs_1_), channel_id=1, source_target_pairs={{0,16},{8,24},{16,0},{24,8},{1,17},{9,25},{17,1},{25,9},{2,18},{10... | collective-permute-start | bytes 184328 | tf_op jit(solution)/shard_map/ppermute | solution.py:526
  15.1 5.8 %collective-permute-start = (f32[120,128]{1,0:T(8,128)S(1)}, f32[120,128]{1,0:T(8,128)S(1)}, u32[]{:S(2)}, u32[]{:S(2)}) collective-permute-start(f32[120,128]{1,0:T(8,128)S(1)} %get-tuple-element.21.refs_1_), channel_id=1, source_target_pairs={{0,8},{8,0},{16,24},{24,16},{1,9},{9,1},{17,25},{25,17},{2,10},{10... | collective-permute-start | bytes 184328 | tf_op jit(solution)/shard_map/ppermute | solution.py:526
  37.2 12.2 %all-to-all-start.2 = ((f32[8,48,128]{2,1,0:T(8,128)}), f32[8,48,128]{2,1,0:T(8,128)S(1)}, u32[]{:S(2)}, u32[]{:S(2)}) async-start(f32[8,48,128]{2,1,0:T(8,128)} %bitcast.6), calls=%async_computation.2 | async-start | bytes 393216 | tf_op jit(solution)/shard_map/all_to_all | solution.py:522
  40.6 6.8 %collective-permute-start.5 = (f32[120,128]{1,0:T(8,128)S(1)}, f32[120,128]{1,0:T(8,128)S(1)}, u32[]{:S(2)}, u32[]{:S(2)}) collective-permute-start(f32[120,128]{1,0:T(8,128)S(1)} %get-tuple-element.26.refs_1_), channel_id=1, source_target_pairs={{0,24},{8,16},{16,8},{24,0},{1,25},{9,17},{17,9},{25,1},{2,26},{10... | collective-permute-start | bytes 184328 | tf_op jit(solution)/shard_map/ppermute | solution.py:526
  43.2 6.2 %collective-permute-start.4 = (f32[120,128]{1,0:T(8,128)S(1)}, f32[120,128]{1,0:T(8,128)S(1)}, u32[]{:S(2)}, u32[]{:S(2)}) collective-permute-start(f32[120,128]{1,0:T(8,128)S(1)} %get-tuple-element.26.refs_1_), channel_id=1, source_target_pairs={{0,16},{8,24},{16,0},{24,8},{1,17},{9,25},{17,1},{25,9},{2,18},{10... | collective-permute-start | bytes 184328 | tf_op jit(solution)/shard_map/ppermute | solution.py:526
  43.3 6.1 %collective-permute-start.3 = (f32[120,128]{1,0:T(8,128)S(1)}, f32[120,128]{1,0:T(8,128)S(1)}, u32[]{:S(2)}, u32[]{:S(2)}) collective-permute-start(f32[120,128]{1,0:T(8,128)S(1)} %get-tuple-element.26.refs_1_), channel_id=1, source_target_pairs={{0,8},{8,0},{16,24},{24,16},{1,9},{9,1},{17,25},{25,17},{2,10},{10... | collective-permute-start | bytes 184328 | tf_op jit(solution)/shard_map/ppermute | solution.py:526

commit v3 on v2

--- a/solution.py
+++ b/solution.py
@@ -14,15 +14,19 @@
 
 LANES = 128
 ROWS = KN // LANES
-ROWS_PAD = (ROWS + 8) // 8 * 8
 AXES = 3
+PART = AXES * ROWS + 8
 PARAMS = 5
 CAP = 8
 EXTRA = PARAMS * CAP
 PIECE = EXTRA + 8
-UNROLL = 32
+UNROLL = 128
 F32 = jnp.float32
 BF16 = jnp.bfloat16
+
+
+def place_of(axis, row):
+    return axis * ROWS + row if row < ROWS else AXES * ROWS + axis
 
 
 def iota(shape, dim):
@@ -61,20 +65,25 @@
     return jnp.broadcast_to(ref[pl.ds(row, 1), :], (8, LANES))
 
 
-def add_adjoint(tiles, values, design, slot_ref, offset_ref, knot_ref, acc, knots):
+def places(t, offset_ref, knot_ref):
+    place = row_of(knot_ref, t) + offset_ref[t] % LANES
+    first = place < LANES
+    return jnp.where(first, place, place - LANES), first
+
+
+def add_adjoint(tiles, values, where, design, slot_ref, offset_ref, acc, knots):
     lane_row = iota((LANES, LANES), 0).astype(F32).astype(BF16)
     yes, no = jnp.ones((), BF16), jnp.zeros((), BF16)
     outs = []
-    for t, resid in zip(tiles, values):
-        shift = offset_ref[t] % LANES
-        place = knot_ref[pl.ds(t, 1), :] + shift
-        first = place < LANES
-        lane = jnp.where(first, place, place - LANES)
+    for t, resid, (lane, first) in zip(tiles, values, where):
+        lane, first = lane[0:1], first[0:1]
         hot = jnp.where(lane_row == lane.astype(F32).astype(BF16), yes, no)
-        spread = jnp.concatenate([design[t, 0:8, :] * resid, design[t, 8:16, :] * resid], axis=0)
-        mask = jnp.broadcast_to(first.astype(F32), spread.shape)
-        here = spread * mask
-        parts = split2(here) + split2(spread - here)
+        high, low = split2(
+            jnp.concatenate([design[t, 0:8, :] * resid, design[t, 8:16, :] * resid], axis=0)
+        )
+        here = jnp.broadcast_to(jnp.where(first, 1.0, 0.0).astype(BF16), high.shape)
+        parts = (high * here, low * here)
+        parts = parts + (high - parts[0], low - parts[1])
         outs.append(
             lax.dot_general(
                 jnp.concatenate(parts, axis=0),
@@ -107,7 +116,8 @@
         both = jnp.where(low, one + moved[1], moved[0] + moved[2])
         both = both + pltpu.roll(both, 4, 0)
         for axis in range(AXES):
-            att_ref[axis * ROWS_PAD + row : axis * ROWS_PAD + row + 1, :] = both[axis : axis + 1]
+            at = place_of(axis, row)
+            att_ref[at : at + 1, :] = both[axis : axis + 1]
         before = now
 
 
@@ -146,7 +156,7 @@
         (knot_hbm, knot_ref),
         (obs_hbm, obs_ref),
         (att_hbm, att_ref),
-        (src_hbm, src_ref),
+        (src_hbm, src_ref.at[0 : src_hbm.shape[0]]),
         (table_hbm, table_ref),
     )
     copies = [pltpu.make_async_copy(a, b, sems.at[k]) for k, (a, b) in enumerate(pairs)]
@@ -175,12 +185,12 @@
             weights = [row_of(wts.at[k], t) for k in range(4)]
             design[t, 0:8, :] = mixed * jnp.where(sub < 4, weights[0], weights[1])
             design[t, 8:16, :] = mixed * jnp.where(sub < 4, weights[2], weights[3])
-            design[t, 16:24, :] = jnp.zeros((8, LANES), F32)
-            design[t, 16 : 16 + PARAMS, :] = jnp.where(
-                live[0:PARAMS], src_ref[pl.ds(t, PARAMS, stride=tiles), :], 0.0
+            design[t, 16:24, :] = jnp.where(
+                live & (sub < PARAMS), src_ref[pl.ds(t, 8, stride=tiles), :], 0.0
             )
         values = [row_of(obs_ref, t) for t in batch]
-        add_adjoint(batch, values, design, slot_ref, offset_ref, knot_ref, acc, knots)
+        where = [places(t, offset_ref, knot_ref) for t in batch]
+        add_adjoint(batch, values, where, design, slot_ref, offset_ref, acc, knots)
         return carry
 
     lax.fori_loop(0, tiles // UNROLL, body, 0)
@@ -196,12 +206,18 @@
         )
 
 
-def owner_kernel(count, with_names, *refs):
-    piece_ref, parts, rest = refs[0], refs[1 : 1 + count], refs[1 + count :]
+def att_kernel(*refs):
+    level, out_ref = [part[...] for part in refs[:-1]], refs[-1]
+    while len(level) > 1:
+        level = [level[k] + level[k + 1] for k in range(0, len(level), 2)]
+    out_ref[...] = level[0]
+
+
+def owner_kernel(with_names, piece_ref, att_ref, *rest):
     if with_names:
-        own_ref, att_ref, back_ref, names_ref = rest
+        own_ref, back_ref, names_ref = rest
     else:
-        names_in, own_in, own_ref, att_ref, back_ref = rest
+        names_in, own_in, own_ref, back_ref = rest
     owners = piece_ref.shape[0]
     rows = owners * CAP
     sub = iota((8, LANES), 0)
@@ -224,12 +240,16 @@
             sums = sums + piece_ref[owner, EXTRA : EXTRA + 8, :]
         sigma = sums[1:2, 0:1] / sums[1:2, 1:2]
         across = jnp.zeros((SB_DEV, LANES), F32)
+    got = jnp.concatenate(
+        [piece_ref[:, p * CAP : p * CAP + CAP, :].reshape(rows, LANES) for p in range(PARAMS)], axis=1
+    )
+    mine_all = jnp.dot(pick, jnp.concatenate(split3(got), axis=0), preferred_element_type=F32)
+    back = jnp.dot(give, jnp.concatenate(split3(mine_all), axis=0), preferred_element_type=F32)
     for param in range(PARAMS):
-        got = piece_ref[:, param * CAP : param * CAP + CAP, :].reshape(rows, LANES)
-        mine = jnp.dot(pick, jnp.concatenate(split3(got), axis=0), preferred_element_type=F32)
+        lanes = slice(param * LANES, param * LANES + LANES)
+        mine = mine_all[:, lanes]
         own_ref[param] = mine
-        back = jnp.dot(give, jnp.concatenate(split3(mine), axis=0), preferred_element_type=F32)
-        back_ref[:, param * CAP : param * CAP + CAP, :] = back.reshape(owners, CAP, LANES)
+        back_ref[:, param * CAP : param * CAP + CAP, :] = back[:, lanes].reshape(owners, CAP, LANES)
         if with_names:
             square = square + mine * mine
         else:
@@ -237,15 +257,11 @@
             rest_ = mine - sigma * before
             square = square + rest_ * rest_
             across = across + rest_ * before
-    level = [part[...] for part in parts]
-    while len(level) > 1:
-        level = [level[k] + level[k + 1] for k in range(0, len(level), 2)]
-    att_ref[...] = level[0]
     extra = jnp.zeros((8, LANES), F32)
     for axis in range(AXES):
-        at = axis * ROWS_PAD
-        extra = jnp.where(sub == axis, level[0][at : at + 1], extra)
-        extra = jnp.where(sub == AXES + axis, level[0][at + ROWS : at + ROWS + 1], extra)
+        for k, row in enumerate((0, ROWS)):
+            at = place_of(axis, row)
+            extra = jnp.where(sub == k * AXES + axis, att_ref[at : at + 1, :], extra)
     lane = iota((8, LANES), 1)
     numbers = jnp.where(lane == 0, total(square), 0.0)
     if not with_names:
@@ -277,7 +293,7 @@
     low = sub < 4
     axis_of = sub % 4
     for axis in range(AXES):
-        at = axis * ROWS_PAD
+        at = axis * ROWS
         true_ref[axis] = part_ref[at : at + ROWS, :]
         true_ref[axis, 0:1, :] = part_ref[at : at + 1, :] + left[AXES + axis : AXES + axis + 1]
 
@@ -286,7 +302,7 @@
             three = [true_ref[axis, row : row + 1, :] for axis in range(AXES)]
         else:
             three = [
-                right[axis : axis + 1] + has_right * part_ref[axis * ROWS_PAD + ROWS : axis * ROWS_PAD + ROWS + 1, :]
+                right[axis : axis + 1] + has_right * part_ref[AXES * ROWS + axis : AXES * ROWS + axis + 1, :]
                 for axis in range(AXES)
             ]
         three = [jnp.broadcast_to(v, (8, LANES)) for v in three]
@@ -307,14 +323,10 @@
         now, now_rolled = after, after_rolled
 
 
-def forward(tiles, design, slot_ref, offset_ref, knot_ref, slots, table):
+def forward(tiles, where, design, slot_ref, offset_ref, slots, table):
     values = []
-    for t in tiles:
-        shift = offset_ref[t] % LANES
+    for t, (lane, first) in zip(tiles, where):
         row = offset_ref[t] // LANES
-        place = row_of(knot_ref, t) + shift
-        first = place < LANES
-        lane = jnp.where(first, place, place - LANES)
         summed = design[t, 16:24, :] * slots[slot_ref[t]]
         for half in (0, 8):
             here = jnp.take_along_axis(table[row, half : half + 8, :], lane, axis=1)
@@ -350,16 +362,17 @@
     sum_ref[...] = jnp.zeros_like(sum_ref)
     load_vector(got_ref, part_ref, slots, table, true_ref)
 
-    def body(step, square):
+    def body(step, carry):
         batch = [step * UNROLL + k for k in range(UNROLL)]
-        values = forward(batch, design, slot_ref, offset_ref, knot_ref, slots, table)
+        where = [places(t, offset_ref, knot_ref) for t in batch]
+        values = forward(batch, where, design, slot_ref, offset_ref, slots, table)
         for t, value in zip(batch, values):
             y_ref[pl.ds(t, 1), :] = value[0:1]
-            square = square + value * value
-        add_adjoint(batch, values, design, slot_ref, offset_ref, knot_ref, acc, knots)
-        return square
-
-    square = lax.fori_loop(0, tiles // UNROLL, body, jnp.zeros((8, LANES), F32))
+        add_adjoint(batch, values, where, design, slot_ref, offset_ref, acc, knots)
+        return carry
+
+    lax.fori_loop(0, tiles // UNROLL, body, 0)
+    square = y_ref[...] * y_ref[...]
     send_sums(acc, knots, piece_ref, sum_ref, owners)
     norm_att = jnp.zeros((ROWS, LANES), F32)
     for axis in range(AXES):
@@ -368,7 +381,7 @@
     sent = got_ref[pl.ds(me * PIECE + EXTRA, 8), :]
     norm = sent[2 * AXES : 2 * AXES + 1, 0:1] + total(norm_att) / copies
     lane = iota((8, LANES), 1)
-    numbers = jnp.where(lane == 0, total(square[0:1]), jnp.where(lane == 1, norm, 0.0))
+    numbers = jnp.where(lane == 0, total(square), jnp.where(lane == 1, norm, 0.0))
     numbers = jnp.where(iota((8, LANES), 0) == 1, numbers, 0.0)
     for owner in range(owners):
         piece_ref[owner * PIECE + EXTRA : owner * PIECE + PIECE, :] = numbers
@@ -389,10 +402,21 @@
     out_ref,
     slots,
     table,
+    after_ref,
 ):
     tiles = design.shape[0]
     owners = got_ref.shape[0] // PIECE
     load_vector(got_ref, part_ref, slots, table, true_ref)
+
+    def body(step, carry):
+        batch = [step * UNROLL + k for k in range(UNROLL)]
+        where = [places(t, offset_ref, knot_ref) for t in batch]
+        values = forward(batch, where, design, slot_ref, offset_ref, slots, table)
+        for t, value in zip(batch, values):
+            after_ref[pl.ds(t, 1), :] = value[0:1]
+        return carry
+
+    lax.fori_loop(0, tiles // UNROLL, body, 0)
     me = lax.axis_index("tm")
     sent = got_ref[pl.ds(me * PIECE + EXTRA, 8), :][2 * AXES : 2 * AXES + 1]
     group = got_ref[EXTRA : EXTRA + 8, :]
@@ -410,21 +434,8 @@
     across_att = total(across_att) / copies
     d_group = group[:, 0:1] + square_att * owners
     tau = sigma + d_group / (s_group + n_group)
-    tau_full = jnp.broadcast_to(tau, (8, LANES))
-
-    def body(step, carry):
-        square, across = carry
-        batch = [step * UNROLL + k for k in range(UNROLL)]
-        values = forward(batch, design, slot_ref, offset_ref, knot_ref, slots, table)
-        for t, value in zip(batch, values):
-            before = row_of(y_ref, t)
-            rest = value - tau_full * before
-            square = square + rest * rest
-            across = across + rest * before
-        return square, across
-
-    zero = jnp.zeros((8, LANES), F32)
-    square, across = lax.fori_loop(0, tiles // UNROLL, body, (zero, zero))
+    rest = after_ref[...] - tau * y_ref[...]
+    square, across = rest * rest, rest * y_ref[...]
     own = numbers_ref[...][EXTRA + 1 : EXTRA + 2]
     numbers = [
         own[:, 1:2],
@@ -432,8 +443,8 @@
         sent[:, 0:1] + square_att,
         sent[:, 1:2] + across_att,
         sigma,
-        total(square[0:1]),
-        total(across[0:1]),
+        total(square),
+        total(across),
         tau,
     ]
     lane = iota((1, LANES), 1)
@@ -478,13 +489,14 @@
 SMEM = pl.BlockSpec(memory_space=pltpu.SMEM)
 HBM = pl.BlockSpec(memory_space=pltpu.HBM)
 PARAMETERS = pltpu.CompilerParams(vmem_limit_bytes=24 * 1024 * 1024)
+HIDES = pl.CostEstimate(flops=0, bytes_accessed=64 * 1024 * 1024, transcendentals=0)
 
 
 def f32(*shape):
     return jax.ShapeDtypeStruct(shape, F32)
 
 
-def call(kernel, out_shape, in_specs, scratch=(), name=None):
+def call(kernel, out_shape, in_specs, scratch=(), name=None, cost=None):
     return pl.pallas_call(
         kernel,
         out_shape=out_shape,
@@ -492,6 +504,7 @@
         out_specs=jax.tree.map(lambda _: VMEM, out_shape),
         scratch_shapes=list(scratch),
         compiler_params=PARAMETERS,
+        cost_estimate=cost,
         name=name,
     )
 
@@ -515,16 +528,17 @@
     acc = pltpu.VMEM((slot_count, 8, LANES), F32)
     knots = pltpu.VMEM((ROWS + 1, 16, LANES), F32)
     piece = f32(owners * PIECE, LANES)
-    part = f32(AXES * ROWS_PAD, LANES)
+    part = f32(PART, LANES)
     true = f32(AXES, ROWS, LANES)
 
     def exchange(pieces):
         return lax.all_to_all(pieces.reshape(owners, PIECE, LANES), "tm", 0, 0, tiled=True)
 
-    def src_parts(own):
-        return [own] + [
+    def att_sum(own):
+        parts = [own] + [
             lax.ppermute(own, "src", [(i, i ^ k) for i in range(copies)]) for k in range(1, copies)
         ]
+        return call(att_kernel, part, [VMEM] * copies, name="att", cost=HIDES)(*parts)
 
     src_rows = jnp.transpose(src_design, (1, 0, 2)).reshape(PARAMS * tiles, LANES)
     att_rows = jnp.transpose(att_design, (1, 0, 2)).reshape(AXES * tiles, LANES)
@@ -535,17 +549,18 @@
         [HBM] * len(inputs),
         [acc, knots, pltpu.VMEM((4, tiles, LANES), F32)]
         + [pltpu.SMEM((tiles,), jnp.int32)] * 3
-        + [pltpu.VMEM(value.shape, value.dtype) for value in inputs[3:]]
+        + [pltpu.VMEM((8 * tiles, LANES), F32)]
+        + [pltpu.VMEM(value.shape, value.dtype) for value in inputs[4:]]
         + [pltpu.SemaphoreType.DMA((len(inputs),))],
         "first",
     )(*[pltpu.with_memory_space_constraint(value, pltpu.HBM) for value in inputs])
-    got, parts = exchange(pieces), src_parts(own)
-    z_src, z_part, back, names = call(
-        functools.partial(owner_kernel, copies, True),
-        (f32(PARAMS, SB_DEV, LANES), part, f32(owners, PIECE, LANES), f32(8, LANES)),
-        [VMEM] * (1 + copies),
+    got, z_part = exchange(pieces), att_sum(own)
+    z_src, back, names = call(
+        functools.partial(owner_kernel, True),
+        (f32(PARAMS, SB_DEV, LANES), f32(owners, PIECE, LANES), f32(8, LANES)),
+        [VMEM] * 2,
         name="owner_first",
-    )(got, *parts)
+    )(got, z_part)
     got = exchange(back).reshape(owners * PIECE, LANES)
     pieces, own, z_att, y = call(
         functools.partial(middle_kernel, copies),
@@ -555,19 +570,19 @@
         "middle",
     )(tile_slot, tile_offset, got, z_part, design, obs_knot)
     numbers = pieces
-    got, parts = exchange(pieces), src_parts(own)
-    w_src, w_part, back = call(
-        functools.partial(owner_kernel, copies, False),
-        (f32(PARAMS, SB_DEV, LANES), part, f32(owners, PIECE, LANES)),
-        [VMEM] * (3 + copies),
+    got, w_part = exchange(pieces), att_sum(own)
+    w_src, back = call(
+        functools.partial(owner_kernel, False),
+        (f32(PARAMS, SB_DEV, LANES), f32(owners, PIECE, LANES)),
+        [VMEM] * 4,
         name="owner_second",
-    )(got, *parts, names, z_src)
+    )(got, w_part, names, z_src)
     got = exchange(back).reshape(owners * PIECE, LANES)
     w_att, row = call(
         functools.partial(last_kernel, copies),
         (true, f32(devices, 1, LANES)),
         [SMEM] * 2 + [VMEM] * 7,
-        [acc, knots],
+        [acc, knots, pltpu.VMEM((tiles, LANES), F32)],
         "last",
     )(tile_slot, tile_offset, got, w_part, design, obs_knot, y, numbers, z_att)
     row = lax.all_to_all(row, ("src", "tm"), 0, 0, tiled=True)

time: 74.3 us -> 70.3 us (0.946)
  Pallas kernels: 16.7 us -> 13.8 us
  waiting for transfers between devices: 9.34 us -> 8.32 us
    pallas_call x1, Pallas kernels: 5.41 us -> 4.26 us  [shards(): call(functools.partial(middle_kernel, copies), (piece, part, true, f32(ti...]
    pallas_call x2 -> x4, Pallas kernels: 1.91 us -> 0.77 us  [the longest x1 0.38 us: shards(): call(functools.partial(owner_kernel, False), (f32(PARAMS, SB_DEV, LANES),...]
    ppermute x6, waiting for transfers between devices: 9.34 us -> 8.32 us  [att_sum(): lax.ppermute(own, 'src', [(i, i ^ k) for i in range(copies)])]
where the time goes in v3:
time: 70.3 us; the launch traced here: 69.9 us
  blocking collectives  29.7 us (42%)
  starting transfers between devices  17.4 us (25%)
  Pallas kernels  13.8 us (20%)
  waiting for transfers between devices  8.32 us (12%)
  between operations  0.72 us (1%)
    all_to_all x2, blocking collectives, exchange(): lax.all_to_all(pieces.reshape(owners, PIECE, LANES), 'tm', 0, 0, tiled=True)  20.1 us
    all_to_all x1, blocking collectives, shards(): row = lax.all_to_all(row, ('src', 'tm'), 0, 0, tiled=True)  9.57 us
    ppermute x6, starting transfers between devices, att_sum(): lax.ppermute(own, 'src', [(i, i ^ k) for i in range(copies)])  8.84 us
    all_to_all x2, starting transfers between devices, exchange(): lax.all_to_all(pieces.reshape(owners, PIECE, LANES), 'tm', 0, 0, tiled=True)  8.57 us
    ppermute x6, waiting for transfers between devices, att_sum(): lax.ppermute(own, 'src', [(i, i ^ k) for i in range(copies)])  8.32 us
    pallas_call x1, Pallas kernels, shards(): call(first_kernel, (f32(tiles, 24, LANES), piece, part), [HBM] * len(inpu...  5.22 us
    pallas_call x1, Pallas kernels, shards(): call(functools.partial(middle_kernel, copies), (piece, part, true, f32(ti...  4.26 us
    pallas_call x1, Pallas kernels, shards(): call(functools.partial(last_kernel, copies), (true, f32(devices, 1, LANES...  2.47 us
  transfers between devices with their start and end apart: 8, of which 4 were waited for; matrix products, arithmetic and copies ran while one was open for 0% of the time, Pallas kernels for 0%

profile of v3, /device:TPU:0, one launch (start us, length us, event | category | flops | bytes accessed | tf_op | source)
XLA Modules:
  0.0 69.9 jit_solution(16900923048555902888)
XLA Ops:
  0.6 0.0 copy-start.2
  0.6 0.0 copy-start.1
  0.7 0.0 copy-start
  0.7 5.2 %first.1 = (f32[128,24,128]{2,1,0:T(8,128)S(1)}, f32[384,128]{1,0:T(8,128)}, f32[104,128]{1,0:T(8,128)S(1)}) custom-call(s32[128]{0:T(128)} %slot_ref.3, s32[128]{0:T(128)} %offset_ref.3, s32[128]{0:T(128)} %valid_hbm.1, f32[640,128]{1,0:T(8,128)} %bitcast.13, f32[384,128]{1,0:T(8,128)} %bitcast.14, f32[128,128]{1,0:T(8,128)} %frac_hbm.1, ...), custom_call_target="tpu_custom_call" | custom-call | tf_op jit(solution)/shard_map/first/pallas_call | solution.py:546
  5.9 5.2 %all-to-all-start = ((f32[8,48,128]{2,1,0:T(8,128)}), f32[8,48,128]{2,1,0:T(8,128)S(1)}, u32[]{:S(2)}, u32[]{:S(2)}) async-start(f32[8,48,128]{2,1,0:T(8,128)} %bitcast.4), calls=%async_computation | async-start | bytes 393216 | tf_op jit(solution)/shard_map/all_to_all | solution.py:535
  11.1 3.6 %collective-permute-start.2 = (f32[104,128]{1,0:T(8,128)S(1)}, f32[104,128]{1,0:T(8,128)S(1)}, u32[]{:S(2)}, u32[]{:S(2)}) collective-permute-start(f32[104,128]{1,0:T(8,128)S(1)} %get-tuple-element.19.refs_0_), channel_id=1, source_target_pairs={{0,24},{8,16},{16,8},{24,0},{1,25},{9,17},{17,9},{25,1},{2,26},{10... | collective-permute-start | bytes 159752 | tf_op jit(solution)/shard_map/ppermute | solution.py:539
  14.7 0.0 collective-permute-start.1
  14.7 0.8 %collective-permute-start = (f32[104,128]{1,0:T(8,128)S(1)}, f32[104,128]{1,0:T(8,128)S(1)}, u32[]{:S(2)}, u32[]{:S(2)}) collective-permute-start(f32[104,128]{1,0:T(8,128)S(1)} %get-tuple-element.19.refs_0_), channel_id=1, source_target_pairs={{0,8},{8,0},{16,24},{24,16},{1,9},{9,1},{17,25},{25,17},{2,10},{10... | collective-permute-start | bytes 159752 | tf_op jit(solution)/shard_map/ppermute | solution.py:539
  15.5 1.8 %collective-permute-done.2.refs_3_ = f32[104,128]{1,0:T(8,128)S(1)} collective-permute-done((f32[104,128]{1,0:T(8,128)S(1)}, f32[104,128]{1,0:T(8,128)S(1)}, u32[]{:S(2)}, u32[]{:S(2)}) %collective-permute-start.2) | collective-permute-done | bytes 53280 | tf_op jit(solution)/shard_map/ppermute | solution.py:539
  17.3 2.7 %collective-permute-done.1.refs_2_ = f32[104,128]{1,0:T(8,128)S(1)} collective-permute-done((f32[104,128]{1,0:T(8,128)S(1)}, f32[104,128]{1,0:T(8,128)S(1)}, u32[]{:S(2)}, u32[]{:S(2)}) %collective-permute-start.1) | collective-permute-done | bytes 53280 | tf_op jit(solution)/shard_map/ppermute | solution.py:539
  19.9 0.0 collective-permute-done.refs_1_
  20.0 0.0 all-to-all-done.piece_ref
  20.0 0.4 owner_first.1
  20.4 10.0 %all_to_all.25 = f32[8,48,128]{2,1,0:T(8,128)S(1)} all-to-all(f32[8,48,128]{2,1,0:T(8,128)S(1)} %get-tuple-element.20), channel_id=1, replica_groups=mesh['src'=4,'tm'=8] {'tm'}, dimensions={0} | all-to-all | bytes 393216 | tf_op jit(solution)/shard_map/all_to_all | solution.py:535
  30.4 0.0 copy-done.2
  30.4 0.0 copy-done.1
  30.4 0.0 copy-done
  30.4 4.3 %middle.1 = (f32[384,128]{1,0:T(8,128)}, f32[104,128]{1,0:T(8,128)S(1)}, f32[3,32,128]{2,1,0:T(8,128)S(1)}, f32[128,128]{1,0:T(8,128)S(1)}) custom-call(s32[128]{0:T(128)S(1)} %copy-done.1, s32[128]{0:T(128)S(1)} %copy-done.2, f32[384,128]{1,0:T(8,128)S(1)} %bitcast.11, f32[104,128]{1,0:T(8,128)S(1)} %att.2.att_ref.part_ref, ...), custom_call_target="tpu_custom_call" | custom-call | tf_op jit(solution)/shard_map/middle/pallas_call | solution.py:565
  34.7 3.4 %all-to-all-start.2 = ((f32[8,48,128]{2,1,0:T(8,128)}), f32[8,48,128]{2,1,0:T(8,128)S(1)}, u32[]{:S(2)}, u32[]{:S(2)}) async-start(f32[8,48,128]{2,1,0:T(8,128)} %bitcast.6), calls=%async_computation.2 | async-start | bytes 393216 | tf_op jit(solution)/shard_map/all_to_all | solution.py:535
  38.1 2.4 %collective-permute-start.5 = (f32[104,128]{1,0:T(8,128)S(1)}, f32[104,128]{1,0:T(8,128)S(1)}, u32[]{:S(2)}, u32[]{:S(2)}) collective-permute-start(f32[104,128]{1,0:T(8,128)S(1)} %get-tuple-element.23.refs_0_), channel_id=1, source_target_pairs={{0,24},{8,16},{16,8},{24,0},{1,25},{9,17},{17,9},{25,1},{2,26},{10... | collective-permute-start | bytes 159752 | tf_op jit(solution)/shard_map/ppermute | solution.py:539
  40.5 0.2 collective-permute-start.4
  40.7 1.8 %collective-permute-start.3 = (f32[104,128]{1,0:T(8,128)S(1)}, f32[104,128]{1,0:T(8,128)S(1)}, u32[]{:S(2)}, u32[]{:S(2)}) collective-permute-start(f32[104,128]{1,0:T(8,128)S(1)} %get-tuple-element.23.refs_0_), channel_id=1, source_target_pairs={{0,8},{8,0},{16,24},{24,16},{1,9},{9,1},{17,25},{25,17},{2,10},{10... | collective-permute-start | bytes 159752 | tf_op jit(solution)/shard_map/ppermute | solution.py:539
  42.5 2.0 %collective-permute-done.5.refs_3_ = f32[104,128]{1,0:T(8,128)S(1)} collective-permute-done((f32[104,128]{1,0:T(8,128)S(1)}, f32[104,128]{1,0:T(8,128)S(1)}, u32[]{:S(2)}, u32[]{:S(2)}) %collective-permute-start.5) | collective-permute-done | bytes 53280 | tf_op jit(solution)/shard_map/ppermute | solution.py:539
  44.5 1.8 %collective-permute-done.4.refs_2_ = f32[104,128]{1,0:T(8,128)S(1)} collective-permute-done((f32[104,128]{1,0:T(8,128)S(1)}, f32[104,128]{1,0:T(8,128)S(1)}, u32[]{:S(2)}, u32[]{:S(2)}) %collective-permute-start.4) | collective-permute-done | bytes 53280 | tf_op jit(solution)/shard_map/ppermute | solution.py:539
  46.3 0.0 collective-permute-done.3.refs_1_
  46.4 0.0 all-to-all-done.2.piece_ref
  46.4 0.4 owner_second.1
  46.8 10.0 %all_to_all.26 = f32[8,48,128]{2,1,0:T(8,128)S(1)} all-to-all(f32[8,48,128]{2,1,0:T(8,128)S(1)} %get-tuple-element.26), channel_id=1, replica_groups=mesh['src'=4,'tm'=8] {'tm'}, dimensions={0} | all-to-all | bytes 393216 | tf_op jit(solution)/shard_map/all_to_all | solution.py:535
  56.8 2.5 %last.1 = (f32[3,32,128]{2,1,0:T(8,128)S(1)}, f32[32,1,128]{2,1,0:T(1,128)S(1)}) custom-call(s32[128]{0:T(128)S(1)} %copy-done.1, s32[128]{0:T(128)S(1)} %copy-done.2, f32[384,128]{1,0:T(8,128)S(1)} %bitcast.12, f32[104,128]{1,0:T(8,128)S(1)} %att.3.att_ref.part_ref, f32[128,24,128]{2,1,0:T(8,128)S(1)} %get-tuple-element.21.design, s32[128,128]{1,0:T(8,128)S(1)} %copy-done, ...), custom_call_target="tpu_custom_call" | custom-call | tf_op jit(solution)/shard_map/last/pallas_call | solution.py:581
  59.3 9.6 %all_to_all.27.got_ref = f32[32,1,128]{2,1,0:T(1,128)S(1)} all-to-all(f32[32,1,128]{2,1,0:T(1,128)S(1)} %get-tuple-element.29), channel_id=1, replica_groups=mesh['src'=4,'tm'=8] {'src','tm'}, dimensions={0} | all-to-all | bytes 32768 | tf_op jit(solution)/shard_map/all_to_all | solution.py:588
  68.8 1.0 %final.1 = (f32[5,32,128]{2,1,0:T(8,128)}, f32[3,4096]{1,0:T(4,128)}) custom-call(f32[32,1,128]{2,1,0:T(1,128)S(1)} %all_to_all.27.got_ref, f32[5,32,128]{2,1,0:T(8,128)S(1)} %get-tuple-element.25.rest_1_.z_src, f32[5,32,128]{2,1,0:T(8,128)S(1)} %get-tuple-element.30.w_src, f32[3,32,128]{2,1,0:T(8,128)S(1)} %get-tuple-element.28.before_ref.z_att, ...), custom_call_target="tpu_custom_call" | custom-call | tf_op jit(solution)/shard_map/final/pallas_call | solution.py:589
  (2 shorter events, 0.0 us)
Async XLA Ops:
  0.6 29.8 %copy-start.2 = (s32[128]{0:T(128)S(1)}, s32[128]{0:T(128)}, u32[]{:S(2)}) copy-start(s32[128]{0:T(128)} %offset_ref.3) | copy-start | bytes 1540
  0.6 29.8 %copy-start.1 = (s32[128]{0:T(128)S(1)}, s32[128]{0:T(128)}, u32[]{:S(2)}) copy-start(s32[128]{0:T(128)} %slot_ref.3) | copy-start | bytes 1540
  0.7 29.8 %copy-start = (s32[128,128]{1,0:T(8,128)S(1)}, s32[128,128]{1,0:T(8,128)}, u32[]{:S(2)}) copy-start(s32[128,128]{1,0:T(8,128)} %knot_ref.3) | copy-start | bytes 196612
  5.9 14.1 %all-to-all-start = ((f32[8,48,128]{2,1,0:T(8,128)}), f32[8,48,128]{2,1,0:T(8,128)S(1)}, u32[]{:S(2)}, u32[]{:S(2)}) async-start(f32[8,48,128]{2,1,0:T(8,128)} %bitcast.4), calls=%async_computation | async-start | bytes 393216 | tf_op jit(solution)/shard_map/all_to_all | solution.py:535
  11.1 6.2 %collective-permute-start.2 = (f32[104,128]{1,0:T(8,128)S(1)}, f32[104,128]{1,0:T(8,128)S(1)}, u32[]{:S(2)}, u32[]{:S(2)}) collective-permute-start(f32[104,128]{1,0:T(8,128)S(1)} %get-tuple-element.19.refs_0_), channel_id=1, source_target_pairs={{0,24},{8,16},{16,8},{24,0},{1,25},{9,17},{17,9},{25,1},{2,26},{10... | collective-permute-start | bytes 159752 | tf_op jit(solution)/shard_map/ppermute | solution.py:539
  14.7 5.3 %collective-permute-start.1 = (f32[104,128]{1,0:T(8,128)S(1)}, f32[104,128]{1,0:T(8,128)S(1)}, u32[]{:S(2)}, u32[]{:S(2)}) collective-permute-start(f32[104,128]{1,0:T(8,128)S(1)} %get-tuple-element.19.refs_0_), channel_id=1, source_target_pairs={{0,16},{8,24},{16,0},{24,8},{1,17},{9,25},{17,1},{25,9},{2,18},{10... | collective-permute-start | bytes 159752 | tf_op jit(solution)/shard_map/ppermute | solution.py:539
  14.7 5.3 %collective-permute-start = (f32[104,128]{1,0:T(8,128)S(1)}, f32[104,128]{1,0:T(8,128)S(1)}, u32[]{:S(2)}, u32[]{:S(2)}) collective-permute-start(f32[104,128]{1,0:T(8,128)S(1)} %get-tuple-element.19.refs_0_), channel_id=1, source_target_pairs={{0,8},{8,0},{16,24},{24,16},{1,9},{9,1},{17,25},{25,17},{2,10},{10... | collective-permute-start | bytes 159752 | tf_op jit(solution)/shard_map/ppermute | solution.py:539
  34.7 11.7 %all-to-all-start.2 = ((f32[8,48,128]{2,1,0:T(8,128)}), f32[8,48,128]{2,1,0:T(8,128)S(1)}, u32[]{:S(2)}, u32[]{:S(2)}) async-start(f32[8,48,128]{2,1,0:T(8,128)} %bitcast.6), calls=%async_computation.2 | async-start | bytes 393216 | tf_op jit(solution)/shard_map/all_to_all | solution.py:535
  38.1 6.5 %collective-permute-start.5 = (f32[104,128]{1,0:T(8,128)S(1)}, f32[104,128]{1,0:T(8,128)S(1)}, u32[]{:S(2)}, u32[]{:S(2)}) collective-permute-start(f32[104,128]{1,0:T(8,128)S(1)} %get-tuple-element.23.refs_0_), channel_id=1, source_target_pairs={{0,24},{8,16},{16,8},{24,0},{1,25},{9,17},{17,9},{25,1},{2,26},{10... | collective-permute-start | bytes 159752 | tf_op jit(solution)/shard_map/ppermute | solution.py:539
  40.5 5.9 %collective-permute-start.4 = (f32[104,128]{1,0:T(8,128)S(1)}, f32[104,128]{1,0:T(8,128)S(1)}, u32[]{:S(2)}, u32[]{:S(2)}) collective-permute-start(f32[104,128]{1,0:T(8,128)S(1)} %get-tuple-element.23.refs_0_), channel_id=1, source_target_pairs={{0,16},{8,24},{16,0},{24,8},{1,17},{9,25},{17,1},{25,9},{2,18},{10... | collective-permute-start | bytes 159752 | tf_op jit(solution)/shard_map/ppermute | solution.py:539
  40.7 5.6 %collective-permute-start.3 = (f32[104,128]{1,0:T(8,128)S(1)}, f32[104,128]{1,0:T(8,128)S(1)}, u32[]{:S(2)}, u32[]{:S(2)}) collective-permute-start(f32[104,128]{1,0:T(8,128)S(1)} %get-tuple-element.23.refs_0_), channel_id=1, source_target_pairs={{0,8},{8,0},{16,24},{24,16},{1,9},{9,1},{17,25},{25,17},{2,10},{10... | collective-permute-start | bytes 159752 | tf_op jit(solution)/shard_map/ppermute | solution.py:539

commit v4 on v2

v4 whole, which is shorter than its diff:
```python
import functools

import jax
import jax.numpy as jnp
from jax import lax
from jax.experimental import pallas as pl
from jax.experimental.pallas import tpu as pltpu
from jax.sharding import PartitionSpec as P

KN = 4096
HW = 128
SB_DEV = 32
damping = 1.0

LANES = 128
ROWS = KN // LANES
ROWS_PAD = (ROWS + 8) // 8 * 8
AXES = 3
PARAMS = 5
CAP = 8
UNROLL = 128
F32 = jnp.float32
BF16 = jnp.bfloat16


def iota(shape, dim):
    return lax.broadcasted_iota(jnp.int32, shape, dim)


def spline_weights(fraction):
    remain = 1.0 - fraction
    square = fraction * fraction
    cubed = square * fraction
    return (
        remain * remain * remain / 6.0,
        (3.0 * cubed - 6.0 * square + 4.0) / 6.0,
        (-3.0 * cubed + 3.0 * square + 3.0 * fraction + 1.0) / 6.0,
        cubed / 6.0,
    )


def split2(value):
    high = value.astype(BF16)
    return high, (value - high.astype(F32)).astype(BF16)


def split3(value):
    high, rest = value.astype(BF16), None
    rest = value - high.astype(F32)
    middle = rest.astype(BF16)
    return high, middle, (rest - middle.astype(F32)).astype(BF16)


def total(value):
    return jnp.sum(jnp.sum(value, axis=0, keepdims=True), axis=1, keepdims=True)


def row_of(ref, row):
    return jnp.broadcast_to(ref[pl.ds(row, 1), :], (8, LANES))


def add_adjoint(tiles, values, design, offset_ref, knot_ref, knots):
    lane_row = iota((LANES, LANES), 0).astype(F32).astype(BF16)
    yes, no = jnp.ones((), BF16), jnp.zeros((), BF16)
    outs = []
    for t, resid in zip(tiles, values):
        shift = offset_ref[t] % LANES
        place = knot_ref[pl.ds(t, 1), :] + shift
        first = place < LANES
        lane = jnp.where(first, place, place - LANES)
        hot = jnp.where(lane_row == lane.astype(F32).astype(BF16), yes, no)
        high, low = split2(
            jnp.concatenate([design[t, 0:8, :] * resid, design[t, 8:16, :] * resid], axis=0)
        )
        here = jnp.broadcast_to(jnp.where(first, 1.0, 0.0).astype(BF16), high.shape)
        parts = (high * here, low * here)
        parts = parts + (high - parts[0], low - parts[1])
        outs.append(
            lax.dot_general(
                jnp.concatenate(parts, axis=0),
                hot,
                (((1,), (1,)), ((), ())),
                preferred_element_type=F32,
            )
        )
    for t, out in zip(tiles, outs):
        row = offset_ref[t] // LANES
        knots[row] += out[0:16] + out[16:32]
        knots[row + 1] += out[32:48] + out[48:64]


def send_sums(knots, att_ref, rim_ref):
    lane = iota((8, LANES), 1)
    low = iota((8, LANES), 0) < 4
    before = [jnp.zeros((8, LANES), F32)] * 3
    for row in range(ROWS + 1):
        one, two = knots[row, 0:8, :], knots[row, 8:16, :]
        now = [pltpu.roll(one, 1, 1), pltpu.roll(two, 2, 1), pltpu.roll(two, 3, 1)]
        moved = [jnp.where(lane >= k + 1, now[k], before[k]) for k in range(3)]
        both = jnp.where(low, one + moved[1], moved[0] + moved[2])
        both = both + pltpu.roll(both, 4, 0)
        for axis in range(AXES):
            att_ref[axis * ROWS_PAD + row : axis * ROWS_PAD + row + 1, :] = both[axis : axis + 1]
        if row == 0:
            rim_ref[...] = both
        before = now
    moved = pltpu.roll(both, 4, 0)
    rim_ref[...] = jnp.where(low, rim_ref[...], moved)


def first_kernel(
    offset_hbm,
    valid_hbm,
    att_hbm,
    frac_hbm,
    knot_hbm,
    obs_hbm,
    design,
    part_ref,
    rim_ref,
    knots,
    wts,
    offset_ref,
    valid_ref,
    att_ref,
    frac_ref,
    knot_ref,
    obs_ref,
    sems,
):
    pairs = (
        (frac_hbm, frac_ref),
        (offset_hbm, offset_ref),
        (valid_hbm, valid_ref),
        (knot_hbm, knot_ref),
        (obs_hbm, obs_ref),
        (att_hbm, att_ref),
    )
    copies = [pltpu.make_async_copy(a, b, sems.at[k]) for k, (a, b) in enumerate(pairs)]
    for copy in copies:
        copy.start()
    tiles = knot_ref.shape[0]
    knots[...] = jnp.zeros_like(knots)
    part_ref[...] = jnp.zeros_like(part_ref)
    for copy in copies:
        copy.wait()
    for k, weight in enumerate(spline_weights(frac_ref[...])):
        wts[k] = weight
    sub = iota((8, LANES), 0)
    lane = iota((8, LANES), 1)
    axis_of = sub % 4

    def body(step, carry):
        batch = [step * UNROLL + k for k in range(UNROLL)]
        for t in batch:
            live = lane < valid_ref[t]
            three = [row_of(att_ref, axis * tiles + t) for axis in range(AXES)]
            mixed = jnp.where(axis_of == 0, three[0], jnp.where(axis_of == 1, three[1], three[2]))
            mixed = jnp.where(live & (axis_of < 3), mixed, 0.0)
            weights = [row_of(wts.at[k], t) for k in range(4)]
            design[t, 0:8, :] = mixed * jnp.where(sub < 4, weights[0], weights[1])
            design[t, 8:16, :] = mixed * jnp.where(sub < 4, weights[2], weights[3])
        values = [row_of(obs_ref, t) for t in batch]
        add_adjoint(batch, values, design, offset_ref, knot_ref, knots)
        return carry

    lax.fori_loop(0, tiles // UNROLL, body, 0)
    send_sums(knots, part_ref, rim_ref)


def send_slots(acc, piece_ref, extra):
    slots = acc.shape[0]
    for param in range(PARAMS):
        for at in range(0, slots, 8):
            piece_ref[param * slots + at : param * slots + at + 8, :] = acc[at : at + 8, param, :]
    piece_ref[PARAMS * slots :, :] = extra


def first_sources(
    slot_ref, valid_ref, src_ref, obs_ref, table_ref, after_ref, design, piece_ref, acc
):
    del after_ref
    tiles = obs_ref.shape[0]
    owners = table_ref.shape[0]
    acc[...] = jnp.zeros_like(acc)
    lane = iota((PARAMS, LANES), 1)
    zero = jnp.zeros((8, LANES), F32)

    def body(step, carry):
        for k in range(UNROLL):
            t = step * UNROLL + k
            rows = jnp.where(lane < valid_ref[t], src_ref[pl.ds(t, PARAMS, stride=tiles), :], 0.0)
            design[t] = zero
            design[t, 0:PARAMS, :] = rows
            acc[slot_ref[t], 0:PARAMS, :] += rows * row_of(obs_ref, t)[0:PARAMS]
        return carry

    lax.fori_loop(0, tiles // UNROLL, body, 0)
    col = iota((CAP, LANES), 1)
    placed = (col % CAP == iota((CAP, LANES), 0)).astype(BF16)
    names = jnp.dot(table_ref[...].astype(F32).astype(BF16), placed, preferred_element_type=F32)
    col = iota((owners, LANES), 1)
    owner = iota((owners, LANES), 0)
    names = jnp.where(col // CAP == owner, names + (owner * SB_DEV).astype(F32), 0.0)
    names = jnp.sum(names, axis=0, keepdims=True)
    names = jnp.where(iota((8, LANES), 0) == 0, jnp.broadcast_to(names, (8, LANES)), 0.0)
    send_slots(acc, piece_ref, names)


def later_sources(slot_ref, design, y_ref, numbers_ref, piece_ref, acc):
    tiles = y_ref.shape[0]
    acc[...] = jnp.zeros_like(acc)

    def body(step, carry):
        for k in range(UNROLL):
            t = step * UNROLL + k
            acc[slot_ref[t]] += design[t] * row_of(y_ref, t)
        return carry

    lax.fori_loop(0, tiles // UNROLL, body, 0)
    send_slots(acc, piece_ref, numbers_ref[...])


def att_kernel(*refs):
    level, out_ref = [part[...] for part in refs[:-1]], refs[-1]
    while len(level) > 1:
        level = [level[k] + level[k + 1] for k in range(0, len(level), 2)]
    out_ref[...] = level[0]


def rim_kernel(part_ref, near_ref, far_ref, out_ref):
    owners = lax.axis_size("tm")
    me = lax.axis_index("tm")
    even = jnp.full((8, LANES), me % 2, jnp.int32) == 0
    near, far = near_ref[...], far_ref[...]
    left = jnp.where(me > 0, jnp.where(even, far, near), 0.0)
    right = jnp.where(me < owners - 1, jnp.where(even, near, far), 0.0)
    has_right = jnp.where(me < owners - 1, 1.0, 0.0)
    out_ref[...] = part_ref[...]
    for axis in range(AXES):
        at = axis * ROWS_PAD
        out_ref[at : at + 1, :] = part_ref[at : at + 1, :] + left[4 + axis : 5 + axis]
        at = at + ROWS
        out_ref[at : at + 1, :] = has_right * part_ref[at : at + 1, :] + right[axis : axis + 1]


def dense_kernel(slots, with_names, *refs):
    if with_names:
        refs, names_out = refs[:-1], refs[-1]
    else:
        names_in, refs = refs[0], refs[1:]
    pieces, dense_ref = refs[:-2], refs[-1]
    blocks = (dense_ref.shape[0] - 8) // PARAMS
    last = PARAMS * slots
    extras = [piece[last : last + 8, :] for piece in pieces]
    if with_names:
        names = [extra[0:1] for extra in extras]
        out = jnp.zeros(names_out.shape, F32)
        for k, name in enumerate(names):
            out = jnp.where(iota(out.shape, 0) == k, jnp.broadcast_to(name, out.shape), out)
        names_out[...] = out
    else:
        names = [names_in[k : k + 1, :] for k in range(len(pieces))]
    block = iota((blocks, slots), 0).astype(F32)
    hot = jnp.concatenate(
        [
            jnp.where(block == jnp.broadcast_to(name[:, 0:slots], block.shape), 1.0, 0.0).astype(BF16)
            for name in names
        ],
        axis=1,
    )
    got = jnp.concatenate(
        [
            jnp.concatenate([piece[p * slots : p * slots + slots, :] for piece in pieces], axis=0)
            for p in range(PARAMS)
        ],
        axis=1,
    )
    three = [jnp.dot(hot, part, preferred_element_type=F32) for part in split3(got)]
    summed = (three[2] + three[1]) + three[0]
    for param in range(PARAMS):
        dense_ref[param * blocks : param * blocks + blocks, :] = summed[:, param * LANES : (param + 1) * LANES]
    numbers = extras[0]
    for extra in extras[1:]:
        numbers = numbers + extra
    dense_ref[PARAMS * blocks :, :] = numbers


def load_vector(mine_ref, other_ref, parts, dense, table, true_ref, own_ref):
    rows = mine_ref.shape[0] - 8
    blocks = rows // PARAMS
    me = lax.axis_index("tm")
    dense[0:rows, :] = mine_ref[0:rows, :] + other_ref[0:rows, :]
    dense[rows:, :] = jnp.zeros((dense.shape[0] - rows, LANES), F32)
    for param in range(PARAMS):
        at = pl.multiple_of(param * blocks + me * SB_DEV, SB_DEV)
        own_ref[param] = dense[pl.ds(at, SB_DEV), :]
    sub = iota((8, LANES), 0)
    lane = iota((8, LANES), 1)
    low = sub < 4
    axis_of = sub % 4
    level = [part[...] for part in parts]
    while len(level) > 1:
        level = [level[k] + level[k + 1] for k in range(0, len(level), 2)]
    att = level[0]
    for axis in range(AXES):
        true_ref[axis] = att[axis * ROWS_PAD : axis * ROWS_PAD + ROWS]

    def mixed(row):
        three = [att[axis * ROWS_PAD + row : axis * ROWS_PAD + row + 1] for axis in range(AXES)]
        three = [jnp.broadcast_to(v, (8, LANES)) for v in three]
        out = jnp.where(axis_of == 0, three[0], jnp.where(axis_of == 1, three[1], three[2]))
        return jnp.where(axis_of < 3, out, 0.0)

    def rolled(value):
        return [pltpu.roll(value, LANES - k, 1) for k in (1, 2, 3)]

    now = mixed(0)
    now_rolled = rolled(now)
    for row in range(ROWS + 1):
        after = mixed(row + 1) if row < ROWS else jnp.zeros((8, LANES), F32)
        after_rolled = rolled(after)
        moved = [jnp.where(lane < LANES - 1 - k, now_rolled[k], after_rolled[k]) for k in range(3)]
        table[row, 0:8, :] = jnp.where(low, now, moved[0])
        table[row, 8:16, :] = jnp.where(low, moved[1], moved[2])
        now, now_rolled = after, after_rolled


def forward(tiles, design, sources, slot_ref, offset_ref, block_ref, knot_ref, dense, table):
    blocks = dense.shape[0] // 8
    values = []
    for t in tiles:
        shift = offset_ref[t] % LANES
        row = offset_ref[t] // LANES
        slot = slot_ref[t]
        block = slot // CAP * SB_DEV + block_ref[slot // CAP, slot % CAP]
        place = row_of(knot_ref, t) + shift
        first = place < LANES
        lane = jnp.where(first, place, place - LANES)
        summed = sources[t] * dense[pl.ds(block, 8, stride=blocks), :]
        for half in (0, 8):
            here = jnp.take_along_axis(table[row, half : half + 8, :], lane, axis=1)
            there = jnp.take_along_axis(table[row + 1, half : half + 8, :], lane, axis=1)
            summed = summed + design[t, half : half + 8, :] * jnp.where(first, here, there)
        summed = summed + pltpu.roll(summed, 4, 0)
        summed = summed + pltpu.roll(summed, 2, 0)
        values.append(summed + pltpu.roll(summed, 1, 0))
    return values


def middle_kernel(
    copies,
    slot_ref,
    offset_ref,
    block_ref,
    mine_ref,
    other_ref,
    design,
    sources,
    knot_ref,
    *refs,
):
    parts = refs[:1]
    numbers_ref, sum_ref, rim_ref, true_ref, own_ref, y_ref, knots, dense, table = refs[1:]
    tiles = design.shape[0]
    knots[...] = jnp.zeros_like(knots)
    sum_ref[...] = jnp.zeros_like(sum_ref)
    load_vector(mine_ref, other_ref, parts, dense, table, true_ref, own_ref)

    def body(step, square):
        batch = [step * UNROLL + k for k in range(UNROLL)]
        values = forward(batch, design, sources, slot_ref, offset_ref, block_ref, knot_ref, dense, table)
        for t, value in zip(batch, values):
            y_ref[pl.ds(t, 1), :] = value[0:1]
            square = square + value * value
        add_adjoint(batch, values, design, offset_ref, knot_ref, knots)
        return square

    square = lax.fori_loop(0, tiles // UNROLL, body, jnp.zeros((8, LANES), F32))
    send_sums(knots, sum_ref, rim_ref)
    norm_att = true_ref[0] * true_ref[0]
    for axis in range(1, AXES):
        norm_att = norm_att + true_ref[axis] * true_ref[axis]
    norm_src = own_ref[0] * own_ref[0]
    for param in range(1, PARAMS):
        norm_src = norm_src + own_ref[param] * own_ref[param]
    norm = total(norm_src) + total(norm_att) / copies
    lane = iota((8, LANES), 1)
    numbers = jnp.where(lane == 0, total(square[0:1]), jnp.where(lane == 1, norm, 0.0))
    numbers_ref[...] = jnp.where(iota((8, LANES), 0) == 1, numbers, 0.0)


def last_kernel(
    copies,
    slot_ref,
    offset_ref,
    block_ref,
    mine_ref,
    other_ref,
    design,
    sources,
    knot_ref,
    y_ref,
    numbers_ref,
    z_att,
    z_src,
    *refs,
):
    parts = refs[:1]
    true_ref, own_ref, out_ref, dense, table = refs[1:]
    tiles = design.shape[0]
    rows = mine_ref.shape[0] - 8
    owners = rows // (PARAMS * SB_DEV)
    load_vector(mine_ref, other_ref, parts, dense, table, true_ref, own_ref)
    group = (mine_ref[rows:, :] + other_ref[rows:, :])[1:2]
    s_group, n_group = group[:, 0:1], group[:, 1:2]
    sigma = s_group / n_group

    def about(new, old, count):
        square, across = None, None
        for k in range(count):
            rest = new[k] - sigma * old[k]
            first, second = rest * rest, rest * old[k]
            square = first if square is None else square + first
            across = second if across is None else across + second
        return total(square), total(across)

    att, src = about(true_ref, z_att, AXES), about(own_ref, z_src, PARAMS)
    d_square = src[0] + att[0] / copies
    d_across = src[1] + att[1] / copies
    tau = sigma + owners * d_square / (s_group + n_group)
    tau_full = jnp.broadcast_to(tau, (8, LANES))

    def body(step, carry):
        square, across = carry
        batch = [step * UNROLL + k for k in range(UNROLL)]
        values = forward(batch, design, sources, slot_ref, offset_ref, block_ref, knot_ref, dense, table)
        for t, value in zip(batch, values):
            before = row_of(y_ref, t)
            rest = value - tau_full * before
            square = square + rest * rest
            across = across + rest * before
        return square, across

    zero = jnp.zeros((8, LANES), F32)
    square, across = lax.fori_loop(0, tiles // UNROLL, body, (zero, zero))
    own = numbers_ref[1:2, :]
    numbers = [
        own[:, 1:2],
        own[:, 0:1],
        d_square,
        d_across,
        sigma,
        total(square[0:1]),
        total(across[0:1]),
        tau,
    ]
    lane = iota((1, LANES), 1)
    out = jnp.zeros((1, LANES), F32)
    for k, number in enumerate(numbers):
        out = jnp.where(lane == k, number, out)
    out_ref[...] = jnp.broadcast_to(out[None], out_ref.shape)


def final_kernel(got_ref, z_src, w_src, z_att, w_att, src_out, att_out):
    devices = got_ref.shape[0]
    got = got_ref[...].reshape(devices, LANES)

    def column(k):
        return got[:, k : k + 1]

    def summed(value):
        return jnp.sum(value, axis=0, keepdims=True)

    n_of, s_of = column(0), column(1)
    n, s = summed(n_of), summed(s_of)
    sigma = s / n
    alpha = n / (s + n)
    off = column(4) - sigma
    d = summed(column(2) + 2.0 * off * column(3) + off * off * n_of)
    gamma = alpha * d / n
    tau = sigma + gamma
    off = column(7) - tau
    e = summed(column(5) + 2.0 * off * column(6) + off * off * s_of)
    second = d / (e + damping * (d + gamma * gamma * n))
    c_z = alpha * (1.0 + second * tau)
    c_w = alpha * second
    for param in range(PARAMS):
        src_out[param] = c_z * z_src[param] - c_w * w_src[param]
    for axis in range(AXES):
        value = c_z * z_att[axis] - c_w * w_att[axis]
        for row in range(ROWS):
            att_out[axis : axis + 1, row * LANES : (row + 1) * LANES] = value[row : row + 1]


VMEM = pl.BlockSpec(memory_space=pltpu.VMEM)
ANY = pl.BlockSpec(memory_space=pl.ANY)
SMEM = pl.BlockSpec(memory_space=pltpu.SMEM)
HBM = pl.BlockSpec(memory_space=pltpu.HBM)
MIB = 1024 * 1024


HIDES = pl.CostEstimate(flops=3 * 10**10, bytes_accessed=0, transcendentals=0)


def f32(*shape):
    return jax.ShapeDtypeStruct(shape, F32)


def call(kernel, out_shape, in_specs, scratch=(), name=None, grant=16, cost=None):
    return pl.pallas_call(
        kernel,
        out_shape=out_shape,
        in_specs=in_specs,
        out_specs=jax.tree.map(lambda _: VMEM, out_shape),
        scratch_shapes=list(scratch),
        compiler_params=pltpu.CompilerParams(vmem_limit_bytes=grant * MIB),
        cost_estimate=cost,
        name=name,
    )


def shards(
    src_design,
    att_design,
    obs_frac,
    obs_knot,
    observed,
    tile_slot,
    tile_offset,
    tile_valid,
    slot_block,
):
    tiles = src_design.shape[0]
    owners = lax.axis_size("tm")
    copies = lax.axis_size("src")
    devices = owners * copies
    slots = owners * CAP
    blocks = owners * SB_DEV
    acc = pltpu.VMEM((slots, 8, LANES), F32)
    knots = pltpu.VMEM((ROWS + 1, 16, LANES), F32)
    dense = pltpu.VMEM((8 * blocks, LANES), F32)
    piece = f32(PARAMS * slots + 8, LANES)
    summed = f32(PARAMS * blocks + 8, LANES)
    part = f32(AXES * ROWS_PAD, LANES)
    true = f32(AXES, ROWS, LANES)
    mine = f32(PARAMS, SB_DEV, LANES)
    rim = f32(8, LANES)

    def flipped(value, axis, bits):
        size = lax.axis_size(axis)
        return lax.ppermute(value, axis, [(i, i ^ bits) for i in range(size)])

    def att_sums(own, rims):
        near = flipped(rims, "tm", 1)
        route = [(i, i + 1) for i in range(1, owners - 1, 2)]
        far = lax.ppermute(rims, "tm", route + [(j, i) for i, j in route])
        own = call(rim_kernel, part, [VMEM] * 3, name="rims")(own, near, far)
        parts = [own] + [flipped(own, "src", k) for k in range(1, copies)]
        return own, call(att_kernel, part, [VMEM] * copies, name="att", cost=HIDES)(*parts)

    def src_sums(pieces, names, after):
        sent = [pieces] + [flipped(pieces, "tm", k) for k in range(2, owners, 2)]
        count = owners // 2
        if names is None:
            half, names = call(
                functools.partial(dense_kernel, slots, True),
                (summed, f32((count + 7) // 8 * 8, LANES)),
                [VMEM] * count + [ANY],
                name="dense_first",
            )(*sent, after)
        else:
            half = call(
                functools.partial(dense_kernel, slots, False),
                summed,
                [VMEM] * (1 + count) + [ANY],
                name="dense_second",
            )(names, *sent, after)
        return half, flipped(half, "tm", 1), names

    src_rows = jnp.transpose(src_design, (1, 0, 2)).reshape(PARAMS * tiles, LANES)
    att_rows = jnp.transpose(att_design, (1, 0, 2)).reshape(AXES * tiles, LANES)
    whole = (tiles, LANES)
    design, own, rims = call(
        first_kernel,
        (f32(tiles, 16, LANES), part, rim),
        [HBM] * 6,
        [
            knots,
            pltpu.VMEM((4, tiles, LANES), F32),
            pltpu.SMEM((tiles,), jnp.int32),
            pltpu.SMEM((tiles,), jnp.int32),
            pltpu.VMEM((AXES * tiles, LANES), F32),
            pltpu.VMEM(whole, F32),
            pltpu.VMEM(whole, jnp.int32),
            pltpu.VMEM(whole, F32),
            pltpu.SemaphoreType.DMA((6,)),
        ],
        "first",
    )(*[
        pltpu.with_memory_space_constraint(value, pltpu.HBM)
        for value in (tile_offset, tile_valid, att_rows, obs_frac, obs_knot, observed)
    ])
    sources, pieces = call(
        first_sources,
        (f32(tiles, 8, LANES), piece),
        [SMEM] * 2 + [VMEM] * 3 + [ANY],
        [acc],
        "first_sources",
    )(tile_slot, tile_valid, src_rows, observed, slot_block, own)
    own, att = att_sums(own, rims)
    half, other, names = src_sums(pieces, None, own)
    numbers, own, rims, z_att, z_src, y = call(
        functools.partial(middle_kernel, copies),
        (rim, part, rim, true, mine, f32(tiles, LANES)),
        [SMEM] * 3 + [VMEM] * 6,
        [knots, dense, knots],
        "middle",
    )(tile_slot, tile_offset, slot_block, half, other, design, sources, obs_knot, att)
    pieces = call(
        later_sources,
        piece,
        [SMEM] + [VMEM] * 3,
        [acc],
        "later_sources",
    )(tile_slot, sources, y, numbers)
    own, att = att_sums(own, rims)
    half, other, names = src_sums(pieces, names, own)
    w_att, w_src, row = call(
        functools.partial(last_kernel, copies),
        (true, mine, f32(devices, 1, LANES)),
        [SMEM] * 3 + [VMEM] * 10,
        [dense, knots],
        "last",
    )(
        tile_slot, tile_offset, slot_block, half, other, design, sources, obs_knot, y, numbers, z_att, z_src, att
    )
    row = lax.all_to_all(row, ("src", "tm"), 0, 0, tiled=True)
    src, att = call(
        final_kernel,
        (mine, f32(AXES, KN)),
        [VMEM] * 5,
        name="final",
    )(row, z_src, w_src, z_att, w_att)
    return jnp.transpose(src, (1, 0, 2)), att


def solution(mesh):
    placed = (
        P(("src", "tm"), None, None),
        P(("src", "tm"), None, None),
        P(("src", "tm"), None),
        P(("src", "tm"), None),
        P(("src", "tm"), None),
        P(("src", "tm")),
        P(("src", "tm")),
        P(("src", "tm")),
        P(("src", "tm"), None),
    )
    return jax.shard_map(
        shards,
        mesh=mesh,
        in_specs=placed,
        out_specs=(P(("src", "tm"), None, None), P(None, "tm")),
        check_vma=False,
    )
```

time: 74.3 us -> 67.5 us (0.908)
  blocking collectives: 29.7 us -> 10.7 us
  starting transfers between devices: 17.4 us -> 29.9 us
  waiting for transfers between devices: 9.34 us -> 7.62 us
  local copies, waits for them, and re-layouts: 0.01 us -> 1.29 us
    ppermute x6 -> x18, starting transfers between devices: 8.84 us -> 29.9 us  [the longest x16 28.4 us: flipped(): return lax.ppermute(value, axis, [(i, i ^ bits) for i in range(size)])]
    all_to_all x2 -> x0, blocking collectives: 20.1 us -> none  [exchange(): lax.all_to_all(pieces.reshape(owners, PIECE, LANES), 'tm', 0, 0, tiled=True)]
    all_to_all x2 -> x0, starting transfers between devices: 8.57 us -> none  [exchange(): lax.all_to_all(pieces.reshape(owners, PIECE, LANES), 'tm', 0, 0, tiled=True)]
    ppermute x6 -> x18, waiting for transfers between devices: 9.34 us -> 7.62 us  [the longest x16 7.61 us: flipped(): return lax.ppermute(value, axis, [(i, i ^ bits) for i in range(size)])]
    unnamed x6 -> x14, local copies, waits for them, and re-layouts: 0.01 us -> 1.29 us
    all_to_all x1, blocking collectives: 9.54 us -> 10.7 us  [shards(): row = lax.all_to_all(row, ('src', 'tm'), 0, 0, tiled=True)]
    pallas_call x6 -> x12, Pallas kernels: 16.7 us -> 16.9 us  [the longest x1 4.76 us: shards(): call(functools.partial(middle_kernel, copies), (rim, part, rim, true, min...]
  transfers between devices with their start and end apart: 8 -> 18, of which waited for: 4 -> 4; matrix products, arithmetic and copies ran while one was open for 0% -> 0% of each run, Pallas kernels for 0% -> 2%
where the time goes in v4:
time: 67.5 us; the launch traced here: 67.3 us
  starting transfers between devices  29.9 us (44%)
  Pallas kernels  16.9 us (25%)
  blocking collectives  10.7 us (16%)
  waiting for transfers between devices  7.62 us (11%)
  local copies, waits for them, and re-layouts  1.29 us (2%)
  between operations  0.82 us (1%)
    ppermute x16, starting transfers between devices, flipped(): return lax.ppermute(value, axis, [(i, i ^ bits) for i in range(size)])  28.4 us
    all_to_all x1, blocking collectives, shards(): row = lax.all_to_all(row, ('src', 'tm'), 0, 0, tiled=True)  10.7 us
    ppermute x16, waiting for transfers between devices, flipped(): return lax.ppermute(value, axis, [(i, i ^ bits) for i in range(size)])  7.61 us
    pallas_call x1, Pallas kernels, shards(): call(functools.partial(middle_kernel, copies), (rim, part, rim, true, min...  4.76 us
    pallas_call x1, Pallas kernels, shards(): call(first_kernel, (f32(tiles, 16, LANES), part, rim), [HBM] * 6, [knots,...  4.29 us
    pallas_call x1, Pallas kernels, shards(): call(functools.partial(last_kernel, copies), (true, mine, f32(devices, 1,...  3.1 us
    ppermute x2, starting transfers between devices, att_sums(): far = lax.ppermute(rims, 'tm', route + [(j, i) for i, j in route])  1.48 us
  transfers between devices with their start and end apart: 18, of which 4 were waited for; matrix products, arithmetic and copies ran while one was open for 0% of the time, Pallas kernels for 2%

profile of v4, /device:TPU:0, one launch (start us, length us, event | category | flops | bytes accessed | tf_op | source)
XLA Modules:
  0.0 67.3 jit_solution(46150114851193972)
XLA Ops:
  0.7 4.3 %first.1 = (f32[128,16,128]{2,1,0:T(8,128)S(1)}, f32[120,128]{1,0:T(8,128)S(1)}, f32[8,128]{1,0:T(8,128)S(1)}) custom-call(s32[128]{0:T(128)} %offset_ref.3, s32[128]{0:T(128)} %valid_ref.1, f32[384,128]{1,0:T(8,128)} %bitcast.8, f32[128,128]{1,0:T(8,128)} %frac_hbm.1, s32[128,128]{1,0:T(8,128)} %knot_ref.3, f32[128,128]{1,0:T(8,128)} %obs_ref.1), custom_call_target="tpu_custom_call" | custom-call | tf_op jit(solution)/shard_map/first/pallas_call | solution.py:584
  5.0 0.6 copy-done.4
  5.6 0.0 copy-done.6
  5.6 1.3 %first_sources.1 = (f32[128,8,128]{2,1,0:T(8,128)S(1)}, f32[328,128]{1,0:T(8,128)S(1)}) custom-call(s32[128]{0:T(128)S(1)} %copy-done.4, s32[128]{0:T(128)S(1)} %copy-done.6, f32[640,128]{1,0:T(8,128)S(1)} %bitcast.7, f32[128,128]{1,0:T(8,128)S(1)} %copy-done.2, s32[8,8]{1,0:T(8,128)S(1)} %copy-done.3, f32[120,128]{1,0:T(8,128)S(1)} %get-tuple-element.20.after_ref.part_ref), custom_call_target="tpu_custom_call" | custom-call | tf_op jit(solution)/shard_map/first_sources/pallas_call | solution.py:604
  7.0 4.0 %collective-permute-start.2 = (f32[328,128]{1,0:T(8,128)S(1)}, f32[328,128]{1,0:T(8,128)S(1)}, u32[]{:S(2)}, u32[]{:S(2)}) collective-permute-start(f32[328,128]{1,0:T(8,128)S(1)} %get-tuple-element.21.refs_0_), channel_id=1, source_target_pairs={{0,6},{1,7},{2,4},{3,5},{4,2},{5,3},{6,0},{7,1},{8,14},{9,15},{10,... | collective-permute-start | bytes 503816 | tf_op jit(solution)/shard_map/ppermute | solution.py:552
  10.9 0.5 collective-permute-start.1
  11.4 0.1 collective-permute-start
  11.6 0.6 collective-permute-start.4
  12.2 3.3 %collective-permute-start.3 = (f32[8,128]{1,0:T(8,128)S(1)}, f32[8,128]{1,0:T(8,128)S(1)}, u32[]{:S(2)}, u32[]{:S(2)}) collective-permute-start(f32[8,128]{1,0:T(8,128)S(1)} %get-tuple-element.22), channel_id=1, source_target_pairs={{0,1},{1,0},{2,3},{3,2},{4,5},{5,4},{6,7},{7,6},{8,9},{9,8},{10,11... | collective-permute-start | bytes 12296 | tf_op jit(solution)/shard_map/ppermute | solution.py:552
  15.5 0.8 %collective-permute-done.3.near_ref = f32[8,128]{1,0:T(8,128)S(1)} collective-permute-done((f32[8,128]{1,0:T(8,128)S(1)}, f32[8,128]{1,0:T(8,128)S(1)}, u32[]{:S(2)}, u32[]{:S(2)}) %collective-permute-start.3) | collective-permute-done | bytes 4128 | tf_op jit(solution)/shard_map/ppermute | solution.py:552
  16.4 3.7 %collective-permute-start.8 = (f32[120,128]{1,0:T(8,128)S(1)}, f32[120,128]{1,0:T(8,128)S(1)}, u32[]{:S(2)}, u32[]{:S(2)}) collective-permute-start(f32[120,128]{1,0:T(8,128)S(1)} %rims.2.refs_4_.refs_0_), channel_id=1, source_target_pairs={{0,24},{8,16},{16,8},{24,0},{1,25},{9,17},{17,9},{25,1},{2,26},{10... | collective-permute-start | bytes 184328 | tf_op jit(solution)/shard_map/ppermute | solution.py:552
  20.1 0.8 %collective-permute-start.6 = (f32[120,128]{1,0:T(8,128)S(1)}, f32[120,128]{1,0:T(8,128)S(1)}, u32[]{:S(2)}, u32[]{:S(2)}) collective-permute-start(f32[120,128]{1,0:T(8,128)S(1)} %rims.2.refs_4_.refs_0_), channel_id=1, source_target_pairs={{0,8},{8,0},{16,24},{24,16},{1,9},{9,1},{17,25},{25,17},{2,10},{10... | collective-permute-start | bytes 184328 | tf_op jit(solution)/shard_map/ppermute | solution.py:552
  20.9 0.5 dense_first.1
  21.4 2.3 %collective-permute-start.5 = (f32[1288,128]{1,0:T(8,128)S(1)}, f32[1288,128]{1,0:T(8,128)S(1)}, u32[]{:S(2)}, u32[]{:S(2)}) collective-permute-start(f32[1288,128]{1,0:T(8,128)S(1)} %get-tuple-element.25.mine_ref), channel_id=1, source_target_pairs={{0,1},{1,0},{2,3},{3,2},{4,5},{5,4},{6,7},{7,6},{8,9},{9,8},{10,11... | collective-permute-start | bytes 1978376 | tf_op jit(solution)/shard_map/ppermute | solution.py:552
  23.7 2.7 %collective-permute-done.7.refs_2_ = f32[120,128]{1,0:T(8,128)S(1)} collective-permute-done((f32[120,128]{1,0:T(8,128)S(1)}, f32[120,128]{1,0:T(8,128)S(1)}, u32[]{:S(2)}, u32[]{:S(2)}) %collective-permute-start.7) | collective-permute-done | bytes 61472 | tf_op jit(solution)/shard_map/ppermute | solution.py:552
  26.4 0.6 copy-done.5
  27.0 4.8 %middle.1 = (f32[8,128]{1,0:T(8,128)S(1)}, f32[120,128]{1,0:T(8,128)S(1)}, f32[8,128]{1,0:T(8,128)S(1)}, f32[3,32,128]{2,1,0:T(8,128)S(1)}, f32[5,32,128]{2,1,0:T(8,128)S(1)}, /*index=5*/f32[128,128]{1,0:T(8,128)S(1)}) custom-call(s32[128]{0:T(128)S(1)} %copy-done.4, s32[128]{0:T(128)S(1)} %copy-done.5, s32[8,8]{1,0:T(8,128)S(1)} %copy-done.3, ...), custom_call_target="tpu_custom_call" | custom-call | tf_op jit(solution)/shard_map/middle/pallas_call | solution.py:613
  31.8 1.3 %later_sources.1.refs_1_ = f32[328,128]{1,0:T(8,128)S(1)} custom-call(s32[128]{0:T(128)S(1)} %copy-done.4, f32[128,8,128]{2,1,0:T(8,128)S(1)} %get-tuple-element.24.sources.design, f32[128,128]{1,0:T(8,128)S(1)} %get-tuple-element.27.y_ref, f32[8,128]{1,0:T(8,128)S(1)} %get-tuple-element.28.numbers_ref), custom_call_target="tpu_custom_call" | custom-call | tf_op jit(solution)/shard_map/later_sources/pallas_call | solution.py:620
  33.1 2.0 %collective-permute-start.11 = (f32[328,128]{1,0:T(8,128)S(1)}, f32[328,128]{1,0:T(8,128)S(1)}, u32[]{:S(2)}, u32[]{:S(2)}) collective-permute-start(f32[328,128]{1,0:T(8,128)S(1)} %later_sources.1.refs_1_), channel_id=1, source_target_pairs={{0,6},{1,7},{2,4},{3,5},{4,2},{5,3},{6,0},{7,1},{8,14},{9,15},{10,... | collective-permute-start | bytes 503816 | tf_op jit(solution)/shard_map/ppermute | solution.py:552
  35.1 2.6 %collective-permute-start.10 = (f32[328,128]{1,0:T(8,128)S(1)}, f32[328,128]{1,0:T(8,128)S(1)}, u32[]{:S(2)}, u32[]{:S(2)}) collective-permute-start(f32[328,128]{1,0:T(8,128)S(1)} %later_sources.1.refs_1_), channel_id=1, source_target_pairs={{0,4},{1,5},{2,6},{3,7},{4,0},{5,1},{6,2},{7,3},{8,12},{9,13},{10,... | collective-permute-start | bytes 503816 | tf_op jit(solution)/shard_map/ppermute | solution.py:552
  37.7 0.8 %collective-permute-start.13 = (f32[8,128]{1,0:T(8,128)S(1)}, f32[8,128]{1,0:T(8,128)S(1)}, u32[]{:S(2)}, u32[]{:S(2)}) collective-permute-start(f32[8,128]{1,0:T(8,128)S(1)} %get-tuple-element.30), channel_id=1, source_target_pairs={{1,2},{3,4},{5,6},{2,1},{4,3},{6,5},{9,10},{11,12},{13,14},{10,9},... | collective-permute-start | bytes 12296 | tf_op jit(solution)/shard_map/ppermute | solution.py:557
  38.5 3.5 %collective-permute-start.12 = (f32[8,128]{1,0:T(8,128)S(1)}, f32[8,128]{1,0:T(8,128)S(1)}, u32[]{:S(2)}, u32[]{:S(2)}) collective-permute-start(f32[8,128]{1,0:T(8,128)S(1)} %get-tuple-element.30), channel_id=1, source_target_pairs={{0,1},{1,0},{2,3},{3,2},{4,5},{5,4},{6,7},{7,6},{8,9},{9,8},{10,11... | collective-permute-start | bytes 12296 | tf_op jit(solution)/shard_map/ppermute | solution.py:552
  42.0 0.8 %collective-permute-done.12.near_ref = f32[8,128]{1,0:T(8,128)S(1)} collective-permute-done((f32[8,128]{1,0:T(8,128)S(1)}, f32[8,128]{1,0:T(8,128)S(1)}, u32[]{:S(2)}, u32[]{:S(2)}) %collective-permute-start.12) | collective-permute-done | bytes 4128 | tf_op jit(solution)/shard_map/ppermute | solution.py:552
  42.8 2.5 %collective-permute-start.17 = (f32[120,128]{1,0:T(8,128)S(1)}, f32[120,128]{1,0:T(8,128)S(1)}, u32[]{:S(2)}, u32[]{:S(2)}) collective-permute-start(f32[120,128]{1,0:T(8,128)S(1)} %rims.3.refs_5_.refs_0_), channel_id=1, source_target_pairs={{0,24},{8,16},{16,8},{24,0},{1,25},{9,17},{17,9},{25,1},{2,26},{10... | collective-permute-start | bytes 184328 | tf_op jit(solution)/shard_map/ppermute | solution.py:552
  45.3 0.3 collective-permute-start.16
  45.6 1.6 %collective-permute-start.15 = (f32[120,128]{1,0:T(8,128)S(1)}, f32[120,128]{1,0:T(8,128)S(1)}, u32[]{:S(2)}, u32[]{:S(2)}) collective-permute-start(f32[120,128]{1,0:T(8,128)S(1)} %rims.3.refs_5_.refs_0_), channel_id=1, source_target_pairs={{0,8},{8,0},{16,24},{24,16},{1,9},{9,1},{17,25},{25,17},{2,10},{10... | collective-permute-start | bytes 184328 | tf_op jit(solution)/shard_map/ppermute | solution.py:552
  47.3 0.5 dense_second.1.mine_ref
  47.8 1.3 %collective-permute-start.14 = (f32[1288,128]{1,0:T(8,128)S(1)}, f32[1288,128]{1,0:T(8,128)S(1)}, u32[]{:S(2)}, u32[]{:S(2)}) collective-permute-start(f32[1288,128]{1,0:T(8,128)S(1)} %dense_second.1.mine_ref), channel_id=1, source_target_pairs={{0,1},{1,0},{2,3},{3,2},{4,5},{5,4},{6,7},{7,6},{8,9},{9,8},{10,11... | collective-permute-start | bytes 1978376 | tf_op jit(solution)/shard_map/ppermute | solution.py:552
  49.1 3.3 %collective-permute-done.16.refs_2_ = f32[120,128]{1,0:T(8,128)S(1)} collective-permute-done((f32[120,128]{1,0:T(8,128)S(1)}, f32[120,128]{1,0:T(8,128)S(1)}, u32[]{:S(2)}, u32[]{:S(2)}) %collective-permute-start.16) | collective-permute-done | bytes 61472 | tf_op jit(solution)/shard_map/ppermute | solution.py:552
  52.4 3.1 %last.1 = (f32[3,32,128]{2,1,0:T(8,128)S(1)}, f32[5,32,128]{2,1,0:T(8,128)S(1)}, f32[32,1,128]{2,1,0:T(1,128)S(1)}) custom-call(s32[128]{0:T(128)S(1)} %copy-done.4, s32[128]{0:T(128)S(1)} %copy-done.5, s32[8,8]{1,0:T(8,128)S(1)} %copy-done.3, f32[1288,128]{1,0:T(8,128)S(1)} %dense_second.1.mine_ref, f32[1288,128]{1,0:T(8,128)S(1)} %collective-permute-done.14.other_ref, ...), custom_call_target="tpu_custom_call" | custom-call | tf_op jit(solution)/shard_map/last/pallas_call | solution.py:629
  55.5 10.7 %all_to_all.5.got_ref = f32[32,1,128]{2,1,0:T(1,128)S(1)} all-to-all(f32[32,1,128]{2,1,0:T(1,128)S(1)} %get-tuple-element.33), channel_id=1, replica_groups=mesh['src'=4,'tm'=8] {'src','tm'}, dimensions={0} | all-to-all | bytes 32768 | tf_op jit(solution)/shard_map/all_to_all | solution.py:638
  66.3 1.0 %final.1 = (f32[5,32,128]{2,1,0:T(8,128)}, f32[3,4096]{1,0:T(4,128)}) custom-call(f32[32,1,128]{2,1,0:T(1,128)S(1)} %all_to_all.5.got_ref, f32[5,32,128]{2,1,0:T(8,128)S(1)} %get-tuple-element.32.z_src, f32[5,32,128]{2,1,0:T(8,128)S(1)} %get-tuple-element.34.w_src, f32[3,32,128]{2,1,0:T(8,128)S(1)} %get-tuple-element.31.z_att, ...), custom_call_target="tpu_custom_call" | custom-call | tf_op jit(solution)/shard_map/final/pallas_call | solution.py:639
  (31 shorter events, 0.1 us)
Async XLA Ops:
  0.6 4.4 %copy-start.1 = (f32[128,5,128]{2,0,1:T(8,128)S(1)}, f32[128,5,128]{2,0,1:T(8,128)}, u32[]{:S(2)}) copy-start(f32[128,5,128]{2,0,1:T(8,128)} %param.9) | copy-start | bytes 983044
  0.6 4.4 %copy-start.2 = (f32[128,128]{1,0:T(8,128)S(1)}, f32[128,128]{1,0:T(8,128)}, u32[]{:S(2)}) copy-start(f32[128,128]{1,0:T(8,128)} %obs_ref.1) | copy-start | bytes 196612
  0.7 4.4 %copy-start.3 = (s32[8,8]{1,0:T(8,128)S(1)}, s32[8,8]{1,0:T(8,128)}, u32[]{:S(2)}) copy-start(s32[8,8]{1,0:T(8,128)} %block_ref.3) | copy-start | bytes 772
  5.0 0.7 copy-start.4
  5.0 0.7 copy-start.6
  7.0 13.1 %collective-permute-start.2 = (f32[328,128]{1,0:T(8,128)S(1)}, f32[328,128]{1,0:T(8,128)S(1)}, u32[]{:S(2)}, u32[]{:S(2)}) collective-permute-start(f32[328,128]{1,0:T(8,128)S(1)} %get-tuple-element.21.refs_0_), channel_id=1, source_target_pairs={{0,6},{1,7},{2,4},{3,5},{4,2},{5,3},{6,0},{7,1},{8,14},{9,15},{10,... | collective-permute-start | bytes 503816 | tf_op jit(solution)/shard_map/ppermute | solution.py:552
  10.9 9.9 %collective-permute-start.1 = (f32[328,128]{1,0:T(8,128)S(1)}, f32[328,128]{1,0:T(8,128)S(1)}, u32[]{:S(2)}, u32[]{:S(2)}) collective-permute-start(f32[328,128]{1,0:T(8,128)S(1)} %get-tuple-element.21.refs_0_), channel_id=1, source_target_pairs={{0,4},{1,5},{2,6},{3,7},{4,0},{5,1},{6,2},{7,3},{8,12},{9,13},{10,... | collective-permute-start | bytes 503816 | tf_op jit(solution)/shard_map/ppermute | solution.py:552
  11.4 9.4 %collective-permute-start = (f32[328,128]{1,0:T(8,128)S(1)}, f32[328,128]{1,0:T(8,128)S(1)}, u32[]{:S(2)}, u32[]{:S(2)}) collective-permute-start(f32[328,128]{1,0:T(8,128)S(1)} %get-tuple-element.21.refs_0_), channel_id=1, source_target_pairs={{0,2},{1,3},{2,0},{3,1},{4,6},{5,7},{6,4},{7,5},{8,10},{9,11},{10,... | collective-permute-start | bytes 503816 | tf_op jit(solution)/shard_map/ppermute | solution.py:552
  11.6 4.0 %collective-permute-start.4 = (f32[8,128]{1,0:T(8,128)S(1)}, f32[8,128]{1,0:T(8,128)S(1)}, u32[]{:S(2)}, u32[]{:S(2)}) collective-permute-start(f32[8,128]{1,0:T(8,128)S(1)} %get-tuple-element.22), channel_id=1, source_target_pairs={{1,2},{3,4},{5,6},{2,1},{4,3},{6,5},{9,10},{11,12},{13,14},{10,9},... | collective-permute-start | bytes 12296 | tf_op jit(solution)/shard_map/ppermute | solution.py:557
  12.2 4.1 %collective-permute-start.3 = (f32[8,128]{1,0:T(8,128)S(1)}, f32[8,128]{1,0:T(8,128)S(1)}, u32[]{:S(2)}, u32[]{:S(2)}) collective-permute-start(f32[8,128]{1,0:T(8,128)S(1)} %get-tuple-element.22), channel_id=1, source_target_pairs={{0,1},{1,0},{2,3},{3,2},{4,5},{5,4},{6,7},{7,6},{8,9},{9,8},{10,11... | collective-permute-start | bytes 12296 | tf_op jit(solution)/shard_map/ppermute | solution.py:552
  16.4 7.3 %collective-permute-start.8 = (f32[120,128]{1,0:T(8,128)S(1)}, f32[120,128]{1,0:T(8,128)S(1)}, u32[]{:S(2)}, u32[]{:S(2)}) collective-permute-start(f32[120,128]{1,0:T(8,128)S(1)} %rims.2.refs_4_.refs_0_), channel_id=1, source_target_pairs={{0,24},{8,16},{16,8},{24,0},{1,25},{9,17},{17,9},{25,1},{2,26},{10... | collective-permute-start | bytes 184328 | tf_op jit(solution)/shard_map/ppermute | solution.py:552
  20.1 6.3 %collective-permute-start.7 = (f32[120,128]{1,0:T(8,128)S(1)}, f32[120,128]{1,0:T(8,128)S(1)}, u32[]{:S(2)}, u32[]{:S(2)}) collective-permute-start(f32[120,128]{1,0:T(8,128)S(1)} %rims.2.refs_4_.refs_0_), channel_id=1, source_target_pairs={{0,16},{8,24},{16,0},{24,8},{1,17},{9,25},{17,1},{25,9},{2,18},{10... | collective-permute-start | bytes 184328 | tf_op jit(solution)/shard_map/ppermute | solution.py:552
  20.1 6.3 %collective-permute-start.6 = (f32[120,128]{1,0:T(8,128)S(1)}, f32[120,128]{1,0:T(8,128)S(1)}, u32[]{:S(2)}, u32[]{:S(2)}) collective-permute-start(f32[120,128]{1,0:T(8,128)S(1)} %rims.2.refs_4_.refs_0_), channel_id=1, source_target_pairs={{0,8},{8,0},{16,24},{24,16},{1,9},{9,1},{17,25},{25,17},{2,10},{10... | collective-permute-start | bytes 184328 | tf_op jit(solution)/shard_map/ppermute | solution.py:552
  21.4 5.0 %copy-start = (s32[128,128]{1,0:T(8,128)S(1)}, s32[128,128]{1,0:T(8,128)}, u32[]{:S(2)}) copy-start(s32[128,128]{1,0:T(8,128)} %knot_ref.3) | copy-start | bytes 196612
  21.4 5.0 %collective-permute-start.5 = (f32[1288,128]{1,0:T(8,128)S(1)}, f32[1288,128]{1,0:T(8,128)S(1)}, u32[]{:S(2)}, u32[]{:S(2)}) collective-permute-start(f32[1288,128]{1,0:T(8,128)S(1)} %get-tuple-element.25.mine_ref), channel_id=1, source_target_pairs={{0,1},{1,0},{2,3},{3,2},{4,5},{5,4},{6,7},{7,6},{8,9},{9,8},{10,11... | collective-permute-start | bytes 1978376 | tf_op jit(solution)/shard_map/ppermute | solution.py:552
  26.4 0.7 copy-start.5
  33.1 12.5 %collective-permute-start.11 = (f32[328,128]{1,0:T(8,128)S(1)}, f32[328,128]{1,0:T(8,128)S(1)}, u32[]{:S(2)}, u32[]{:S(2)}) collective-permute-start(f32[328,128]{1,0:T(8,128)S(1)} %later_sources.1.refs_1_), channel_id=1, source_target_pairs={{0,6},{1,7},{2,4},{3,5},{4,2},{5,3},{6,0},{7,1},{8,14},{9,15},{10,... | collective-permute-start | bytes 503816 | tf_op jit(solution)/shard_map/ppermute | solution.py:552
  35.1 12.2 %collective-permute-start.10 = (f32[328,128]{1,0:T(8,128)S(1)}, f32[328,128]{1,0:T(8,128)S(1)}, u32[]{:S(2)}, u32[]{:S(2)}) collective-permute-start(f32[328,128]{1,0:T(8,128)S(1)} %later_sources.1.refs_1_), channel_id=1, source_target_pairs={{0,4},{1,5},{2,6},{3,7},{4,0},{5,1},{6,2},{7,3},{8,12},{9,13},{10,... | collective-permute-start | bytes 503816 | tf_op jit(solution)/shard_map/ppermute | solution.py:552
  37.7 9.6 %collective-permute-start.9 = (f32[328,128]{1,0:T(8,128)S(1)}, f32[328,128]{1,0:T(8,128)S(1)}, u32[]{:S(2)}, u32[]{:S(2)}) collective-permute-start(f32[328,128]{1,0:T(8,128)S(1)} %later_sources.1.refs_1_), channel_id=1, source_target_pairs={{0,2},{1,3},{2,0},{3,1},{4,6},{5,7},{6,4},{7,5},{8,10},{9,11},{10,... | collective-permute-start | bytes 503816 | tf_op jit(solution)/shard_map/ppermute | solution.py:552
  37.7 4.3 %collective-permute-start.13 = (f32[8,128]{1,0:T(8,128)S(1)}, f32[8,128]{1,0:T(8,128)S(1)}, u32[]{:S(2)}, u32[]{:S(2)}) collective-permute-start(f32[8,128]{1,0:T(8,128)S(1)} %get-tuple-element.30), channel_id=1, source_target_pairs={{1,2},{3,4},{5,6},{2,1},{4,3},{6,5},{9,10},{11,12},{13,14},{10,9},... | collective-permute-start | bytes 12296 | tf_op jit(solution)/shard_map/ppermute | solution.py:557
  38.5 4.3 %collective-permute-start.12 = (f32[8,128]{1,0:T(8,128)S(1)}, f32[8,128]{1,0:T(8,128)S(1)}, u32[]{:S(2)}, u32[]{:S(2)}) collective-permute-start(f32[8,128]{1,0:T(8,128)S(1)} %get-tuple-element.30), channel_id=1, source_target_pairs={{0,1},{1,0},{2,3},{3,2},{4,5},{5,4},{6,7},{7,6},{8,9},{9,8},{10,11... | collective-permute-start | bytes 12296 | tf_op jit(solution)/shard_map/ppermute | solution.py:552
  42.8 6.3 %collective-permute-start.17 = (f32[120,128]{1,0:T(8,128)S(1)}, f32[120,128]{1,0:T(8,128)S(1)}, u32[]{:S(2)}, u32[]{:S(2)}) collective-permute-start(f32[120,128]{1,0:T(8,128)S(1)} %rims.3.refs_5_.refs_0_), channel_id=1, source_target_pairs={{0,24},{8,16},{16,8},{24,0},{1,25},{9,17},{17,9},{25,1},{2,26},{10... | collective-permute-start | bytes 184328 | tf_op jit(solution)/shard_map/ppermute | solution.py:552
  45.3 7.1 %collective-permute-start.16 = (f32[120,128]{1,0:T(8,128)S(1)}, f32[120,128]{1,0:T(8,128)S(1)}, u32[]{:S(2)}, u32[]{:S(2)}) collective-permute-start(f32[120,128]{1,0:T(8,128)S(1)} %rims.3.refs_5_.refs_0_), channel_id=1, source_target_pairs={{0,16},{8,24},{16,0},{24,8},{1,17},{9,25},{17,1},{25,9},{2,18},{10... | collective-permute-start | bytes 184328 | tf_op jit(solution)/shard_map/ppermute | solution.py:552
  45.6 6.8 %collective-permute-start.15 = (f32[120,128]{1,0:T(8,128)S(1)}, f32[120,128]{1,0:T(8,128)S(1)}, u32[]{:S(2)}, u32[]{:S(2)}) collective-permute-start(f32[120,128]{1,0:T(8,128)S(1)} %rims.3.refs_5_.refs_0_), channel_id=1, source_target_pairs={{0,8},{8,0},{16,24},{24,16},{1,9},{9,1},{17,25},{25,17},{2,10},{10... | collective-permute-start | bytes 184328 | tf_op jit(solution)/shard_map/ppermute | solution.py:552
  47.8 4.6 %collective-permute-start.14 = (f32[1288,128]{1,0:T(8,128)S(1)}, f32[1288,128]{1,0:T(8,128)S(1)}, u32[]{:S(2)}, u32[]{:S(2)}) collective-permute-start(f32[1288,128]{1,0:T(8,128)S(1)} %dense_second.1.mine_ref), channel_id=1, source_target_pairs={{0,1},{1,0},{2,3},{3,2},{4,5},{5,4},{6,7},{7,6},{8,9},{9,8},{10,11... | collective-permute-start | bytes 1978376 | tf_op jit(solution)/shard_map/ppermute | solution.py:552

commit v5 on v4

--- a/solution.py
+++ b/solution.py
@@ -59,15 +59,18 @@
     return jnp.broadcast_to(ref[pl.ds(row, 1), :], (8, LANES))
 
 
-def add_adjoint(tiles, values, design, offset_ref, knot_ref, knots):
+def places(t, offset_ref, knot_ref):
+    place = row_of(knot_ref, t) + offset_ref[t] % LANES
+    first = place < LANES
+    return jnp.where(first, place, place - LANES), first
+
+
+def add_adjoint(tiles, values, where, design, offset_ref, knots):
     lane_row = iota((LANES, LANES), 0).astype(F32).astype(BF16)
     yes, no = jnp.ones((), BF16), jnp.zeros((), BF16)
     outs = []
-    for t, resid in zip(tiles, values):
-        shift = offset_ref[t] % LANES
-        place = knot_ref[pl.ds(t, 1), :] + shift
-        first = place < LANES
-        lane = jnp.where(first, place, place - LANES)
+    for t, resid, (lane, first) in zip(tiles, values, where):
+        lane, first = lane[0:1], first[0:1]
         hot = jnp.where(lane_row == lane.astype(F32).astype(BF16), yes, no)
         high, low = split2(
             jnp.concatenate([design[t, 0:8, :] * resid, design[t, 8:16, :] * resid], axis=0)
@@ -161,11 +164,19 @@
             design[t, 0:8, :] = mixed * jnp.where(sub < 4, weights[0], weights[1])
             design[t, 8:16, :] = mixed * jnp.where(sub < 4, weights[2], weights[3])
         values = [row_of(obs_ref, t) for t in batch]
-        add_adjoint(batch, values, design, offset_ref, knot_ref, knots)
+        where = [places(t, offset_ref, knot_ref) for t in batch]
+        add_adjoint(batch, values, where, design, offset_ref, knots)
         return carry
 
     lax.fori_loop(0, tiles // UNROLL, body, 0)
     send_sums(knots, part_ref, rim_ref)
+
+
+def begin_copies(pairs, sems):
+    copies = [pltpu.make_async_copy(a, b, sems.at[k]) for k, (a, b) in enumerate(pairs)]
+    for copy in copies:
+        copy.start()
+    return copies
 
 
 def send_slots(acc, piece_ref, extra):
@@ -177,14 +188,17 @@
 
 
 def first_sources(
-    slot_ref, valid_ref, src_ref, obs_ref, table_ref, after_ref, design, piece_ref, acc
+    slot_hbm, valid_hbm, src_ref, obs_ref, table_ref, after_ref, design, piece_ref, acc, slot_ref, valid_ref, sems
 ):
     del after_ref
+    copies = begin_copies(((slot_hbm, slot_ref), (valid_hbm, valid_ref)), sems)
     tiles = obs_ref.shape[0]
     owners = table_ref.shape[0]
     acc[...] = jnp.zeros_like(acc)
     lane = iota((PARAMS, LANES), 1)
     zero = jnp.zeros((8, LANES), F32)
+    for copy in copies:
+        copy.wait()
 
     def body(step, carry):
         for k in range(UNROLL):
@@ -207,9 +221,12 @@
     send_slots(acc, piece_ref, names)
 
 
-def later_sources(slot_ref, design, y_ref, numbers_ref, piece_ref, acc):
+def later_sources(slot_hbm, design, y_ref, numbers_ref, piece_ref, acc, slot_ref, sems):
+    [copy] = begin_copies(((slot_hbm, slot_ref),), sems)
     tiles = y_ref.shape[0]
     acc[...] = jnp.zeros_like(acc)
+
+    copy.wait()
 
     def body(step, carry):
         for k in range(UNROLL):
@@ -326,17 +343,13 @@
         now, now_rolled = after, after_rolled
 
 
-def forward(tiles, design, sources, slot_ref, offset_ref, block_ref, knot_ref, dense, table):
+def forward(tiles, where, design, sources, slot_ref, offset_ref, block_ref, dense, table):
     blocks = dense.shape[0] // 8
     values = []
-    for t in tiles:
-        shift = offset_ref[t] % LANES
+    for t, (lane, first) in zip(tiles, where):
         row = offset_ref[t] // LANES
         slot = slot_ref[t]
         block = slot // CAP * SB_DEV + block_ref[slot // CAP, slot % CAP]
-        place = row_of(knot_ref, t) + shift
-        first = place < LANES
-        lane = jnp.where(first, place, place - LANES)
         summed = sources[t] * dense[pl.ds(block, 8, stride=blocks), :]
         for half in (0, 8):
             here = jnp.take_along_axis(table[row, half : half + 8, :], lane, axis=1)
@@ -350,9 +363,9 @@
 
 def middle_kernel(
     copies,
-    slot_ref,
-    offset_ref,
-    block_ref,
+    slot_hbm,
+    offset_hbm,
+    block_hbm,
     mine_ref,
     other_ref,
     design,
@@ -361,22 +374,29 @@
     *refs,
 ):
     parts = refs[:1]
-    numbers_ref, sum_ref, rim_ref, true_ref, own_ref, y_ref, knots, dense, table = refs[1:]
+    numbers_ref, sum_ref, rim_ref, true_ref, own_ref, y_ref, knots, dense, table, slot_ref, offset_ref, block_ref, sems = refs[1:]
+    copies_in = begin_copies(
+        ((slot_hbm, slot_ref), (offset_hbm, offset_ref), (block_hbm, block_ref)), sems
+    )
     tiles = design.shape[0]
     knots[...] = jnp.zeros_like(knots)
     sum_ref[...] = jnp.zeros_like(sum_ref)
     load_vector(mine_ref, other_ref, parts, dense, table, true_ref, own_ref)
 
-    def body(step, square):
+    for copy in copies_in:
+        copy.wait()
+
+    def body(step, carry):
         batch = [step * UNROLL + k for k in range(UNROLL)]
-        values = forward(batch, design, sources, slot_ref, offset_ref, block_ref, knot_ref, dense, table)
+        where = [places(t, offset_ref, knot_ref) for t in batch]
+        values = forward(batch, where, design, sources, slot_ref, offset_ref, block_ref, dense, table)
         for t, value in zip(batch, values):
             y_ref[pl.ds(t, 1), :] = value[0:1]
-            square = square + value * value
-        add_adjoint(batch, values, design, offset_ref, knot_ref, knots)
-        return square
-
-    square = lax.fori_loop(0, tiles // UNROLL, body, jnp.zeros((8, LANES), F32))
+        add_adjoint(batch, values, where, design, offset_ref, knots)
+        return carry
+
+    lax.fori_loop(0, tiles // UNROLL, body, 0)
+    square = y_ref[...] * y_ref[...]
     send_sums(knots, sum_ref, rim_ref)
     norm_att = true_ref[0] * true_ref[0]
     for axis in range(1, AXES):
@@ -386,15 +406,15 @@
         norm_src = norm_src + own_ref[param] * own_ref[param]
     norm = total(norm_src) + total(norm_att) / copies
     lane = iota((8, LANES), 1)
-    numbers = jnp.where(lane == 0, total(square[0:1]), jnp.where(lane == 1, norm, 0.0))
+    numbers = jnp.where(lane == 0, total(square), jnp.where(lane == 1, norm, 0.0))
     numbers_ref[...] = jnp.where(iota((8, LANES), 0) == 1, numbers, 0.0)
 
 
 def last_kernel(
     copies,
-    slot_ref,
-    offset_ref,
-    block_ref,
+    slot_hbm,
+    offset_hbm,
+    block_hbm,
     mine_ref,
     other_ref,
     design,
@@ -407,7 +427,10 @@
     *refs,
 ):
     parts = refs[:1]
-    true_ref, own_ref, out_ref, dense, table = refs[1:]
+    true_ref, own_ref, out_ref, dense, table, after_ref, slot_ref, offset_ref, block_ref, sems = refs[1:]
+    copies_in = begin_copies(
+        ((slot_hbm, slot_ref), (offset_hbm, offset_ref), (block_hbm, block_ref)), sems
+    )
     tiles = design.shape[0]
     rows = mine_ref.shape[0] - 8
     owners = rows // (PARAMS * SB_DEV)
@@ -429,21 +452,21 @@
     d_square = src[0] + att[0] / copies
     d_across = src[1] + att[1] / copies
     tau = sigma + owners * d_square / (s_group + n_group)
-    tau_full = jnp.broadcast_to(tau, (8, LANES))
+
+    for copy in copies_in:
+        copy.wait()
 
     def body(step, carry):
-        square, across = carry
         batch = [step * UNROLL + k for k in range(UNROLL)]
-        values = forward(batch, design, sources, slot_ref, offset_ref, block_ref, knot_ref, dense, table)
+        where = [places(t, offset_ref, knot_ref) for t in batch]
+        values = forward(batch, where, design, sources, slot_ref, offset_ref, block_ref, dense, table)
         for t, value in zip(batch, values):
-            before = row_of(y_ref, t)
-            rest = value - tau_full * before
-            square = square + rest * rest
-            across = across + rest * before
-        return square, across
-
-    zero = jnp.zeros((8, LANES), F32)
-    square, across = lax.fori_loop(0, tiles // UNROLL, body, (zero, zero))
+            after_ref[pl.ds(t, 1), :] = value[0:1]
+        return carry
+
+    lax.fori_loop(0, tiles // UNROLL, body, 0)
+    rest = after_ref[...] - tau * y_ref[...]
+    square, across = rest * rest, rest * y_ref[...]
     own = numbers_ref[1:2, :]
     numbers = [
         own[:, 1:2],
@@ -451,8 +474,8 @@
         d_square,
         d_across,
         sigma,
-        total(square[0:1]),
-        total(across[0:1]),
+        total(square),
+        total(across),
         tau,
     ]
     lane = iota((1, LANES), 1)
@@ -578,6 +601,9 @@
             )(names, *sent, after)
         return half, flipped(half, "tm", 1), names
 
+    def held(value):
+        return pltpu.with_memory_space_constraint(value, pltpu.HBM)
+
     src_rows = jnp.transpose(src_design, (1, 0, 2)).reshape(PARAMS * tiles, LANES)
     att_rows = jnp.transpose(att_design, (1, 0, 2)).reshape(AXES * tiles, LANES)
     whole = (tiles, LANES)
@@ -604,36 +630,40 @@
     sources, pieces = call(
         first_sources,
         (f32(tiles, 8, LANES), piece),
-        [SMEM] * 2 + [VMEM] * 3 + [ANY],
-        [acc],
+        [HBM] * 2 + [VMEM] * 3 + [ANY],
+        [acc] + [pltpu.SMEM((tiles,), jnp.int32)] * 2 + [pltpu.SemaphoreType.DMA((2,))],
         "first_sources",
-    )(tile_slot, tile_valid, src_rows, observed, slot_block, own)
+    )(held(tile_slot), held(tile_valid), src_rows, observed, slot_block, own)
     own, att = att_sums(own, rims)
     half, other, names = src_sums(pieces, None, own)
     numbers, own, rims, z_att, z_src, y = call(
         functools.partial(middle_kernel, copies),
         (rim, part, rim, true, mine, f32(tiles, LANES)),
-        [SMEM] * 3 + [VMEM] * 6,
-        [knots, dense, knots],
+        [HBM] * 3 + [VMEM] * 6,
+        [knots, dense, knots]
+        + [pltpu.SMEM((tiles,), jnp.int32)] * 2
+        + [pltpu.SMEM(slot_block.shape, jnp.int32), pltpu.SemaphoreType.DMA((3,))],
         "middle",
-    )(tile_slot, tile_offset, slot_block, half, other, design, sources, obs_knot, att)
+    )(held(tile_slot), held(tile_offset), held(slot_block), half, other, design, sources, obs_knot, att)
     pieces = call(
         later_sources,
         piece,
-        [SMEM] + [VMEM] * 3,
-        [acc],
+        [HBM] + [VMEM] * 3,
+        [acc, pltpu.SMEM((tiles,), jnp.int32), pltpu.SemaphoreType.DMA((1,))],
         "later_sources",
-    )(tile_slot, sources, y, numbers)
+    )(held(tile_slot), sources, y, numbers)
     own, att = att_sums(own, rims)
     half, other, names = src_sums(pieces, names, own)
     w_att, w_src, row = call(
         functools.partial(last_kernel, copies),
         (true, mine, f32(devices, 1, LANES)),
-        [SMEM] * 3 + [VMEM] * 10,
-        [dense, knots],
+        [HBM] * 3 + [VMEM] * 10,
+        [dense, knots, pltpu.VMEM((tiles, LANES), F32)]
+        + [pltpu.SMEM((tiles,), jnp.int32)] * 2
+        + [pltpu.SMEM(slot_block.shape, jnp.int32), pltpu.SemaphoreType.DMA((3,))],
         "last",
     )(
-        tile_slot, tile_offset, slot_block, half, other, design, sources, obs_knot, y, numbers, z_att, z_src, att
+        held(tile_slot), held(tile_offset), held(slot_block), half, other, design, sources, obs_knot, y, numbers, z_att, z_src, att
     )
     row = lax.all_to_all(row, ("src", "tm"), 0, 0, tiled=True)
     src, att = call(

time: 67.5 us -> 66.4 us (0.984)
  local copies, waits for them, and re-layouts: 1.29 us -> 0.02 us
    unnamed x14 -> x8, local copies, waits for them, and re-layouts: 1.29 us -> 0.02 us
where the time goes in v5:
time: 66.4 us; the launch traced here: 66 us
  starting transfers between devices  29.9 us (45%)
  Pallas kernels  16.9 us (25%)
  blocking collectives  11 us (17%)
  waiting for transfers between devices  7.38 us (11%)
  between operations  0.8 us (1%)
    ppermute x16, starting transfers between devices, flipped(): return lax.ppermute(value, axis, [(i, i ^ bits) for i in range(size)])  28.6 us
    all_to_all x1, blocking collectives, shards(): row = lax.all_to_all(row, ('src', 'tm'), 0, 0, tiled=True)  11 us
    ppermute x16, waiting for transfers between devices, flipped(): return lax.ppermute(value, axis, [(i, i ^ bits) for i in range(size)])  7.38 us
    pallas_call x1, Pallas kernels, shards(): call(functools.partial(middle_kernel, copies), (rim, part, rim, true, min...  4.76 us
    pallas_call x1, Pallas kernels, shards(): call(first_kernel, (f32(tiles, 16, LANES), part, rim), [HBM] * 6, [knots,...  4.29 us
    pallas_call x1, Pallas kernels, shards(): call(functools.partial(last_kernel, copies), (true, mine, f32(devices, 1,...  2.86 us
    pallas_call x1, Pallas kernels, shards(): call(first_sources, (f32(tiles, 8, LANES), piece), [HBM] * 2 + [VMEM] * 3...  1.46 us
    pallas_call x1, Pallas kernels, shards(): call(later_sources, piece, [HBM] + [VMEM] * 3, [acc, pltpu.SMEM((tiles,),...  1.39 us
  transfers between devices with their start and end apart: 18, of which 4 were waited for; matrix products, arithmetic and copies ran while one was open for 0% of the time, Pallas kernels for 2%

profile of v5, /device:TPU:0, one launch (start us, length us, event | category | flops | bytes accessed | tf_op | source)
XLA Modules:
  0.0 66.0 jit_solution(17623768847123288405)
XLA Ops:
  0.7 0.0 copy-start.3
  0.7 4.3 %first.1 = (f32[128,16,128]{2,1,0:T(8,128)S(1)}, f32[120,128]{1,0:T(8,128)S(1)}, f32[8,128]{1,0:T(8,128)S(1)}) custom-call(s32[128]{0:T(128)} %offset_hbm.5, s32[128]{0:T(128)} %valid_hbm.3, f32[384,128]{1,0:T(8,128)} %bitcast.8, f32[128,128]{1,0:T(8,128)} %frac_hbm.1, s32[128,128]{1,0:T(8,128)} %knot_ref.3, f32[128,128]{1,0:T(8,128)} %obs_ref.1), custom_call_target="tpu_custom_call" | custom-call | tf_op jit(solution)/shard_map/first/pallas_call | solution.py:610
  5.0 1.5 %first_sources.1 = (f32[128,8,128]{2,1,0:T(8,128)S(1)}, f32[328,128]{1,0:T(8,128)S(1)}) custom-call(s32[128]{0:T(128)} %slot_hbm.7, s32[128]{0:T(128)} %valid_hbm.3, f32[640,128]{1,0:T(8,128)S(1)} %bitcast.7, f32[128,128]{1,0:T(8,128)S(1)} %copy-done.2, s32[8,8]{1,0:T(8,128)S(1)} %copy-done.3, f32[120,128]{1,0:T(8,128)S(1)} %get-tuple-element.20.after_ref.part_ref), custom_call_target="tpu_custom_call" | custom-call | tf_op jit(solution)/shard_map/first_sources/pallas_call | solution.py:630
  6.5 4.0 %collective-permute-start.2 = (f32[328,128]{1,0:T(8,128)S(1)}, f32[328,128]{1,0:T(8,128)S(1)}, u32[]{:S(2)}, u32[]{:S(2)}) collective-permute-start(f32[328,128]{1,0:T(8,128)S(1)} %get-tuple-element.21.refs_0_), channel_id=1, source_target_pairs={{0,6},{1,7},{2,4},{3,5},{4,2},{5,3},{6,0},{7,1},{8,14},{9,15},{10,... | collective-permute-start | bytes 503816 | tf_op jit(solution)/shard_map/ppermute | solution.py:575
  10.4 0.5 collective-permute-start.1
  10.9 0.1 collective-permute-start
  11.1 0.6 collective-permute-start.4
  11.7 3.3 %collective-permute-start.3 = (f32[8,128]{1,0:T(8,128)S(1)}, f32[8,128]{1,0:T(8,128)S(1)}, u32[]{:S(2)}, u32[]{:S(2)}) collective-permute-start(f32[8,128]{1,0:T(8,128)S(1)} %get-tuple-element.22), channel_id=1, source_target_pairs={{0,1},{1,0},{2,3},{3,2},{4,5},{5,4},{6,7},{7,6},{8,9},{9,8},{10,11... | collective-permute-start | bytes 12296 | tf_op jit(solution)/shard_map/ppermute | solution.py:575
  15.0 0.0 collective-permute-done.4.far_ref
  15.0 0.8 %collective-permute-done.3.near_ref = f32[8,128]{1,0:T(8,128)S(1)} collective-permute-done((f32[8,128]{1,0:T(8,128)S(1)}, f32[8,128]{1,0:T(8,128)S(1)}, u32[]{:S(2)}, u32[]{:S(2)}) %collective-permute-start.3) | collective-permute-done | bytes 4128 | tf_op jit(solution)/shard_map/ppermute | solution.py:575
  15.9 3.7 %collective-permute-start.8 = (f32[120,128]{1,0:T(8,128)S(1)}, f32[120,128]{1,0:T(8,128)S(1)}, u32[]{:S(2)}, u32[]{:S(2)}) collective-permute-start(f32[120,128]{1,0:T(8,128)S(1)} %rims.2.refs_4_.refs_0_), channel_id=1, source_target_pairs={{0,24},{8,16},{16,8},{24,0},{1,25},{9,17},{17,9},{25,1},{2,26},{10... | collective-permute-start | bytes 184328 | tf_op jit(solution)/shard_map/ppermute | solution.py:575
  19.5 0.8 %collective-permute-start.6 = (f32[120,128]{1,0:T(8,128)S(1)}, f32[120,128]{1,0:T(8,128)S(1)}, u32[]{:S(2)}, u32[]{:S(2)}) collective-permute-start(f32[120,128]{1,0:T(8,128)S(1)} %rims.2.refs_4_.refs_0_), channel_id=1, source_target_pairs={{0,8},{8,0},{16,24},{24,16},{1,9},{9,1},{17,25},{25,17},{2,10},{10... | collective-permute-start | bytes 184328 | tf_op jit(solution)/shard_map/ppermute | solution.py:575
  20.3 0.5 dense_first.1
  20.9 0.0 copy-start
  20.9 2.3 %collective-permute-start.5 = (f32[1288,128]{1,0:T(8,128)S(1)}, f32[1288,128]{1,0:T(8,128)S(1)}, u32[]{:S(2)}, u32[]{:S(2)}) collective-permute-start(f32[1288,128]{1,0:T(8,128)S(1)} %get-tuple-element.25.mine_ref), channel_id=1, source_target_pairs={{0,1},{1,0},{2,3},{3,2},{4,5},{5,4},{6,7},{7,6},{8,9},{9,8},{10,11... | collective-permute-start | bytes 1978376 | tf_op jit(solution)/shard_map/ppermute | solution.py:575
  23.1 2.7 %collective-permute-done.7.refs_2_ = f32[120,128]{1,0:T(8,128)S(1)} collective-permute-done((f32[120,128]{1,0:T(8,128)S(1)}, f32[120,128]{1,0:T(8,128)S(1)}, u32[]{:S(2)}, u32[]{:S(2)}) %collective-permute-start.7) | collective-permute-done | bytes 61472 | tf_op jit(solution)/shard_map/ppermute | solution.py:575
  25.9 4.8 %middle.1 = (f32[8,128]{1,0:T(8,128)S(1)}, f32[120,128]{1,0:T(8,128)S(1)}, f32[8,128]{1,0:T(8,128)S(1)}, f32[3,32,128]{2,1,0:T(8,128)S(1)}, f32[5,32,128]{2,1,0:T(8,128)S(1)}, /*index=5*/f32[128,128]{1,0:T(8,128)S(1)}) custom-call(s32[128]{0:T(128)} %slot_hbm.7, s32[128]{0:T(128)} %offset_hbm.5, s32[8,8]{1,0:T(8,128)} %block_hbm.3, ...), custom_call_target="tpu_custom_call" | custom-call | tf_op jit(solution)/shard_map/middle/pallas_call | solution.py:639
  30.7 1.4 %later_sources.1.refs_1_ = f32[328,128]{1,0:T(8,128)S(1)} custom-call(s32[128]{0:T(128)} %slot_hbm.7, f32[128,8,128]{2,1,0:T(8,128)S(1)} %get-tuple-element.24.sources.design, f32[128,128]{1,0:T(8,128)S(1)} %get-tuple-element.27.y_ref, f32[8,128]{1,0:T(8,128)S(1)} %get-tuple-element.28.numbers_ref), custom_call_target="tpu_custom_call" | custom-call | tf_op jit(solution)/shard_map/later_sources/pallas_call | solution.py:648
  32.1 2.0 %collective-permute-start.11 = (f32[328,128]{1,0:T(8,128)S(1)}, f32[328,128]{1,0:T(8,128)S(1)}, u32[]{:S(2)}, u32[]{:S(2)}) collective-permute-start(f32[328,128]{1,0:T(8,128)S(1)} %later_sources.1.refs_1_), channel_id=1, source_target_pairs={{0,6},{1,7},{2,4},{3,5},{4,2},{5,3},{6,0},{7,1},{8,14},{9,15},{10,... | collective-permute-start | bytes 503816 | tf_op jit(solution)/shard_map/ppermute | solution.py:575
  34.0 2.6 %collective-permute-start.10 = (f32[328,128]{1,0:T(8,128)S(1)}, f32[328,128]{1,0:T(8,128)S(1)}, u32[]{:S(2)}, u32[]{:S(2)}) collective-permute-start(f32[328,128]{1,0:T(8,128)S(1)} %later_sources.1.refs_1_), channel_id=1, source_target_pairs={{0,4},{1,5},{2,6},{3,7},{4,0},{5,1},{6,2},{7,3},{8,12},{9,13},{10,... | collective-permute-start | bytes 503816 | tf_op jit(solution)/shard_map/ppermute | solution.py:575
  36.6 0.7 collective-permute-start.13
  37.3 3.5 %collective-permute-start.12 = (f32[8,128]{1,0:T(8,128)S(1)}, f32[8,128]{1,0:T(8,128)S(1)}, u32[]{:S(2)}, u32[]{:S(2)}) collective-permute-start(f32[8,128]{1,0:T(8,128)S(1)} %get-tuple-element.30), channel_id=1, source_target_pairs={{0,1},{1,0},{2,3},{3,2},{4,5},{5,4},{6,7},{7,6},{8,9},{9,8},{10,11... | collective-permute-start | bytes 12296 | tf_op jit(solution)/shard_map/ppermute | solution.py:575
  40.7 0.8 %collective-permute-done.12.near_ref = f32[8,128]{1,0:T(8,128)S(1)} collective-permute-done((f32[8,128]{1,0:T(8,128)S(1)}, f32[8,128]{1,0:T(8,128)S(1)}, u32[]{:S(2)}, u32[]{:S(2)}) %collective-permute-start.12) | collective-permute-done | bytes 4128 | tf_op jit(solution)/shard_map/ppermute | solution.py:575
  41.6 2.5 %collective-permute-start.17 = (f32[120,128]{1,0:T(8,128)S(1)}, f32[120,128]{1,0:T(8,128)S(1)}, u32[]{:S(2)}, u32[]{:S(2)}) collective-permute-start(f32[120,128]{1,0:T(8,128)S(1)} %rims.3.refs_5_.refs_0_), channel_id=1, source_target_pairs={{0,24},{8,16},{16,8},{24,0},{1,25},{9,17},{17,9},{25,1},{2,26},{10... | collective-permute-start | bytes 184328 | tf_op jit(solution)/shard_map/ppermute | solution.py:575
  44.1 0.3 collective-permute-start.16
  44.4 1.6 %collective-permute-start.15 = (f32[120,128]{1,0:T(8,128)S(1)}, f32[120,128]{1,0:T(8,128)S(1)}, u32[]{:S(2)}, u32[]{:S(2)}) collective-permute-start(f32[120,128]{1,0:T(8,128)S(1)} %rims.3.refs_5_.refs_0_), channel_id=1, source_target_pairs={{0,8},{8,0},{16,24},{24,16},{1,9},{9,1},{17,25},{25,17},{2,10},{10... | collective-permute-start | bytes 184328 | tf_op jit(solution)/shard_map/ppermute | solution.py:575
  46.0 0.5 dense_second.1.mine_ref
  46.6 1.5 %collective-permute-start.14 = (f32[1288,128]{1,0:T(8,128)S(1)}, f32[1288,128]{1,0:T(8,128)S(1)}, u32[]{:S(2)}, u32[]{:S(2)}) collective-permute-start(f32[1288,128]{1,0:T(8,128)S(1)} %dense_second.1.mine_ref), channel_id=1, source_target_pairs={{0,1},{1,0},{2,3},{3,2},{4,5},{5,4},{6,7},{7,6},{8,9},{9,8},{10,11... | collective-permute-start | bytes 1978376 | tf_op jit(solution)/shard_map/ppermute | solution.py:575
  48.0 3.0 %collective-permute-done.16.refs_2_ = f32[120,128]{1,0:T(8,128)S(1)} collective-permute-done((f32[120,128]{1,0:T(8,128)S(1)}, f32[120,128]{1,0:T(8,128)S(1)}, u32[]{:S(2)}, u32[]{:S(2)}) %collective-permute-start.16) | collective-permute-done | bytes 61472 | tf_op jit(solution)/shard_map/ppermute | solution.py:575
  51.1 2.9 %last.1 = (f32[3,32,128]{2,1,0:T(8,128)S(1)}, f32[5,32,128]{2,1,0:T(8,128)S(1)}, f32[32,1,128]{2,1,0:T(1,128)S(1)}) custom-call(s32[128]{0:T(128)} %slot_hbm.7, s32[128]{0:T(128)} %offset_hbm.5, s32[8,8]{1,0:T(8,128)} %block_hbm.3, f32[1288,128]{1,0:T(8,128)S(1)} %dense_second.1.mine_ref, f32[1288,128]{1,0:T(8,128)S(1)} %collective-permute-done.14.other_ref, ...), custom_call_target="tpu_custom_call" | custom-call | tf_op jit(solution)/shard_map/last/pallas_call | solution.py:657
  54.0 11.0 %all_to_all.5.got_ref = f32[32,1,128]{2,1,0:T(1,128)S(1)} all-to-all(f32[32,1,128]{2,1,0:T(1,128)S(1)} %get-tuple-element.33), channel_id=1, replica_groups=mesh['src'=4,'tm'=8] {'src','tm'}, dimensions={0} | all-to-all | bytes 32768 | tf_op jit(solution)/shard_map/all_to_all | solution.py:668
  65.0 1.0 %final.1 = (f32[5,32,128]{2,1,0:T(8,128)}, f32[3,4096]{1,0:T(4,128)}) custom-call(f32[32,1,128]{2,1,0:T(1,128)S(1)} %all_to_all.5.got_ref, f32[5,32,128]{2,1,0:T(8,128)S(1)} %get-tuple-element.32.z_src, f32[5,32,128]{2,1,0:T(8,128)S(1)} %get-tuple-element.34.w_src, f32[3,32,128]{2,1,0:T(8,128)S(1)} %get-tuple-element.31.z_att, ...), custom_call_target="tpu_custom_call" | custom-call | tf_op jit(solution)/shard_map/final/pallas_call | solution.py:669
  (25 shorter events, 0.1 us)
Async XLA Ops:
  0.6 4.3 %copy-start.1 = (f32[128,5,128]{2,0,1:T(8,128)S(1)}, f32[128,5,128]{2,0,1:T(8,128)}, u32[]{:S(2)}) copy-start(f32[128,5,128]{2,0,1:T(8,128)} %param.9) | copy-start | bytes 983044
  0.6 4.3 %copy-start.2 = (f32[128,128]{1,0:T(8,128)S(1)}, f32[128,128]{1,0:T(8,128)}, u32[]{:S(2)}) copy-start(f32[128,128]{1,0:T(8,128)} %obs_ref.1) | copy-start | bytes 196612
  0.7 4.3 %copy-start.3 = (s32[8,8]{1,0:T(8,128)S(1)}, s32[8,8]{1,0:T(8,128)}, u32[]{:S(2)}) copy-start(s32[8,8]{1,0:T(8,128)} %block_hbm.3) | copy-start | bytes 772
  6.5 13.1 %collective-permute-start.2 = (f32[328,128]{1,0:T(8,128)S(1)}, f32[328,128]{1,0:T(8,128)S(1)}, u32[]{:S(2)}, u32[]{:S(2)}) collective-permute-start(f32[328,128]{1,0:T(8,128)S(1)} %get-tuple-element.21.refs_0_), channel_id=1, source_target_pairs={{0,6},{1,7},{2,4},{3,5},{4,2},{5,3},{6,0},{7,1},{8,14},{9,15},{10,... | collective-permute-start | bytes 503816 | tf_op jit(solution)/shard_map/ppermute | solution.py:575
  10.4 9.9 %collective-permute-start.1 = (f32[328,128]{1,0:T(8,128)S(1)}, f32[328,128]{1,0:T(8,128)S(1)}, u32[]{:S(2)}, u32[]{:S(2)}) collective-permute-start(f32[328,128]{1,0:T(8,128)S(1)} %get-tuple-element.21.refs_0_), channel_id=1, source_target_pairs={{0,4},{1,5},{2,6},{3,7},{4,0},{5,1},{6,2},{7,3},{8,12},{9,13},{10,... | collective-permute-start | bytes 503816 | tf_op jit(solution)/shard_map/ppermute | solution.py:575
  10.9 9.4 %collective-permute-start = (f32[328,128]{1,0:T(8,128)S(1)}, f32[328,128]{1,0:T(8,128)S(1)}, u32[]{:S(2)}, u32[]{:S(2)}) collective-permute-start(f32[328,128]{1,0:T(8,128)S(1)} %get-tuple-element.21.refs_0_), channel_id=1, source_target_pairs={{0,2},{1,3},{2,0},{3,1},{4,6},{5,7},{6,4},{7,5},{8,10},{9,11},{10,... | collective-permute-start | bytes 503816 | tf_op jit(solution)/shard_map/ppermute | solution.py:575
  11.1 4.0 %collective-permute-start.4 = (f32[8,128]{1,0:T(8,128)S(1)}, f32[8,128]{1,0:T(8,128)S(1)}, u32[]{:S(2)}, u32[]{:S(2)}) collective-permute-start(f32[8,128]{1,0:T(8,128)S(1)} %get-tuple-element.22), channel_id=1, source_target_pairs={{1,2},{3,4},{5,6},{2,1},{4,3},{6,5},{9,10},{11,12},{13,14},{10,9},... | collective-permute-start | bytes 12296 | tf_op jit(solution)/shard_map/ppermute | solution.py:580
  11.7 4.1 %collective-permute-start.3 = (f32[8,128]{1,0:T(8,128)S(1)}, f32[8,128]{1,0:T(8,128)S(1)}, u32[]{:S(2)}, u32[]{:S(2)}) collective-permute-start(f32[8,128]{1,0:T(8,128)S(1)} %get-tuple-element.22), channel_id=1, source_target_pairs={{0,1},{1,0},{2,3},{3,2},{4,5},{5,4},{6,7},{7,6},{8,9},{9,8},{10,11... | collective-permute-start | bytes 12296 | tf_op jit(solution)/shard_map/ppermute | solution.py:575
  15.9 7.3 %collective-permute-start.8 = (f32[120,128]{1,0:T(8,128)S(1)}, f32[120,128]{1,0:T(8,128)S(1)}, u32[]{:S(2)}, u32[]{:S(2)}) collective-permute-start(f32[120,128]{1,0:T(8,128)S(1)} %rims.2.refs_4_.refs_0_), channel_id=1, source_target_pairs={{0,24},{8,16},{16,8},{24,0},{1,25},{9,17},{17,9},{25,1},{2,26},{10... | collective-permute-start | bytes 184328 | tf_op jit(solution)/shard_map/ppermute | solution.py:575
  19.5 6.3 %collective-permute-start.7 = (f32[120,128]{1,0:T(8,128)S(1)}, f32[120,128]{1,0:T(8,128)S(1)}, u32[]{:S(2)}, u32[]{:S(2)}) collective-permute-start(f32[120,128]{1,0:T(8,128)S(1)} %rims.2.refs_4_.refs_0_), channel_id=1, source_target_pairs={{0,16},{8,24},{16,0},{24,8},{1,17},{9,25},{17,1},{25,9},{2,18},{10... | collective-permute-start | bytes 184328 | tf_op jit(solution)/shard_map/ppermute | solution.py:575
  19.5 6.3 %collective-permute-start.6 = (f32[120,128]{1,0:T(8,128)S(1)}, f32[120,128]{1,0:T(8,128)S(1)}, u32[]{:S(2)}, u32[]{:S(2)}) collective-permute-start(f32[120,128]{1,0:T(8,128)S(1)} %rims.2.refs_4_.refs_0_), channel_id=1, source_target_pairs={{0,8},{8,0},{16,24},{24,16},{1,9},{9,1},{17,25},{25,17},{2,10},{10... | collective-permute-start | bytes 184328 | tf_op jit(solution)/shard_map/ppermute | solution.py:575
  20.9 5.0 %copy-start = (s32[128,128]{1,0:T(8,128)S(1)}, s32[128,128]{1,0:T(8,128)}, u32[]{:S(2)}) copy-start(s32[128,128]{1,0:T(8,128)} %knot_ref.3) | copy-start | bytes 196612
  20.9 5.0 %collective-permute-start.5 = (f32[1288,128]{1,0:T(8,128)S(1)}, f32[1288,128]{1,0:T(8,128)S(1)}, u32[]{:S(2)}, u32[]{:S(2)}) collective-permute-start(f32[1288,128]{1,0:T(8,128)S(1)} %get-tuple-element.25.mine_ref), channel_id=1, source_target_pairs={{0,1},{1,0},{2,3},{3,2},{4,5},{5,4},{6,7},{7,6},{8,9},{9,8},{10,11... | collective-permute-start | bytes 1978376 | tf_op jit(solution)/shard_map/ppermute | solution.py:575
  32.1 12.4 %collective-permute-start.11 = (f32[328,128]{1,0:T(8,128)S(1)}, f32[328,128]{1,0:T(8,128)S(1)}, u32[]{:S(2)}, u32[]{:S(2)}) collective-permute-start(f32[328,128]{1,0:T(8,128)S(1)} %later_sources.1.refs_1_), channel_id=1, source_target_pairs={{0,6},{1,7},{2,4},{3,5},{4,2},{5,3},{6,0},{7,1},{8,14},{9,15},{10,... | collective-permute-start | bytes 503816 | tf_op jit(solution)/shard_map/ppermute | solution.py:575
  34.0 12.0 %collective-permute-start.10 = (f32[328,128]{1,0:T(8,128)S(1)}, f32[328,128]{1,0:T(8,128)S(1)}, u32[]{:S(2)}, u32[]{:S(2)}) collective-permute-start(f32[328,128]{1,0:T(8,128)S(1)} %later_sources.1.refs_1_), channel_id=1, source_target_pairs={{0,4},{1,5},{2,6},{3,7},{4,0},{5,1},{6,2},{7,3},{8,12},{9,13},{10,... | collective-permute-start | bytes 503816 | tf_op jit(solution)/shard_map/ppermute | solution.py:575
  36.6 9.4 %collective-permute-start.9 = (f32[328,128]{1,0:T(8,128)S(1)}, f32[328,128]{1,0:T(8,128)S(1)}, u32[]{:S(2)}, u32[]{:S(2)}) collective-permute-start(f32[328,128]{1,0:T(8,128)S(1)} %later_sources.1.refs_1_), channel_id=1, source_target_pairs={{0,2},{1,3},{2,0},{3,1},{4,6},{5,7},{6,4},{7,5},{8,10},{9,11},{10,... | collective-permute-start | bytes 503816 | tf_op jit(solution)/shard_map/ppermute | solution.py:575
  36.6 4.1 %collective-permute-start.13 = (f32[8,128]{1,0:T(8,128)S(1)}, f32[8,128]{1,0:T(8,128)S(1)}, u32[]{:S(2)}, u32[]{:S(2)}) collective-permute-start(f32[8,128]{1,0:T(8,128)S(1)} %get-tuple-element.30), channel_id=1, source_target_pairs={{1,2},{3,4},{5,6},{2,1},{4,3},{6,5},{9,10},{11,12},{13,14},{10,9},... | collective-permute-start | bytes 12296 | tf_op jit(solution)/shard_map/ppermute | solution.py:580
  37.3 4.3 %collective-permute-start.12 = (f32[8,128]{1,0:T(8,128)S(1)}, f32[8,128]{1,0:T(8,128)S(1)}, u32[]{:S(2)}, u32[]{:S(2)}) collective-permute-start(f32[8,128]{1,0:T(8,128)S(1)} %get-tuple-element.30), channel_id=1, source_target_pairs={{0,1},{1,0},{2,3},{3,2},{4,5},{5,4},{6,7},{7,6},{8,9},{9,8},{10,11... | collective-permute-start | bytes 12296 | tf_op jit(solution)/shard_map/ppermute | solution.py:575
  41.6 6.5 %collective-permute-start.17 = (f32[120,128]{1,0:T(8,128)S(1)}, f32[120,128]{1,0:T(8,128)S(1)}, u32[]{:S(2)}, u32[]{:S(2)}) collective-permute-start(f32[120,128]{1,0:T(8,128)S(1)} %rims.3.refs_5_.refs_0_), channel_id=1, source_target_pairs={{0,24},{8,16},{16,8},{24,0},{1,25},{9,17},{17,9},{25,1},{2,26},{10... | collective-permute-start | bytes 184328 | tf_op jit(solution)/shard_map/ppermute | solution.py:575
  44.1 6.9 %collective-permute-start.16 = (f32[120,128]{1,0:T(8,128)S(1)}, f32[120,128]{1,0:T(8,128)S(1)}, u32[]{:S(2)}, u32[]{:S(2)}) collective-permute-start(f32[120,128]{1,0:T(8,128)S(1)} %rims.3.refs_5_.refs_0_), channel_id=1, source_target_pairs={{0,16},{8,24},{16,0},{24,8},{1,17},{9,25},{17,1},{25,9},{2,18},{10... | collective-permute-start | bytes 184328 | tf_op jit(solution)/shard_map/ppermute | solution.py:575
  44.4 6.6 %collective-permute-start.15 = (f32[120,128]{1,0:T(8,128)S(1)}, f32[120,128]{1,0:T(8,128)S(1)}, u32[]{:S(2)}, u32[]{:S(2)}) collective-permute-start(f32[120,128]{1,0:T(8,128)S(1)} %rims.3.refs_5_.refs_0_), channel_id=1, source_target_pairs={{0,8},{8,0},{16,24},{24,16},{1,9},{9,1},{17,25},{25,17},{2,10},{10... | collective-permute-start | bytes 184328 | tf_op jit(solution)/shard_map/ppermute | solution.py:575
  46.6 4.5 %collective-permute-start.14 = (f32[1288,128]{1,0:T(8,128)S(1)}, f32[1288,128]{1,0:T(8,128)S(1)}, u32[]{:S(2)}, u32[]{:S(2)}) collective-permute-start(f32[1288,128]{1,0:T(8,128)S(1)} %dense_second.1.mine_ref), channel_id=1, source_target_pairs={{0,1},{1,0},{2,3},{3,2},{4,5},{5,4},{6,7},{7,6},{8,9},{9,8},{10,11... | collective-permute-start | bytes 1978376 | tf_op jit(solution)/shard_map/ppermute | solution.py:575

commit v6 on v5

--- a/solution.py
+++ b/solution.py
@@ -14,13 +14,17 @@
 
 LANES = 128
 ROWS = KN // LANES
-ROWS_PAD = (ROWS + 8) // 8 * 8
 AXES = 3
+PART = AXES * ROWS + 8
 PARAMS = 5
 CAP = 8
 UNROLL = 128
 F32 = jnp.float32
 BF16 = jnp.bfloat16
+
+
+def place_of(axis, row):
+    return axis * ROWS + row if row < ROWS else AXES * ROWS + axis
 
 
 def iota(shape, dim):
@@ -103,7 +107,8 @@
         both = jnp.where(low, one + moved[1], moved[0] + moved[2])
         both = both + pltpu.roll(both, 4, 0)
         for axis in range(AXES):
-            att_ref[axis * ROWS_PAD + row : axis * ROWS_PAD + row + 1, :] = both[axis : axis + 1]
+            at = place_of(axis, row)
+            att_ref[at : at + 1, :] = both[axis : axis + 1]
         if row == 0:
             rim_ref[...] = both
         before = now
@@ -255,9 +260,9 @@
     has_right = jnp.where(me < owners - 1, 1.0, 0.0)
     out_ref[...] = part_ref[...]
     for axis in range(AXES):
-        at = axis * ROWS_PAD
+        at = place_of(axis, 0)
         out_ref[at : at + 1, :] = part_ref[at : at + 1, :] + left[4 + axis : 5 + axis]
-        at = at + ROWS
+        at = place_of(axis, ROWS)
         out_ref[at : at + 1, :] = has_right * part_ref[at : at + 1, :] + right[axis : axis + 1]
 
 
@@ -321,10 +326,10 @@
         level = [level[k] + level[k + 1] for k in range(0, len(level), 2)]
     att = level[0]
     for axis in range(AXES):
-        true_ref[axis] = att[axis * ROWS_PAD : axis * ROWS_PAD + ROWS]
+        true_ref[axis] = att[axis * ROWS : axis * ROWS + ROWS]
 
     def mixed(row):
-        three = [att[axis * ROWS_PAD + row : axis * ROWS_PAD + row + 1] for axis in range(AXES)]
+        three = [att[place_of(axis, row) : place_of(axis, row) + 1] for axis in range(AXES)]
         three = [jnp.broadcast_to(v, (8, LANES)) for v in three]
         out = jnp.where(axis_of == 0, three[0], jnp.where(axis_of == 1, three[1], three[2]))
         return jnp.where(axis_of < 3, out, 0.0)
@@ -565,7 +570,7 @@
     dense = pltpu.VMEM((8 * blocks, LANES), F32)
     piece = f32(PARAMS * slots + 8, LANES)
     summed = f32(PARAMS * blocks + 8, LANES)
-    part = f32(AXES * ROWS_PAD, LANES)
+    part = f32(PART, LANES)
     true = f32(AXES, ROWS, LANES)
     mine = f32(PARAMS, SB_DEV, LANES)
     rim = f32(8, LANES)

time: 66.4 us -> 65.3 us (0.983)
  waiting for transfers between devices: 7.38 us -> 5.96 us
    ppermute x16, waiting for transfers between devices: 7.38 us -> 5.95 us  [flipped(): return lax.ppermute(value, axis, [(i, i ^ bits) for i in range(size)])]
where the time goes in v6:
time: 65.3 us; the launch traced here: 65 us
  starting transfers between devices  30.2 us (46%)
  Pallas kernels  16.9 us (26%)
  blocking collectives  11 us (17%)
  waiting for transfers between devices  5.96 us (9%)
  between operations  0.79 us (1%)
    ppermute x16, starting transfers between devices, flipped(): return lax.ppermute(value, axis, [(i, i ^ bits) for i in range(size)])  28.9 us
    all_to_all x1, blocking collectives, shards(): row = lax.all_to_all(row, ('src', 'tm'), 0, 0, tiled=True)  11 us
    ppermute x16, waiting for transfers between devices, flipped(): return lax.ppermute(value, axis, [(i, i ^ bits) for i in range(size)])  5.95 us
    pallas_call x1, Pallas kernels, shards(): call(functools.partial(middle_kernel, copies), (rim, part, rim, true, min...  4.76 us
    pallas_call x1, Pallas kernels, shards(): call(first_kernel, (f32(tiles, 16, LANES), part, rim), [HBM] * 6, [knots,...  4.3 us
    pallas_call x1, Pallas kernels, shards(): call(functools.partial(last_kernel, copies), (true, mine, f32(devices, 1,...  2.87 us
    pallas_call x1, Pallas kernels, shards(): call(first_sources, (f32(tiles, 8, LANES), piece), [HBM] * 2 + [VMEM] * 3...  1.45 us
    pallas_call x1, Pallas kernels, shards(): call(later_sources, piece, [HBM] + [VMEM] * 3, [acc, pltpu.SMEM((tiles,),...  1.38 us
  transfers between devices with their start and end apart: 18, of which 4 were waited for; matrix products, arithmetic and copies ran while one was open for 0% of the time, Pallas kernels for 2%

profile of v6, /device:TPU:0, one launch (start us, length us, event | category | flops | bytes accessed | tf_op | source)
XLA Modules:
  0.0 65.0 jit_solution(14331708704734516046)
XLA Ops:
  0.7 0.0 copy-start.3
  0.7 4.3 %first.1 = (f32[128,16,128]{2,1,0:T(8,128)S(1)}, f32[104,128]{1,0:T(8,128)S(1)}, f32[8,128]{1,0:T(8,128)S(1)}) custom-call(s32[128]{0:T(128)} %offset_hbm.5, s32[128]{0:T(128)} %valid_hbm.3, f32[384,128]{1,0:T(8,128)} %bitcast.8, f32[128,128]{1,0:T(8,128)} %frac_hbm.1, s32[128,128]{1,0:T(8,128)} %knot_ref.3, f32[128,128]{1,0:T(8,128)} %obs_ref.1), custom_call_target="tpu_custom_call" | custom-call | tf_op jit(solution)/shard_map/first/pallas_call | solution.py:615
  5.0 1.5 %first_sources.1 = (f32[128,8,128]{2,1,0:T(8,128)S(1)}, f32[328,128]{1,0:T(8,128)S(1)}) custom-call(s32[128]{0:T(128)} %slot_hbm.7, s32[128]{0:T(128)} %valid_hbm.3, f32[640,128]{1,0:T(8,128)S(1)} %bitcast.7, f32[128,128]{1,0:T(8,128)S(1)} %copy-done.2, s32[8,8]{1,0:T(8,128)S(1)} %copy-done.3, f32[104,128]{1,0:T(8,128)S(1)} %get-tuple-element.20.after_ref.part_ref), custom_call_target="tpu_custom_call" | custom-call | tf_op jit(solution)/shard_map/first_sources/pallas_call | solution.py:635
  6.5 4.0 %collective-permute-start.2 = (f32[328,128]{1,0:T(8,128)S(1)}, f32[328,128]{1,0:T(8,128)S(1)}, u32[]{:S(2)}, u32[]{:S(2)}) collective-permute-start(f32[328,128]{1,0:T(8,128)S(1)} %get-tuple-element.21.refs_0_), channel_id=1, source_target_pairs={{0,6},{1,7},{2,4},{3,5},{4,2},{5,3},{6,0},{7,1},{8,14},{9,15},{10,... | collective-permute-start | bytes 503816 | tf_op jit(solution)/shard_map/ppermute | solution.py:580
  10.4 0.5 collective-permute-start.1
  10.9 0.1 collective-permute-start
  11.1 0.6 collective-permute-start.4
  11.7 3.3 %collective-permute-start.3 = (f32[8,128]{1,0:T(8,128)S(1)}, f32[8,128]{1,0:T(8,128)S(1)}, u32[]{:S(2)}, u32[]{:S(2)}) collective-permute-start(f32[8,128]{1,0:T(8,128)S(1)} %get-tuple-element.22), channel_id=1, source_target_pairs={{0,1},{1,0},{2,3},{3,2},{4,5},{5,4},{6,7},{7,6},{8,9},{9,8},{10,11... | collective-permute-start | bytes 12296 | tf_op jit(solution)/shard_map/ppermute | solution.py:580
  15.0 0.8 %collective-permute-done.3.near_ref = f32[8,128]{1,0:T(8,128)S(1)} collective-permute-done((f32[8,128]{1,0:T(8,128)S(1)}, f32[8,128]{1,0:T(8,128)S(1)}, u32[]{:S(2)}, u32[]{:S(2)}) %collective-permute-start.3) | collective-permute-done | bytes 4128 | tf_op jit(solution)/shard_map/ppermute | solution.py:580
  15.9 3.7 %collective-permute-start.8 = (f32[104,128]{1,0:T(8,128)S(1)}, f32[104,128]{1,0:T(8,128)S(1)}, u32[]{:S(2)}, u32[]{:S(2)}) collective-permute-start(f32[104,128]{1,0:T(8,128)S(1)} %rims.2.refs_4_.refs_0_), channel_id=1, source_target_pairs={{0,24},{8,16},{16,8},{24,0},{1,25},{9,17},{17,9},{25,1},{2,26},{10... | collective-permute-start | bytes 159752 | tf_op jit(solution)/shard_map/ppermute | solution.py:580
  19.5 0.8 %collective-permute-start.6 = (f32[104,128]{1,0:T(8,128)S(1)}, f32[104,128]{1,0:T(8,128)S(1)}, u32[]{:S(2)}, u32[]{:S(2)}) collective-permute-start(f32[104,128]{1,0:T(8,128)S(1)} %rims.2.refs_4_.refs_0_), channel_id=1, source_target_pairs={{0,8},{8,0},{16,24},{24,16},{1,9},{9,1},{17,25},{25,17},{2,10},{10... | collective-permute-start | bytes 159752 | tf_op jit(solution)/shard_map/ppermute | solution.py:580
  20.3 0.5 dense_first.1
  20.9 0.0 copy-start
  20.9 2.3 %collective-permute-start.5 = (f32[1288,128]{1,0:T(8,128)S(1)}, f32[1288,128]{1,0:T(8,128)S(1)}, u32[]{:S(2)}, u32[]{:S(2)}) collective-permute-start(f32[1288,128]{1,0:T(8,128)S(1)} %get-tuple-element.25.mine_ref), channel_id=1, source_target_pairs={{0,1},{1,0},{2,3},{3,2},{4,5},{5,4},{6,7},{7,6},{8,9},{9,8},{10,11... | collective-permute-start | bytes 1978376 | tf_op jit(solution)/shard_map/ppermute | solution.py:580
  23.1 1.7 %collective-permute-done.7.refs_2_ = f32[104,128]{1,0:T(8,128)S(1)} collective-permute-done((f32[104,128]{1,0:T(8,128)S(1)}, f32[104,128]{1,0:T(8,128)S(1)}, u32[]{:S(2)}, u32[]{:S(2)}) %collective-permute-start.7) | collective-permute-done | bytes 53280 | tf_op jit(solution)/shard_map/ppermute | solution.py:580
  24.8 0.0 collective-permute-done.5.other_ref
  24.9 4.8 %middle.1 = (f32[8,128]{1,0:T(8,128)S(1)}, f32[104,128]{1,0:T(8,128)S(1)}, f32[8,128]{1,0:T(8,128)S(1)}, f32[3,32,128]{2,1,0:T(8,128)S(1)}, f32[5,32,128]{2,1,0:T(8,128)S(1)}, /*index=5*/f32[128,128]{1,0:T(8,128)S(1)}) custom-call(s32[128]{0:T(128)} %slot_hbm.7, s32[128]{0:T(128)} %offset_hbm.5, s32[8,8]{1,0:T(8,128)} %block_hbm.3, ...), custom_call_target="tpu_custom_call" | custom-call | tf_op jit(solution)/shard_map/middle/pallas_call | solution.py:644
  29.6 1.4 %later_sources.1.refs_1_ = f32[328,128]{1,0:T(8,128)S(1)} custom-call(s32[128]{0:T(128)} %slot_hbm.7, f32[128,8,128]{2,1,0:T(8,128)S(1)} %get-tuple-element.24.sources.design, f32[128,128]{1,0:T(8,128)S(1)} %get-tuple-element.27.y_ref, f32[8,128]{1,0:T(8,128)S(1)} %get-tuple-element.28.numbers_ref), custom_call_target="tpu_custom_call" | custom-call | tf_op jit(solution)/shard_map/later_sources/pallas_call | solution.py:653
  31.0 2.9 %collective-permute-start.11 = (f32[328,128]{1,0:T(8,128)S(1)}, f32[328,128]{1,0:T(8,128)S(1)}, u32[]{:S(2)}, u32[]{:S(2)}) collective-permute-start(f32[328,128]{1,0:T(8,128)S(1)} %later_sources.1.refs_1_), channel_id=1, source_target_pairs={{0,6},{1,7},{2,4},{3,5},{4,2},{5,3},{6,0},{7,1},{8,14},{9,15},{10,... | collective-permute-start | bytes 503816 | tf_op jit(solution)/shard_map/ppermute | solution.py:580
  33.9 2.0 %collective-permute-start.10 = (f32[328,128]{1,0:T(8,128)S(1)}, f32[328,128]{1,0:T(8,128)S(1)}, u32[]{:S(2)}, u32[]{:S(2)}) collective-permute-start(f32[328,128]{1,0:T(8,128)S(1)} %later_sources.1.refs_1_), channel_id=1, source_target_pairs={{0,4},{1,5},{2,6},{3,7},{4,0},{5,1},{6,2},{7,3},{8,12},{9,13},{10,... | collective-permute-start | bytes 503816 | tf_op jit(solution)/shard_map/ppermute | solution.py:580
  36.0 0.7 %collective-permute-start.13 = (f32[8,128]{1,0:T(8,128)S(1)}, f32[8,128]{1,0:T(8,128)S(1)}, u32[]{:S(2)}, u32[]{:S(2)}) collective-permute-start(f32[8,128]{1,0:T(8,128)S(1)} %get-tuple-element.30), channel_id=1, source_target_pairs={{1,2},{3,4},{5,6},{2,1},{4,3},{6,5},{9,10},{11,12},{13,14},{10,9},... | collective-permute-start | bytes 12296 | tf_op jit(solution)/shard_map/ppermute | solution.py:585
  36.6 3.5 %collective-permute-start.12 = (f32[8,128]{1,0:T(8,128)S(1)}, f32[8,128]{1,0:T(8,128)S(1)}, u32[]{:S(2)}, u32[]{:S(2)}) collective-permute-start(f32[8,128]{1,0:T(8,128)S(1)} %get-tuple-element.30), channel_id=1, source_target_pairs={{0,1},{1,0},{2,3},{3,2},{4,5},{5,4},{6,7},{7,6},{8,9},{9,8},{10,11... | collective-permute-start | bytes 12296 | tf_op jit(solution)/shard_map/ppermute | solution.py:580
  40.1 0.8 %collective-permute-done.12.near_ref = f32[8,128]{1,0:T(8,128)S(1)} collective-permute-done((f32[8,128]{1,0:T(8,128)S(1)}, f32[8,128]{1,0:T(8,128)S(1)}, u32[]{:S(2)}, u32[]{:S(2)}) %collective-permute-start.12) | collective-permute-done | bytes 4128 | tf_op jit(solution)/shard_map/ppermute | solution.py:580
  40.9 2.5 %collective-permute-start.17 = (f32[104,128]{1,0:T(8,128)S(1)}, f32[104,128]{1,0:T(8,128)S(1)}, u32[]{:S(2)}, u32[]{:S(2)}) collective-permute-start(f32[104,128]{1,0:T(8,128)S(1)} %rims.3.refs_5_.refs_0_), channel_id=1, source_target_pairs={{0,24},{8,16},{16,8},{24,0},{1,25},{9,17},{17,9},{25,1},{2,26},{10... | collective-permute-start | bytes 159752 | tf_op jit(solution)/shard_map/ppermute | solution.py:580
  43.4 0.5 collective-permute-start.16
  43.9 1.5 %collective-permute-start.15 = (f32[104,128]{1,0:T(8,128)S(1)}, f32[104,128]{1,0:T(8,128)S(1)}, u32[]{:S(2)}, u32[]{:S(2)}) collective-permute-start(f32[104,128]{1,0:T(8,128)S(1)} %rims.3.refs_5_.refs_0_), channel_id=1, source_target_pairs={{0,8},{8,0},{16,24},{24,16},{1,9},{9,1},{17,25},{25,17},{2,10},{10... | collective-permute-start | bytes 159752 | tf_op jit(solution)/shard_map/ppermute | solution.py:580
  45.4 0.5 dense_second.1.mine_ref
  45.9 1.5 %collective-permute-start.14 = (f32[1288,128]{1,0:T(8,128)S(1)}, f32[1288,128]{1,0:T(8,128)S(1)}, u32[]{:S(2)}, u32[]{:S(2)}) collective-permute-start(f32[1288,128]{1,0:T(8,128)S(1)} %dense_second.1.mine_ref), channel_id=1, source_target_pairs={{0,1},{1,0},{2,3},{3,2},{4,5},{5,4},{6,7},{7,6},{8,9},{9,8},{10,11... | collective-permute-start | bytes 1978376 | tf_op jit(solution)/shard_map/ppermute | solution.py:580
  47.4 2.6 %collective-permute-done.16.refs_2_ = f32[104,128]{1,0:T(8,128)S(1)} collective-permute-done((f32[104,128]{1,0:T(8,128)S(1)}, f32[104,128]{1,0:T(8,128)S(1)}, u32[]{:S(2)}, u32[]{:S(2)}) %collective-permute-start.16) | collective-permute-done | bytes 53280 | tf_op jit(solution)/shard_map/ppermute | solution.py:580
  50.0 2.9 %last.1 = (f32[3,32,128]{2,1,0:T(8,128)S(1)}, f32[5,32,128]{2,1,0:T(8,128)S(1)}, f32[32,1,128]{2,1,0:T(1,128)S(1)}) custom-call(s32[128]{0:T(128)} %slot_hbm.7, s32[128]{0:T(128)} %offset_hbm.5, s32[8,8]{1,0:T(8,128)} %block_hbm.3, f32[1288,128]{1,0:T(8,128)S(1)} %dense_second.1.mine_ref, f32[1288,128]{1,0:T(8,128)S(1)} %collective-permute-done.14.other_ref, ...), custom_call_target="tpu_custom_call" | custom-call | tf_op jit(solution)/shard_map/last/pallas_call | solution.py:662
  52.9 11.0 %all_to_all.5.got_ref = f32[32,1,128]{2,1,0:T(1,128)S(1)} all-to-all(f32[32,1,128]{2,1,0:T(1,128)S(1)} %get-tuple-element.33), channel_id=1, replica_groups=mesh['src'=4,'tm'=8] {'src','tm'}, dimensions={0} | all-to-all | bytes 32768 | tf_op jit(solution)/shard_map/all_to_all | solution.py:673
  63.9 1.0 %final.1 = (f32[5,32,128]{2,1,0:T(8,128)}, f32[3,4096]{1,0:T(4,128)}) custom-call(f32[32,1,128]{2,1,0:T(1,128)S(1)} %all_to_all.5.got_ref, f32[5,32,128]{2,1,0:T(8,128)S(1)} %get-tuple-element.32.z_src, f32[5,32,128]{2,1,0:T(8,128)S(1)} %get-tuple-element.34.w_src, f32[3,32,128]{2,1,0:T(8,128)S(1)} %get-tuple-element.31.z_att, ...), custom_call_target="tpu_custom_call" | custom-call | tf_op jit(solution)/shard_map/final/pallas_call | solution.py:674
  (25 shorter events, 0.1 us)
Async XLA Ops:
  0.6 4.3 %copy-start.1 = (f32[128,5,128]{2,0,1:T(8,128)S(1)}, f32[128,5,128]{2,0,1:T(8,128)}, u32[]{:S(2)}) copy-start(f32[128,5,128]{2,0,1:T(8,128)} %param.9) | copy-start | bytes 983044
  0.6 4.3 %copy-start.2 = (f32[128,128]{1,0:T(8,128)S(1)}, f32[128,128]{1,0:T(8,128)}, u32[]{:S(2)}) copy-start(f32[128,128]{1,0:T(8,128)} %obs_ref.1) | copy-start | bytes 196612
  0.7 4.3 %copy-start.3 = (s32[8,8]{1,0:T(8,128)S(1)}, s32[8,8]{1,0:T(8,128)}, u32[]{:S(2)}) copy-start(s32[8,8]{1,0:T(8,128)} %block_hbm.3) | copy-start | bytes 772
  6.5 13.1 %collective-permute-start.2 = (f32[328,128]{1,0:T(8,128)S(1)}, f32[328,128]{1,0:T(8,128)S(1)}, u32[]{:S(2)}, u32[]{:S(2)}) collective-permute-start(f32[328,128]{1,0:T(8,128)S(1)} %get-tuple-element.21.refs_0_), channel_id=1, source_target_pairs={{0,6},{1,7},{2,4},{3,5},{4,2},{5,3},{6,0},{7,1},{8,14},{9,15},{10,... | collective-permute-start | bytes 503816 | tf_op jit(solution)/shard_map/ppermute | solution.py:580
  10.4 9.9 %collective-permute-start.1 = (f32[328,128]{1,0:T(8,128)S(1)}, f32[328,128]{1,0:T(8,128)S(1)}, u32[]{:S(2)}, u32[]{:S(2)}) collective-permute-start(f32[328,128]{1,0:T(8,128)S(1)} %get-tuple-element.21.refs_0_), channel_id=1, source_target_pairs={{0,4},{1,5},{2,6},{3,7},{4,0},{5,1},{6,2},{7,3},{8,12},{9,13},{10,... | collective-permute-start | bytes 503816 | tf_op jit(solution)/shard_map/ppermute | solution.py:580
  10.9 9.4 %collective-permute-start = (f32[328,128]{1,0:T(8,128)S(1)}, f32[328,128]{1,0:T(8,128)S(1)}, u32[]{:S(2)}, u32[]{:S(2)}) collective-permute-start(f32[328,128]{1,0:T(8,128)S(1)} %get-tuple-element.21.refs_0_), channel_id=1, source_target_pairs={{0,2},{1,3},{2,0},{3,1},{4,6},{5,7},{6,4},{7,5},{8,10},{9,11},{10,... | collective-permute-start | bytes 503816 | tf_op jit(solution)/shard_map/ppermute | solution.py:580
  11.1 4.0 %collective-permute-start.4 = (f32[8,128]{1,0:T(8,128)S(1)}, f32[8,128]{1,0:T(8,128)S(1)}, u32[]{:S(2)}, u32[]{:S(2)}) collective-permute-start(f32[8,128]{1,0:T(8,128)S(1)} %get-tuple-element.22), channel_id=1, source_target_pairs={{1,2},{3,4},{5,6},{2,1},{4,3},{6,5},{9,10},{11,12},{13,14},{10,9},... | collective-permute-start | bytes 12296 | tf_op jit(solution)/shard_map/ppermute | solution.py:585
  11.7 4.1 %collective-permute-start.3 = (f32[8,128]{1,0:T(8,128)S(1)}, f32[8,128]{1,0:T(8,128)S(1)}, u32[]{:S(2)}, u32[]{:S(2)}) collective-permute-start(f32[8,128]{1,0:T(8,128)S(1)} %get-tuple-element.22), channel_id=1, source_target_pairs={{0,1},{1,0},{2,3},{3,2},{4,5},{5,4},{6,7},{7,6},{8,9},{9,8},{10,11... | collective-permute-start | bytes 12296 | tf_op jit(solution)/shard_map/ppermute | solution.py:580
  15.9 7.3 %collective-permute-start.8 = (f32[104,128]{1,0:T(8,128)S(1)}, f32[104,128]{1,0:T(8,128)S(1)}, u32[]{:S(2)}, u32[]{:S(2)}) collective-permute-start(f32[104,128]{1,0:T(8,128)S(1)} %rims.2.refs_4_.refs_0_), channel_id=1, source_target_pairs={{0,24},{8,16},{16,8},{24,0},{1,25},{9,17},{17,9},{25,1},{2,26},{10... | collective-permute-start | bytes 159752 | tf_op jit(solution)/shard_map/ppermute | solution.py:580
  19.5 5.3 %collective-permute-start.7 = (f32[104,128]{1,0:T(8,128)S(1)}, f32[104,128]{1,0:T(8,128)S(1)}, u32[]{:S(2)}, u32[]{:S(2)}) collective-permute-start(f32[104,128]{1,0:T(8,128)S(1)} %rims.2.refs_4_.refs_0_), channel_id=1, source_target_pairs={{0,16},{8,24},{16,0},{24,8},{1,17},{9,25},{17,1},{25,9},{2,18},{10... | collective-permute-start | bytes 159752 | tf_op jit(solution)/shard_map/ppermute | solution.py:580
  19.5 5.3 %collective-permute-start.6 = (f32[104,128]{1,0:T(8,128)S(1)}, f32[104,128]{1,0:T(8,128)S(1)}, u32[]{:S(2)}, u32[]{:S(2)}) collective-permute-start(f32[104,128]{1,0:T(8,128)S(1)} %rims.2.refs_4_.refs_0_), channel_id=1, source_target_pairs={{0,8},{8,0},{16,24},{24,16},{1,9},{9,1},{17,25},{25,17},{2,10},{10... | collective-permute-start | bytes 159752 | tf_op jit(solution)/shard_map/ppermute | solution.py:580
  20.9 4.0 %copy-start = (s32[128,128]{1,0:T(8,128)S(1)}, s32[128,128]{1,0:T(8,128)}, u32[]{:S(2)}) copy-start(s32[128,128]{1,0:T(8,128)} %knot_ref.3) | copy-start | bytes 196612
  20.9 4.0 %collective-permute-start.5 = (f32[1288,128]{1,0:T(8,128)S(1)}, f32[1288,128]{1,0:T(8,128)S(1)}, u32[]{:S(2)}, u32[]{:S(2)}) collective-permute-start(f32[1288,128]{1,0:T(8,128)S(1)} %get-tuple-element.25.mine_ref), channel_id=1, source_target_pairs={{0,1},{1,0},{2,3},{3,2},{4,5},{5,4},{6,7},{7,6},{8,9},{9,8},{10,11... | collective-permute-start | bytes 1978376 | tf_op jit(solution)/shard_map/ppermute | solution.py:580
  31.0 12.9 %collective-permute-start.11 = (f32[328,128]{1,0:T(8,128)S(1)}, f32[328,128]{1,0:T(8,128)S(1)}, u32[]{:S(2)}, u32[]{:S(2)}) collective-permute-start(f32[328,128]{1,0:T(8,128)S(1)} %later_sources.1.refs_1_), channel_id=1, source_target_pairs={{0,6},{1,7},{2,4},{3,5},{4,2},{5,3},{6,0},{7,1},{8,14},{9,15},{10,... | collective-permute-start | bytes 503816 | tf_op jit(solution)/shard_map/ppermute | solution.py:580
  33.9 11.4 %collective-permute-start.10 = (f32[328,128]{1,0:T(8,128)S(1)}, f32[328,128]{1,0:T(8,128)S(1)}, u32[]{:S(2)}, u32[]{:S(2)}) collective-permute-start(f32[328,128]{1,0:T(8,128)S(1)} %later_sources.1.refs_1_), channel_id=1, source_target_pairs={{0,4},{1,5},{2,6},{3,7},{4,0},{5,1},{6,2},{7,3},{8,12},{9,13},{10,... | collective-permute-start | bytes 503816 | tf_op jit(solution)/shard_map/ppermute | solution.py:580
  36.0 9.4 %collective-permute-start.9 = (f32[328,128]{1,0:T(8,128)S(1)}, f32[328,128]{1,0:T(8,128)S(1)}, u32[]{:S(2)}, u32[]{:S(2)}) collective-permute-start(f32[328,128]{1,0:T(8,128)S(1)} %later_sources.1.refs_1_), channel_id=1, source_target_pairs={{0,2},{1,3},{2,0},{3,1},{4,6},{5,7},{6,4},{7,5},{8,10},{9,11},{10,... | collective-permute-start | bytes 503816 | tf_op jit(solution)/shard_map/ppermute | solution.py:580
  36.0 4.1 %collective-permute-start.13 = (f32[8,128]{1,0:T(8,128)S(1)}, f32[8,128]{1,0:T(8,128)S(1)}, u32[]{:S(2)}, u32[]{:S(2)}) collective-permute-start(f32[8,128]{1,0:T(8,128)S(1)} %get-tuple-element.30), channel_id=1, source_target_pairs={{1,2},{3,4},{5,6},{2,1},{4,3},{6,5},{9,10},{11,12},{13,14},{10,9},... | collective-permute-start | bytes 12296 | tf_op jit(solution)/shard_map/ppermute | solution.py:585
  36.6 4.3 %collective-permute-start.12 = (f32[8,128]{1,0:T(8,128)S(1)}, f32[8,128]{1,0:T(8,128)S(1)}, u32[]{:S(2)}, u32[]{:S(2)}) collective-permute-start(f32[8,128]{1,0:T(8,128)S(1)} %get-tuple-element.30), channel_id=1, source_target_pairs={{0,1},{1,0},{2,3},{3,2},{4,5},{5,4},{6,7},{7,6},{8,9},{9,8},{10,11... | collective-permute-start | bytes 12296 | tf_op jit(solution)/shard_map/ppermute | solution.py:580
  40.9 6.5 %collective-permute-start.17 = (f32[104,128]{1,0:T(8,128)S(1)}, f32[104,128]{1,0:T(8,128)S(1)}, u32[]{:S(2)}, u32[]{:S(2)}) collective-permute-start(f32[104,128]{1,0:T(8,128)S(1)} %rims.3.refs_5_.refs_0_), channel_id=1, source_target_pairs={{0,24},{8,16},{16,8},{24,0},{1,25},{9,17},{17,9},{25,1},{2,26},{10... | collective-permute-start | bytes 159752 | tf_op jit(solution)/shard_map/ppermute | solution.py:580
  43.4 6.6 %collective-permute-start.16 = (f32[104,128]{1,0:T(8,128)S(1)}, f32[104,128]{1,0:T(8,128)S(1)}, u32[]{:S(2)}, u32[]{:S(2)}) collective-permute-start(f32[104,128]{1,0:T(8,128)S(1)} %rims.3.refs_5_.refs_0_), channel_id=1, source_target_pairs={{0,16},{8,24},{16,0},{24,8},{1,17},{9,25},{17,1},{25,9},{2,18},{10... | collective-permute-start | bytes 159752 | tf_op jit(solution)/shard_map/ppermute | solution.py:580
  43.9 6.1 %collective-permute-start.15 = (f32[104,128]{1,0:T(8,128)S(1)}, f32[104,128]{1,0:T(8,128)S(1)}, u32[]{:S(2)}, u32[]{:S(2)}) collective-permute-start(f32[104,128]{1,0:T(8,128)S(1)} %rims.3.refs_5_.refs_0_), channel_id=1, source_target_pairs={{0,8},{8,0},{16,24},{24,16},{1,9},{9,1},{17,25},{25,17},{2,10},{10... | collective-permute-start | bytes 159752 | tf_op jit(solution)/shard_map/ppermute | solution.py:580
  45.9 4.1 %collective-permute-start.14 = (f32[1288,128]{1,0:T(8,128)S(1)}, f32[1288,128]{1,0:T(8,128)S(1)}, u32[]{:S(2)}, u32[]{:S(2)}) collective-permute-start(f32[1288,128]{1,0:T(8,128)S(1)} %dense_second.1.mine_ref), channel_id=1, source_target_pairs={{0,1},{1,0},{2,3},{3,2},{4,5},{5,4},{6,7},{7,6},{8,9},{9,8},{10,11... | collective-permute-start | bytes 1978376 | tf_op jit(solution)/shard_map/ppermute | solution.py:580
